TPU v7x, 32 devices: a whole 2x2x4 slice. The times are simulated.
32 devices in a mesh: row: 8 (over y, x, core), col: 4 (over z).
Axes of the slice: x: 2, y: 2, z: 4, core: 2. Of those that a mesh axis runs over, the one named last changes fastest.
Arguments:
- ancestor: bfloat16 [16384, 16384], P('row', 'col'), as said below
- panels: bfloat16 [3, 8192, 256], P(None, ('row', 'col')), may hold values from -0.625 to 0.625
- row_index: int32 [3, 8192], P(None, ('row', 'col')), may hold values from 0 to 16383, as said below
- diag_inverse: float32 [3, 256, 256], replicated, may hold values from -6 to 6
Outputs:
- off_block: bfloat16 [16384, 768], P(('row', 'col'))
- diag_block: float32 [3, 256, 256], replicated
Inputs may be any that keep to these rules, and one draw needn't show every extreme that they name: `row_index`: each of the 3 lists names 8192 different ancestor rows; row 0 and row 16383 are in every list. `ancestor`: entries on and below the diagonal are read; diagonal entries lie between 0.75 and 1.25 plus the off-diagonal spread.
All inputs are finite; a program needn't handle non-finite values.
Results may differ from a plain program's by a relative error of at most 0.014.
Values may be sent and summed in bfloat16 or wider, within the bound.
No kernel may reach another device: no remote copies, remote signals or barrier semaphores. Data moves between devices by JAX's collectives and lax.ppermute only.
A program may use at most 128 MiB of HBM per device.

v0:
```python
import jax
import jax.numpy as jnp
from jax import lax
from jax.sharding import PartitionSpec as P


def place_rows(table, offset, values, targets):
    limit_rows = table.shape[0]
    local_rows = targets - offset
    inside = (local_rows >= 0) & (local_rows < limit_rows)
    local_rows = jnp.where(inside, local_rows, limit_rows)
    sibling = lax.broadcasted_iota(jnp.int32, targets.shape, 0)
    return table.at[local_rows, sibling].set(values, mode="drop")


def per_device(ancestor, panels, row_index, diag_inverse):
    row_count = lax.axis_size("row")
    col_count = lax.axis_size("col")
    block_rows, block_cols = ancestor.shape
    sib_count = panels.shape[0]
    width = panels.shape[2]
    features = sib_count * width
    halves = row_count // col_count
    owned_rows = block_rows // col_count
    row_place = lax.axis_index("row")
    col_place = lax.axis_index("col")
    row_start = row_place * block_rows
    col_start = col_place * block_cols
    values = lax.all_gather(panels, ("row", "col"), axis=1, tiled=True)
    targets = lax.all_gather(row_index, ("row", "col"), axis=1, tiled=True)
    collect_row_table = jnp.zeros((block_rows, sib_count, width), jnp.bfloat16)
    collect_col_table = jnp.zeros((block_cols, sib_count, width), jnp.bfloat16)
    member = jnp.zeros((block_rows, sib_count), jnp.float32)
    marks = jnp.ones(targets.shape, jnp.float32)
    row_table, col_table, member = (
        place_rows(collect_row_table, row_start, values, targets),
        place_rows(collect_col_table, col_start, values, targets),
        place_rows(member, row_start, marks, targets),
    )
    row_ids = row_start + lax.broadcasted_iota(jnp.int32, (block_rows, block_cols), 0)
    col_ids = col_start + lax.broadcasted_iota(jnp.int32, (block_rows, block_cols), 1)
    nothing_bf = jnp.zeros((), jnp.bfloat16)

    def compute(unused):
        lower_part = jnp.where(col_ids <= row_ids, ancestor, nothing_bf)
        strict = jnp.where(col_ids < row_ids, ancestor, nothing_bf)
        direct = jnp.dot(
            lower_part, col_table.reshape(block_cols, features), preferred_element_type=jnp.float32
        )
        mirrored = jnp.einsum(
            "rhjo,rk->jhok",
            strict.reshape(block_rows, halves, col_count, owned_rows),
            row_table.reshape(block_rows, features),
            preferred_element_type=jnp.float32,
        )
        return (
            direct.reshape(col_count, owned_rows, features).astype(jnp.bfloat16),
            mirrored.astype(jnp.bfloat16),
        )

    def skipped(unused):
        return (
            jnp.zeros((col_count, owned_rows, features), jnp.bfloat16),
            jnp.zeros((col_count, halves, owned_rows, features), jnp.bfloat16),
        )

    direct, mirrored = lax.cond(col_start > row_start + block_rows - 1, skipped, compute, 0)
    received = lax.all_to_all(mirrored, "col", split_axis=0, concat_axis=0, tiled=True)
    stacked = received.reshape(row_count, owned_rows, features)
    mirror_own = lax.psum_scatter(stacked, "row", scatter_dimension=0, tiled=True).astype(
        jnp.float32
    )[0]
    direct_own = lax.psum_scatter(direct, "col", scatter_dimension=0, tiled=True).astype(
        jnp.float32
    )[0]
    summed = direct_own + mirror_own
    member_own = lax.dynamic_slice_in_dim(member, col_place * owned_rows, owned_rows, 0)
    panel_own = lax.dynamic_slice_in_dim(row_table, col_place * owned_rows, owned_rows, 0)
    product = summed.reshape(owned_rows, sib_count, width)
    off_block = (
        jnp.where(member_own[:, :, None] > 0.5, -product, 0.0)
        .astype(jnp.bfloat16)
        .reshape(owned_rows, features)
    )
    partial_value = jnp.einsum(
        "osw,osv->swv", panel_own.astype(jnp.float32), product, precision=lax.Precision.HIGHEST
    )
    diag_block = diag_inverse + lax.psum(partial_value, ("row", "col"))
    return (off_block, diag_block)


def solution(mesh):
    in_specs = (P("row", "col"), P(None, ("row", "col"), None), P(None, ("row", "col")), P())
    out_specs = (P(("row", "col"), None), P())
    return jax.shard_map(
        per_device, mesh=mesh, in_specs=in_specs, out_specs=out_specs, check_vma=False
    )
```

profile of v0, /device:TPU:4, one launch (start us, length us, event | category | flops | bytes accessed | tf_op | source)
XLA Modules:
  0.0 847.2 jit_solution(14951620065716616872)
XLA Ops:
  7.2 0.7 all-gather.2.cloned.1.call-update
  7.9 70.1 %all_gather.6 = s32[3,8192]{1,0:T(4,128)S(1)} all-gather(s32[3,256]{1,0:T(4,128)} %param.8), channel_id=1, replica_groups=mesh['row'=8,'col'=4] {'row','col'}, dimensions={1}, use_global_device_ids=true | all-gather | bytes 101376 | tf_op jit(solution)/shard_map/all_gather | solution.py:30
  78.0 0.1 fusion.7
  78.2 1.0 multiply_reduce_fusion
  79.1 1.1 and_reduce_fusion
  80.2 0.1 broadcast_select_fusion
  80.5 28.7 %all-gather.2.cloned.1.call-done = bf16[3,8192,256]{2,1,0:T(8,128)(2,1)} async-done(((bf16[3,256,256]{2,1,0:T(8,128)(2,1)}), bf16[3,8192,256]{2,1,0:T(8,128)(2,1)}) %all-gather.2.cloned.1.call-update) | async-done | bytes 12582928 | tf_op jit(solution)/shard_map/all_gather | solution.py:29
  109.2 104.4 %scatter_custom_fusion.2 = bf16[6144,256]{1,0:T(8,128)(2,1)S(1)} fusion(s32[24576]{0:T(1024)S(1)} %reshape.55, bf16[24576,256]{1,0:T(8,128)(2,1)} %bitcast.51, bf16[]{:T(256)} %constant.14.clone.1), kind=kCustom, calls=%fused_computation.13 | custom fusion | bytes 3146240
  213.6 107.1 %scatter_custom_fusion.1 = bf16[12288,256]{1,0:T(8,128)(2,1)} fusion(s32[24576]{0:T(1024)S(1)} %reshape.61, bf16[24576,256]{1,0:T(8,128)(2,1)} %bitcast.52, bf16[]{:T(256)} %constant.14.clone.1), kind=kCustom, calls=%fused_computation.9 | custom fusion | bytes 6291968
  320.8 113.2 %conditional.1 = (bf16[4,512,768]{2,1,0:T(8,128)(2,1)}, bf16[4,2,512,768]{3,2,0,1:T(8,128)(2,1)}) conditional(s32[]{:T(128)} %convert_element_type.23, (s32[]{:T(128)}, s32[4096]{0:T(1024)S(1)}, s32[]{:T(128)}, s32[2048]{0:T(1024)S(1)}, bf16[2048,4096]{1,0:T(8,128)(2,1)}, /*index=5*/bf16[4096,3,256]{2,0,1:T(8,128)(2,1)}, ...), branch_computations={%region_3.4_spmd, %region_4.5_spmd} | conditional | flops 25808082944 | bytes 201400368 | solution.py:67
  320.8 3.1 copy.28
  323.9 8.7 %copy.27 = bf16[4096,3,256]{0,2,1:T(8,128)(2,1)} copy(bf16[4096,3,256]{2,0,1:T(8,128)(2,1)} %get-tuple-element.56) | data formatting | bytes 12582912 | tf_op jit(solution)/shard_map
  332.6 22.6 %copy.26 = bf16[2048,4096]{0,1:T(8,128)(2,1)} copy(bf16[2048,4096]{1,0:T(8,128)(2,1)} %get-tuple-element.55) | data formatting | bytes 33554432 | tf_op jit(solution)/shard_map
  355.2 19.9 %compare_select_fusion = (bf16[2048,4096]{0,1:T(8,128)(2,1)}, bf16[2048,4096]{0,1:T(8,128)(2,1)}) fusion(bf16[2048,4096]{0,1:T(8,128)(2,1)} %copy.26, s32[2048]{0:T(1024)S(1)} %broadcast_add_fusion.1, s32[4096]{0:T(1024)S(1)} %broadcast_add_fusion), kind=kLoop, calls=%fused_computation.3 | loop fusion | flops 33554432 | bytes 50356224 | tf_op jit(solution)/shard_map/cond/branch_0_fun/jit(_where)/select_n | solution.py:46
  375.1 18.7 %convert_bitcast_fusion = bf16[4,2,512,768]{3,2,0,1:T(8,128)(2,1)} fusion(bf16[2048,2,4,512]{0,3,2,1:T(8,128)(2,1)} %bitcast.44, bf16[2048,768,1,1]{0,1,3,2:T(8,128)(2,1)S(1)} %bitcast.50), kind=kOutput, calls=%fused_computation.5 | convolution fusion | flops 12888047616 | bytes 26214400 | tf_op jit(solution)/shard_map/cond/branch_0_fun/rhjo,rk->jhok/dot_general | solution.py:50
  393.7 20.7 %copy.38 = bf16[2048,4096]{1,0:T(8,128)(2,1)} copy(bf16[2048,4096]{0,1:T(8,128)(2,1)} %get-tuple-element.65) | data formatting | bytes 33554432 | tf_op jit(solution)/shard_map/cond/branch_0_fun/dot_general | solution.py:47
  414.4 19.5 %convolution_convert_fusion = bf16[4,512,768]{2,1,0:T(8,128)(2,1)} fusion(bf16[4,512,4096]{2,1,0:T(8,128)(2,1)} %bitcast.45, bf16[4096,768,1]{0,1,2:T(8,128)(2,1)} %bitcast.48), kind=kOutput, calls=%fused_computation.6 | convolution fusion | flops 12886474752 | bytes 26214400 | tf_op jit(solution)/shard_map/cond/branch_0_fun/dot_general | solution.py:47
  434.0 5.8 copy.30
  439.8 5.2 all-to-all-start
  445.1 4.7 copy.29
  449.9 184.6 %all-to-all-done = bf16[4,2,512,768]{3,2,1,0:T(8,128)(2,1)} async-done(((bf16[4,2,512,768]{3,2,1,0:T(8,128)(2,1)}), bf16[4,2,512,768]{3,2,1,0:T(8,128)(2,1)}, u32[]{:S(2)}, u32[]{:S(2)}) %all-to-all-start) | async-done | bytes 6291488 | tf_op jit(solution)/shard_map/all_to_all | solution.py:68
  634.4 8.6 %copy.31 = bf16[4,2,512,768]{2,3,1,0:T(8,128)(2,1)} copy(bf16[4,2,512,768]{3,2,1,0:T(8,128)(2,1)} %all-to-all-done) | data formatting | bytes 12582912 | tf_op jit(solution)/shard_map/all_to_all | solution.py:68
  643.2 0.9 constant_dynamic-slice_fusion
  644.1 1.5 copy.41
  645.6 57.5 %reduce-scatter.5.cloned.1.call-done = bf16[1,512,768]{1,2,0:T(8,128)(2,1)} async-done(((bf16[8,512,768]{1,2,0:T(8,128)(2,1)}), bf16[1,512,768]{1,2,0:T(8,128)(2,1)}) %reduce-scatter.5.cloned.1.call-update) | async-done | bytes 786448 | tf_op jit(solution)/shard_map/reduce_scatter | solution.py:70
  703.1 1.7 convert_add_fusion
  704.8 1.8 fusion.5
  706.6 90.2 %scatter_custom_fusion = f32[6144]{0:T(1024)S(1)} fusion(s32[24576]{0:T(1024)S(1)} %reshape.55, f32[24576]{0:T(1024)S(1)} %broadcast.82, f32[]{:T(128)} %constant.16.clone.1), kind=kCustom, calls=%fused_computation.30 | custom fusion | bytes 24580
  796.9 0.3 fusion.2
  797.2 1.2 copy.34
  798.4 40.2 %all-reduce.2.cloned.1.call-done = f32[3,256,256]{2,1,0:T(8,128)} async-done(((f32[3,256,256]{2,1,0:T(8,128)}), f32[3,256,256]{2,1,0:T(8,128)}) %all-reduce.2.cloned.1.call-update) | async-done | bytes 786448 | tf_op jit(solution)/shard_map/psum | solution.py:88
  838.6 2.1 add.58
  (26 shorter events, 0.5 us)
Async XLA Ops:
  7.2 102.0 %all-gather.2.cloned.1.call-start = ((), (), s32[]{:S(2)}) async-start(), calls=%async_computation.3 | async-start | bytes 12976128 | tf_op jit(solution)/shard_map/all_gather | solution.py:29
  355.2 19.9 %copy-start = (bf16[2048,3,256]{0,2,1:T(8,128)(2,1)S(1)}, bf16[2048,3,256]{0,2,1:T(8,128)(2,1)}, u32[]{:S(2)}) copy-start(bf16[2048,3,256]{0,2,1:T(8,128)(2,1)} %copy.28) | copy-start | bytes 9437188 | tf_op jit(solution)/shard_map/cond
  439.8 194.6 %all-to-all-start = ((bf16[4,2,512,768]{3,2,1,0:T(8,128)(2,1)}), bf16[4,2,512,768]{3,2,1,0:T(8,128)(2,1)}, u32[]{:S(2)}, u32[]{:S(2)}) async-start(bf16[4,2,512,768]{3,2,1,0:T(8,128)(2,1)} %copy.30), calls=%async_computation.1 | async-start | bytes 12582912 | tf_op jit(solution)/shard_map/all_to_all | solution.py:68
  445.0 200.6 %reduce-scatter.3.cloned.1.call-start = ((), (), s32[]{:S(2)}) async-start(), calls=%async_computation.4 | async-start | bytes 3932160 | tf_op jit(solution)/shard_map/reduce_scatter | solution.py:73
  449.8 253.3 %reduce-scatter.5.cloned.1.call-start = ((), (), s32[]{:S(2)}) async-start(), calls=%async_computation.5 | async-start | bytes 7077888 | tf_op jit(solution)/shard_map/reduce_scatter | solution.py:70
  643.1 195.4 %all-reduce.2.cloned.1.call-start = ((), (), s32[]{:S(2)}) async-start(), calls=%async_computation.6 | async-start | bytes 1572864 | tf_op jit(solution)/shard_map/psum | solution.py:88
  644.1 194.5 %copy-start.3 = (f32[3,256,256]{2,1,0:T(8,128)S(1)}, f32[3,256,256]{2,1,0:T(8,128)}, u32[]{:S(2)}) copy-start(f32[3,256,256]{2,1,0:T(8,128)} %param.9) | copy-start | bytes 2359300
  645.6 151.3 %copy-start.1 = (bf16[1,512,768]{1,2,0:T(8,128)(2,1)S(1)}, bf16[1,512,768]{1,2,0:T(8,128)(2,1)}, u32[]{:S(2)}) copy-start(bf16[1,512,768]{1,2,0:T(8,128)(2,1)} %reduce-scatter.3.cloned.1.call-done) | copy-start | bytes 2359300
  703.1 93.9 %copy-start.2 = (bf16[1,512,768]{1,2,0:T(8,128)(2,1)S(1)}, bf16[1,512,768]{1,2,0:T(8,128)(2,1)}, u32[]{:S(2)}) copy-start(bf16[1,512,768]{1,2,0:T(8,128)(2,1)} %reduce-scatter.5.cloned.1.call-done) | copy-start | bytes 2359300
Sparse Core Ops, SparseCore 0:
  11.1 98.0 all-gather.1
  449.9 112.1 reduce-scatter.2
  643.2 59.7 reduce-scatter.4
  709.5 128.9 all-reduce.1
where the time goes:
time: 851 us; the launch traced here: 847 us
  local copies, waits for them, and re-layouts  380 us (45%)
  waiting for transfers between devices  312 us (37%)
  blocking collectives  70.1 us (8%)
  matrix products  40 us (5%)
  other arithmetic  26.2 us (3%)
  between operations  13.9 us (2%)
    unnamed x16, local copies, waits for them, and re-layouts  306 us
    all_to_all x1, waiting for transfers between devices, per_device(): lax.all_to_all(mirrored, 'col', split_axis=0, concat_axis=0, tiled=True)  185 us
    all_gather x1, blocking collectives, per_device(): targets = lax.all_gather(row_index, ('row', 'col'), axis=1, tiled=True)  70.1 us
    reduce_scatter x1, waiting for transfers between devices, per_device(): lax.psum_scatter(stacked, 'row', scatter_dimension=0, tiled=True)  57.5 us
    psum x1, waiting for transfers between devices, per_device(): diag_block = diag_inverse + lax.psum(partial_value, ('row', 'col'))  40.2 us
    another operation x3, local copies, waits for them, and re-layouts  34.4 us
    all_gather x1, waiting for transfers between devices, per_device(): values = lax.all_gather(panels, ('row', 'col'), axis=1, tiled=True)  28.7 us
    dot_general x1, local copies, waits for them, and re-layouts, compute(): jnp.dot(lower_part, col_table.reshape(block_cols, features), preferred_el...  20.7 us
  transfers between devices with their start and end apart: 5, of which 4 were waited for; matrix products, arithmetic and copies ran while one was open for 13% of the time, Pallas kernels for 0%

commit v1 on v0

v1 whole, which is shorter than its diff:
```python
import functools

import jax
import jax.numpy as jnp
from jax import lax
from jax.experimental import pallas as pl
from jax.experimental.pallas import tpu as pltpu
from jax.sharding import PartitionSpec as P

LANES = 128
BF = jnp.bfloat16
F32 = jnp.float32


def swap(x, axis, bit):
    count = lax.axis_size(axis)
    return lax.ppermute(x, axis, [(i, i ^ bit) for i in range(count)])


def row_bits(row_count):
    return [b for b in (1 << n for n in range(1, 20)) if b < row_count]


def collect(own, dim):
    col_count = lax.axis_size("col")
    bits = row_bits(lax.axis_size("row"))
    lines = [own] + [swap(own, "col", d) for d in range(1, col_count)]
    first = jnp.concatenate(lines[: col_count // 2], dim)
    second = jnp.concatenate(lines[col_count // 2 :], dim)
    for one, other in zip(bits, bits[::-1]):
        first, second = (
            jnp.concatenate([first, swap(first, "row", one)], dim),
            jnp.concatenate([second, swap(second, "row", other)], dim),
        )
    return [first, second, swap(first, "row", 1), swap(second, "row", 1)], lines


def invert_kernel(index_ref, out_ref):
    sibs, listed = index_ref.shape
    lines = out_ref.shape[1]
    step = min(listed, 2048)
    for s in range(sibs):
        total = jnp.zeros((lines, 2 * LANES), F32)
        for n in range(0, listed, step):
            index = index_ref[s : s + 1, n : n + step]
            place = n + 1 + lax.broadcasted_iota(jnp.int32, (1, step), 1)
            line_of = index // LANES
            lane_of = index % LANES
            high = (place // LANES).astype(F32)
            low = (place % LANES).astype(F32)
            on_line = lax.broadcasted_iota(jnp.int32, (lines, step), 0) == line_of
            on_lane = lax.broadcasted_iota(jnp.int32, (LANES, step), 0) == lane_of
            left = jnp.where(on_line, 1.0, 0.0).astype(BF)
            right = jnp.concatenate(
                [jnp.where(on_lane, high, 0.0), jnp.where(on_lane, low, 0.0)], 0
            ).astype(BF)
            total += lax.dot_general(
                left, right, (((1,), (1,)), ((), ())), preferred_element_type=F32
            )
        out_ref[s] = (total[:, :LANES] * LANES + total[:, LANES:]).astype(jnp.int32)


def invert(index, rows):
    sibs = index.shape[0]
    return pl.pallas_call(
        invert_kernel,
        out_shape=jax.ShapeDtypeStruct((sibs, rows // LANES, LANES), jnp.int32),
        compiler_params=pltpu.CompilerParams(vmem_limit_bytes=32 * 2**20),
        cost_estimate=pl.CostEstimate(
            flops=4 * sibs * rows * index.shape[1], bytes_accessed=4 * sibs * rows, transcendentals=0
        ),
    )(index)


def tables_kernel(
    row_inv, col_inv, p0, p1, p2, p3, row_out, col_out, source, target
):
    step = 256
    width = col_out.shape[1]
    parts = width // LANES
    source[0 : 8 * parts, :] = jnp.zeros((8 * parts, LANES), F32)
    base = 1
    for piece in (p0, p1, p2, p3):
        rows = piece.shape[0]

        def fill(n, unused, piece=piece, base=base):
            at = pl.multiple_of(n * step, step)
            values = piece[pl.ds(at, step), :].astype(F32)
            for q in range(parts):
                source[pl.ds(parts * (base + at) + q, step, stride=parts), :] = values[
                    :, q * LANES : (q + 1) * LANES
                ]
            return unused

        lax.fori_loop(0, rows // step, fill, 0)
        base += rows

    def pick(inv):
        batch = 16

        def line(h, unused):
            for first in range(0, LANES, batch):
                found = [
                    source[pl.ds(pl.multiple_of(parts * inv[h, first + u], parts), parts), :]
                    for u in range(batch)
                ]
                for u in range(batch):
                    target[
                        pl.ds(pl.multiple_of(parts * (h * LANES + first + u), parts), parts), :
                    ] = found[u]
            return unused

        lax.fori_loop(0, inv.shape[0], line, 0)

    pick(row_inv)
    for n in range(row_out.shape[1] // step):
        for q in range(parts):
            values = target[pl.ds(parts * n * step + q, step, stride=parts), :]
            row_out[q * LANES : (q + 1) * LANES, n * step : (n + 1) * step] = values.T.astype(BF)
    pick(col_inv)

    def drain(n, unused):
        at = pl.multiple_of(n * step, step)
        for q in range(parts):
            values = target[pl.ds(parts * at + q, step, stride=parts), :]
            col_out[pl.ds(at, step), q * LANES : (q + 1) * LANES] = values.astype(BF)
        return unused

    lax.fori_loop(0, col_out.shape[0] // step, drain, 0)


def tables(pieces, row_inv, col_inv):
    width = pieces[0].shape[1]
    listed = sum(p.shape[0] for p in pieces)
    parts = width // LANES
    rows, cols = row_inv.size, col_inv.size
    vmem = pl.BlockSpec(memory_space=pltpu.VMEM)
    smem = pl.BlockSpec(memory_space=pltpu.SMEM)
    return pl.pallas_call(
        tables_kernel,
        in_specs=[smem, smem] + [vmem] * 4,
        out_specs=[vmem, vmem],
        out_shape=[
            jax.ShapeDtypeStruct((width, rows), BF),
            jax.ShapeDtypeStruct((cols, width), BF),
        ],
        scratch_shapes=[
            pltpu.VMEM((parts * (listed + 8), LANES), F32),
            pltpu.VMEM((parts * max(rows, cols), LANES), F32),
        ],
        compiler_params=pltpu.CompilerParams(vmem_limit_bytes=48 * 2**20),
        cost_estimate=pl.CostEstimate(
            flops=10**10, bytes_accessed=2 * width * (listed + rows + cols), transcendentals=0
        ),
    )(row_inv, col_inv, *pieces)


def terms_kernel(
    plan, block, row_t, col, m_send, m_keep, d_send, d_keep, y_send, y_keep, total, mirror_y, lower, strict
):
    i = pl.program_id(0)
    steps = pl.num_programs(0)
    tile = block.shape[1]
    rows = block.shape[0]
    row_start = plan[steps]
    first_col = plan[steps + 1] + plan[i] * tile

    @pl.when(i == 0)
    def start():
        total[...] = jnp.zeros_like(total)
        mirror_y[...] = jnp.zeros_like(mirror_y)

    def work(low_ref, strict_ref):
        mirrored = jnp.dot(row_t[...], strict_ref[...], preferred_element_type=F32).astype(BF)

        @pl.when(i < steps // 2)
        def sent():
            m_send[0] = mirrored

        @pl.when(i >= steps // 2)
        def kept():
            m_keep[0] = mirrored

        mirror_y[...] += jnp.dot(mirrored, col[...], preferred_element_type=F32)
        step = 256

        def direct(n, unused):
            at = pl.ds(pl.multiple_of(n * step, step), step)
            total[at, :] += jnp.dot(low_ref[at, :], col[...], preferred_element_type=F32)
            return unused

        lax.fori_loop(0, rows // step, direct, 0)

    full = row_start >= first_col + tile
    none = row_start + rows <= first_col

    @pl.when(full)
    def whole():
        work(block, block)

    @pl.when(jnp.logical_not(jnp.logical_or(full, none)))
    def cut():
        step = 256

        def mask(n, unused):
            at = pl.ds(pl.multiple_of(n * step, step), step)
            row_ids = row_start + n * step + lax.broadcasted_iota(jnp.int32, (step, tile), 0)
            col_ids = first_col + lax.broadcasted_iota(jnp.int32, (step, tile), 1)
            values = block[at, :]
            nothing = jnp.zeros((), BF)
            lower[at, :] = jnp.where(col_ids <= row_ids, values, nothing)
            strict[at, :] = jnp.where(col_ids < row_ids, values, nothing)
            return unused

        lax.fori_loop(0, rows // step, mask, 0)
        work(lower, strict)

    @pl.when(none)
    def nothing_here():
        zero = jnp.zeros(m_send.shape[1:], BF)

        @pl.when(i < steps // 2)
        def sent():
            m_send[0] = zero

        @pl.when(i >= steps // 2)
        def kept():
            m_keep[0] = zero

    @pl.when(i == steps - 1)
    def finish():
        owned = d_send.shape[1]
        count = rows // owned
        place = plan[steps + 2]
        direct_y = jnp.zeros(mirror_y.shape, F32)
        for e in range(count):
            at = pl.multiple_of((e ^ place) * owned, owned)
            term = total[pl.ds(at, owned), :].astype(BF)
            if e % 2:
                d_send[e // 2] = term
            else:
                d_keep[e // 2] = term
            direct_y += jnp.dot(row_t[:, pl.ds(at, owned)], term, preferred_element_type=F32)
        y = direct_y + mirror_y[...].T
        half = y.shape[0] // 2
        core = plan[steps + 3]

        @pl.when(core == 0)
        def first_core():
            y_keep[...] = y[:half]
            y_send[...] = y[half:]

        @pl.when(core != 0)
        def second_core():
            y_keep[...] = y[half:]
            y_send[...] = y[:half]


def terms(plan, ancestor, row_t, col, owned):
    rows, cols = ancestor.shape
    width = col.shape[1]
    steps = cols // owned
    count = rows // owned
    half = steps // 2
    grid_spec = pltpu.PrefetchScalarGridSpec(
        num_scalar_prefetch=1,
        grid=(steps,),
        in_specs=[
            pl.BlockSpec((rows, owned), lambda i, plan: (0, plan[i])),
            pl.BlockSpec((width, rows), lambda i, plan: (0, 0)),
            pl.BlockSpec((owned, width), lambda i, plan: (plan[i], 0)),
        ],
        out_specs=[
            pl.BlockSpec((1, width, owned), lambda i, plan: (jnp.minimum(i, half - 1), 0, 0)),
            pl.BlockSpec((1, width, owned), lambda i, plan: (jnp.maximum(i - half, 0), 0, 0)),
            pl.BlockSpec((count // 2, owned, width), lambda i, plan: (0, 0, 0)),
            pl.BlockSpec((count // 2, owned, width), lambda i, plan: (0, 0, 0)),
            pl.BlockSpec((width // 2, width), lambda i, plan: (0, 0)),
            pl.BlockSpec((width // 2, width), lambda i, plan: (0, 0)),
        ],
        scratch_shapes=[
            pltpu.VMEM((rows, width), F32),
            pltpu.VMEM((width, width), F32),
            pltpu.VMEM((rows, owned), BF),
            pltpu.VMEM((rows, owned), BF),
        ],
    )
    return pl.pallas_call(
        terms_kernel,
        grid_spec=grid_spec,
        out_shape=[
            jax.ShapeDtypeStruct((half, width, owned), BF),
            jax.ShapeDtypeStruct((half, width, owned), BF),
            jax.ShapeDtypeStruct((count // 2, owned, width), BF),
            jax.ShapeDtypeStruct((count // 2, owned, width), BF),
            jax.ShapeDtypeStruct((width // 2, width), F32),
            jax.ShapeDtypeStruct((width // 2, width), F32),
        ],
        compiler_params=pltpu.CompilerParams(vmem_limit_bytes=56 * 2**20),
        cost_estimate=pl.CostEstimate(
            flops=4 * rows * cols * width, bytes_accessed=2 * rows * cols, transcendentals=0
        ),
    )(plan, ancestor, row_t, col)


def add(a, b):
    return (a.astype(F32) + b.astype(F32)).astype(a.dtype)


def halve(values, bits, axis, labels, shift):
    for bit in bits:
        at = labels.index(bit)
        sent = lax.index_in_dim(values, 1, at, keepdims=False)
        kept = lax.index_in_dim(values, 0, at, keepdims=False)
        labels = labels[:at] + labels[at + 1 :]
        values = add(kept, swap(sent, axis, bit << shift))
    return values


def reversed_bits(value, bits):
    return sum(((value >> n) & 1) << (bits - 1 - n) for n in range(bits))


def to_owner(x):
    row_count = lax.axis_size("row")
    col_count = lax.axis_size("col")
    bits = col_count.bit_length() - 1
    pairs = []
    for row in range(row_count):
        for col in range(col_count):
            place = (row // 2) ^ reversed_bits(col, bits)
            pairs.append((row * col_count + col, (2 * col + row % 2) * col_count + place))
    return lax.ppermute(x, ("row", "col"), pairs)


def per_device(ancestor, panels, row_index, diag_inverse):
    row_count = lax.axis_size("row")
    col_count = lax.axis_size("col")
    assert row_count == 2 * col_count
    block_rows, block_cols = ancestor.shape
    sib_count, _, width = panels.shape
    owned = block_rows // col_count
    row_place = lax.axis_index("row")
    col_place = lax.axis_index("col")
    core = row_place % 2
    chip = row_place // 2
    col_bits = col_count.bit_length() - 1

    index_pieces, _ = collect(row_index, 1)
    inverse = invert(jnp.concatenate(index_pieces, 1), block_rows * row_count)
    row_inv = lax.dynamic_slice_in_dim(
        inverse, row_place * (block_rows // LANES), block_rows // LANES, 1
    )
    col_inv = lax.dynamic_slice_in_dim(
        inverse, col_place * (block_cols // LANES), block_cols // LANES, 1
    )
    own_inv = lax.dynamic_slice_in_dim(
        inverse, row_place * (block_rows // LANES) + col_place * (owned // LANES), owned // LANES, 1
    )
    member = own_inv.reshape(sib_count, owned) > 0

    slots = jnp.arange(col_count, dtype=jnp.int32)
    mixed = sum(((col_place >> n) & 1) << (col_bits - 1 - n) for n in range(col_bits))
    places = slots ^ (chip ^ mixed).astype(jnp.int32)
    plan = jnp.concatenate(
        [
            places + (1 - core) * col_count,
            places + core * col_count,
            jnp.stack([row_place * block_rows, col_place * block_cols, col_place, core]),
        ]
    ).astype(jnp.int32)

    before = None
    offs = []
    diags = []
    for s in range(sib_count):
        own = panels[s]
        if before is not None:
            own, _ = lax.optimization_barrier((own, before))
        pieces, before = collect(own, 0)
        row_t, col = tables(pieces, row_inv[s], col_inv[s])
        m_send, m_keep, d_send, d_keep, y_send, y_keep = terms(plan, ancestor, row_t, col, owned)

        m_got = swap(m_send, "row", 1)
        d_got = swap(d_send, "col", 1)
        mirrored = add(m_keep, m_got).reshape((2,) * col_bits + (2, width // 2, owned))
        labels = [1 << n for n in range(col_bits)][::-1]
        first = lax.index_in_dim(mirrored, 0, col_bits, keepdims=False)
        second = lax.index_in_dim(mirrored, 1, col_bits, keepdims=False)
        first = halve(first, labels[::-1], "row", labels, 1)
        second = halve(second, labels, "row", labels, 1)
        first, second = to_owner(first), to_owner(second)

        direct = add(d_keep, d_got).reshape((2,) * (col_bits - 1) + (owned, width))
        labels = [1 << n for n in range(1, col_bits)][::-1]
        for bit in labels[:0:-1]:
            at = labels.index(bit)
            sent = lax.index_in_dim(direct, 1, at, keepdims=False)
            kept = lax.index_in_dim(direct, 0, at, keepdims=False)
            labels = labels[:at] + labels[at + 1 :]
            direct = add(kept, swap(sent, "col", bit))
        got = swap(direct[1], "col", labels[0])
        product = (
            direct[0].astype(F32)
            + got.astype(F32)
            + jnp.concatenate([first, second], 0).astype(F32).T
        )
        offs.append(jnp.where(member[s][:, None], -product, 0.0).astype(BF))

        y = y_keep + swap(y_send, "row", 1)
        for bit in row_bits(row_count):
            y = y + swap(y, "row", bit)
        for n in range(col_bits):
            y = y + swap(y, "col", 1 << n)
        other = swap(y, "row", 1)
        diags.append(
            jnp.where(core == 0, jnp.concatenate([y, other], 0), jnp.concatenate([other, y], 0))
        )
    return jnp.concatenate(offs, 1), diag_inverse + jnp.stack(diags)


def solution(mesh):
    in_specs = (P("row", "col"), P(None, ("row", "col"), None), P(None, ("row", "col")), P())
    out_specs = (P(("row", "col"), None), P())
    return jax.shard_map(
        per_device, mesh=mesh, in_specs=in_specs, out_specs=out_specs, check_vma=False
    )
```

time: 851 us -> 393 us (0.46)
  local copies, waits for them, and re-layouts: 380 us -> 19.2 us
  waiting for transfers between devices: 312 us -> 120 us
  Pallas kernels: 0 us -> 122 us
  starting transfers between devices: 5.4 us -> 112 us
  blocking collectives: 70.1 us -> 0 us
  matrix products: 40 us -> 0 us
  between operations: 13.9 us -> 1.62 us
    unnamed x16 -> x61, local copies, waits for them, and re-layouts: 306 us -> 11.1 us
    all_to_all x1 -> x0, waiting for transfers between devices: 185 us -> none  [per_device(): lax.all_to_all(mirrored, 'col', split_axis=0, concat_axis=0, tiled=True)]
    pallas_call x0 -> x7, Pallas kernels: none -> 122 us  [the longest x3 85.5 us: terms(): pl.pallas_call(terms_kernel, grid_spec=grid_spec, out_shape=[jax.ShapeDty...]
    ppermute x0 -> x81, waiting for transfers between devices: none -> 120 us  [the longest x75 115 us: swap(): return lax.ppermute(x, axis, [(i, i ^ bit) for i in range(count)])]
    ppermute x0 -> x81, starting transfers between devices: none -> 112 us  [the longest x75 84.8 us: swap(): return lax.ppermute(x, axis, [(i, i ^ bit) for i in range(count)])]
    all_gather x1 -> x0, blocking collectives: 70.1 us -> none  [per_device(): targets = lax.all_gather(row_index, ('row', 'col'), axis=1, tiled=True)]
    reduce_scatter x2 -> x0, waiting for transfers between devices: 57.5 us -> none  [the longest x1 57.5 us: per_device(): lax.psum_scatter(stacked, 'row', scatter_dimension=0, tiled=True)]
    psum x1 -> x0, waiting for transfers between devices: 40.2 us -> none  [per_device(): diag_block = diag_inverse + lax.psum(partial_value, ('row', 'col'))]
  transfers between devices with their start and end apart: 5 -> 81, of which waited for: 4 -> 34; matrix products, arithmetic and copies ran while one was open for 13% -> 8% of each run, Pallas kernels for 0% -> 31%
where the time goes in v1:
time: 393 us
  Pallas kernels  122 us (31%)
  waiting for transfers between devices  120 us (31%)
  starting transfers between devices  112 us (28%)
  local copies, waits for them, and re-layouts  19.2 us (5%)
  other arithmetic  17.8 us (5%)
    ppermute x75, waiting for transfers between devices, swap(): return lax.ppermute(x, axis, [(i, i ^ bit) for i in range(count)])  115 us
    pallas_call x3, Pallas kernels, terms(): pl.pallas_call(terms_kernel, grid_spec=grid_spec, out_shape=[jax.ShapeDty...  85.5 us
    ppermute x75, starting transfers between devices, swap(): return lax.ppermute(x, axis, [(i, i ^ bit) for i in range(count)])  84.8 us
    pallas_call x3, Pallas kernels, tables(): pl.pallas_call(tables_kernel, in_specs=[smem, smem] + [vmem] * 4, out_spe...  31.6 us
    ppermute x6, starting transfers between devices, to_owner(): return lax.ppermute(x, ('row', 'col'), pairs)  27 us
    unnamed x61, local copies, waits for them, and re-layouts  11.1 us
  transfers between devices with their start and end apart: 81, of which 34 were waited for; matrix products, arithmetic and copies ran while one was open for 8% of the time, Pallas kernels for 31%

profile of v1, /device:TPU:4, one launch (start us, length us, event | category | flops | bytes accessed | tf_op | source)
XLA Modules:
  0.0 392.5 jit_solution(3913200325286962726)
XLA Ops:
  6.9 3.5 collective-permute-start.12
  22.8 4.6 %shard_map.59 = s32[3,128,128]{2,1,0:T(8,128)S(1)} custom-call(s32[3,8192]{1,0:T(4,128)S(1)} %constant_dynamic-update-slice_fusion.index_ref), custom_call_target="tpu_custom_call" | custom-call | flops 1610612736 | bytes 196608 | tf_op jit(solution)/shard_map/pallas_call | solution.py:65
  28.0 3.8 collective-permute-start.30
  35.8 6.0 %collective-permute-done.30 = bf16[256,256]{1,0:T(8,128)(2,1)S(1)} collective-permute-done((bf16[256,256]{1,0:T(8,128)(2,1)S(1)}, bf16[256,256]{1,0:T(8,128)(2,1)S(1)}, u32[]{:S(2)}, u32[]{:S(2)}) %collective-permute-start.30) | collective-permute-done | bytes 131104 | tf_op jit(solution)/shard_map/ppermute | solution.py:17
  50.8 6.5 %collective-permute-done.48 = bf16[256,256]{1,0:T(8,128)(2,1)S(1)} collective-permute-done((bf16[256,256]{1,0:T(8,128)(2,1)S(1)}, bf16[256,256]{1,0:T(8,128)(2,1)S(1)}, u32[]{:S(2)}, u32[]{:S(2)}) %collective-permute-start.48) | collective-permute-done | bytes 131104 | tf_op jit(solution)/shard_map/ppermute | solution.py:17
  62.5 4.0 %collective-permute-done.32 = bf16[512,256]{1,0:T(8,128)(2,1)S(1)} collective-permute-done((bf16[512,256]{1,0:T(8,128)(2,1)S(1)}, bf16[512,256]{1,0:T(8,128)(2,1)S(1)}, u32[]{:S(2)}, u32[]{:S(2)}) %collective-permute-start.32) | collective-permute-done | bytes 262176 | tf_op jit(solution)/shard_map/ppermute | solution.py:17
  67.3 15.9 %collective-permute-done.11 = bf16[1024,256]{1,0:T(8,128)(2,1)S(1)} collective-permute-done((bf16[1024,256]{1,0:T(8,128)(2,1)S(1)}, bf16[1024,256]{1,0:T(8,128)(2,1)S(1)}, u32[]{:S(2)}, u32[]{:S(2)}) %collective-permute-start.11) | collective-permute-done | bytes 524320 | tf_op jit(solution)/shard_map/ppermute | solution.py:17
  85.2 5.3 %collective-permute-done.29 = bf16[1024,256]{1,0:T(8,128)(2,1)S(1)} collective-permute-done((bf16[1024,256]{1,0:T(8,128)(2,1)S(1)}, bf16[1024,256]{1,0:T(8,128)(2,1)S(1)}, u32[]{:S(2)}, u32[]{:S(2)}) %collective-permute-start.29) | collective-permute-done | bytes 524320 | tf_op jit(solution)/shard_map/ppermute | solution.py:17
  90.6 8.2 %collective-permute-done.33 = bf16[1024,256]{1,0:T(8,128)(2,1)S(1)} collective-permute-done((bf16[1024,256]{1,0:T(8,128)(2,1)S(1)}, bf16[1024,256]{1,0:T(8,128)(2,1)S(1)}, u32[]{:S(2)}, u32[]{:S(2)}) %collective-permute-start.33) | collective-permute-done | bytes 524320 | tf_op jit(solution)/shard_map/ppermute | solution.py:17
  100.0 9.0 %collective-permute-done.51 = bf16[1024,256]{1,0:T(8,128)(2,1)S(1)} collective-permute-done((bf16[1024,256]{1,0:T(8,128)(2,1)S(1)}, bf16[1024,256]{1,0:T(8,128)(2,1)S(1)}, u32[]{:S(2)}, u32[]{:S(2)}) %collective-permute-start.51) | collective-permute-done | bytes 524320 | tf_op jit(solution)/shard_map/ppermute | solution.py:17
  109.7 10.5 %shard_map.60 = (bf16[256,2048]{1,0:T(8,128)(2,1)S(1)}, bf16[4096,256]{1,0:T(8,128)(2,1)}) custom-call(s32[16,128]{1,0:T(8,128)S(1)} %get-tuple-element.66.row_inv, s32[32,128]{1,0:T(8,128)S(1)} %get-tuple-element.63.col_inv, bf16[2048,256]{1,0:T(8,128)(2,1)S(1)} %pad_maximum_fusion.p0, bf16[2048,256]{1,0:T(8,128)(2,1)S(1)} %constant_dynamic-update-slice_fusion.10.p1, ...), custom_call_target="tpu_custom_call" | custom-call | flops 10000000000 | bytes 7340032 | tf_op jit(solution)/shard_map/pallas_call | solution.py:139
  121.2 28.4 %shard_map.61 = (bf16[4,256,512]{2,1,0:T(8,128)(2,1)}, bf16[4,256,512]{2,1,0:T(8,128)(2,1)}, bf16[2,512,256]{2,1,0:T(8,128)(2,1)}, bf16[2,512,256]{2,1,0:T(8,128...) custom-call(s32[12]{0:T(128)} %concatenate.186.plan, bf16[2048,4096]{1,0:T(8,128)(2,1)} %block.5, ...), custom_call_target="tpu_custom_call" | custom-call | flops 8589934592 | bytes 16777216 | tf_op jit(solution)/shard_map/pallas_call | solution.py:288
  149.8 10.7 %shard_map.62 = (bf16[256,2048]{1,0:T(8,128)(2,1)S(1)}, bf16[4096,256]{1,0:T(8,128)(2,1)}) custom-call(s32[16,128]{1,0:T(8,128)S(1)} %get-tuple-element.67.row_inv, s32[32,128]{1,0:T(8,128)S(1)} %get-tuple-element.64.col_inv, bf16[2048,256]{1,0:T(8,128)(2,1)S(1)} %constant_dynamic-update-slice_fusion.14.p0, ...), custom_call_target="tpu_custom_call" | custom-call | flops 10000000000 | bytes 7340032 | tf_op jit(solution)/shard_map/pallas_call | solution.py:139
  161.5 28.5 %shard_map.63 = (bf16[4,256,512]{2,1,0:T(8,128)(2,1)}, bf16[4,256,512]{2,1,0:T(8,128)(2,1)}, bf16[2,512,256]{2,1,0:T(8,128)(2,1)}, bf16[2,512,256]{2,1,0:T(8,128...) custom-call(s32[12]{0:T(128)} %concatenate.186.plan, bf16[2048,4096]{1,0:T(8,128)(2,1)} %block.5, ...), custom_call_target="tpu_custom_call" | custom-call | flops 8589934592 | bytes 16777216 | tf_op jit(solution)/shard_map/pallas_call | solution.py:288
  191.2 10.4 %shard_map.64 = (bf16[256,2048]{1,0:T(8,128)(2,1)S(1)}, bf16[4096,256]{1,0:T(8,128)(2,1)}) custom-call(s32[16,128]{1,0:T(8,128)S(1)} %get-tuple-element.68.row_inv, s32[32,128]{1,0:T(8,128)S(1)} %get-tuple-element.65.col_inv, bf16[2048,256]{1,0:T(8,128)(2,1)S(1)} %constant_dynamic-update-slice_fusion.22.p0, ...), custom_call_target="tpu_custom_call" | custom-call | flops 10000000000 | bytes 7340032 | tf_op jit(solution)/shard_map/pallas_call | solution.py:139
  202.6 28.5 %shard_map.65 = (bf16[4,256,512]{2,1,0:T(8,128)(2,1)}, bf16[4,256,512]{2,1,0:T(8,128)(2,1)}, bf16[2,512,256]{2,1,0:T(8,128)(2,1)}, bf16[2,512,256]{2,1,0:T(8,128...) custom-call(s32[12]{0:T(128)} %concatenate.186.plan, bf16[2048,4096]{1,0:T(8,128)(2,1)} %block.5, ...), custom_call_target="tpu_custom_call" | custom-call | flops 8589934592 | bytes 16777216 | tf_op jit(solution)/shard_map/pallas_call | solution.py:288
  234.9 4.5 %collective-permute-start.65 = (f32[128,256]{1,0:T(8,128)S(1)}, f32[128,256]{1,0:T(8,128)S(1)}, u32[]{:S(2)}, u32[]{:S(2)}) collective-permute-start(f32[128,256]{1,0:T(8,128)S(1)} %add.187), channel_id=1, source_target_pairs={{0,16},{4,20},{8,24},{12,28},{16,0},{20,4},{24,8},{28,12},{1,17},{... | collective-permute-start | bytes 393224 | tf_op jit(solution)/shard_map/ppermute | solution.py:17
  251.5 8.3 %collective-permute-done.66 = f32[128,256]{1,0:T(8,128)S(1)} collective-permute-done((f32[128,256]{1,0:T(8,128)S(1)}, f32[128,256]{1,0:T(8,128)S(1)}, u32[]{:S(2)}, u32[]{:S(2)}) %collective-permute-start.66) | collective-permute-done | bytes 131104 | tf_op jit(solution)/shard_map/ppermute | solution.py:17
  259.9 7.0 %collective-permute-start.77 = (f32[128,256]{1,0:T(8,128)S(1)}, f32[128,256]{1,0:T(8,128)S(1)}, u32[]{:S(2)}, u32[]{:S(2)}) collective-permute-start(f32[128,256]{1,0:T(8,128)S(1)} %add.197), channel_id=1, source_target_pairs={{0,16},{4,20},{8,24},{12,28},{16,0},{20,4},{24,8},{28,12},{1,17},{... | collective-permute-start | bytes 393224 | tf_op jit(solution)/shard_map/ppermute | solution.py:17
  273.7 3.5 collective-permute-done.67
  280.5 7.7 %collective-permute-done.73 = f32[128,256]{1,0:T(8,128)S(1)} collective-permute-done((f32[128,256]{1,0:T(8,128)S(1)}, f32[128,256]{1,0:T(8,128)S(1)}, u32[]{:S(2)}, u32[]{:S(2)}) %collective-permute-start.73) | collective-permute-done | bytes 131104 | tf_op jit(solution)/shard_map/ppermute | solution.py:17
  317.6 3.6 collective-permute-done.42
  324.3 7.4 %collective-permute-done.25 = bf16[128,512]{0,1:T(8,128)(2,1)S(1)} collective-permute-done((bf16[128,512]{0,1:T(8,128)(2,1)S(1)}, bf16[128,512]{0,1:T(8,128)(2,1)S(1)}, u32[]{:S(2)}, u32[]{:S(2)}) %collective-permute-start.25) | collective-permute-done | bytes 131104 | tf_op jit(solution)/shard_map/ppermute | solution.py:17
  332.7 4.0 %collective-permute-done.22 = bf16[128,512]{0,1:T(8,128)(2,1)S(1)} collective-permute-done((bf16[128,512]{0,1:T(8,128)(2,1)S(1)}, bf16[128,512]{0,1:T(8,128)(2,1)S(1)}, u32[]{:S(2)}, u32[]{:S(2)}) %collective-permute-start.22) | collective-permute-done | bytes 131104 | tf_op jit(solution)/shard_map/ppermute | solution.py:17
  337.4 4.2 %collective-permute-done.43 = bf16[128,512]{0,1:T(8,128)(2,1)S(1)} collective-permute-done((bf16[128,512]{0,1:T(8,128)(2,1)S(1)}, bf16[128,512]{0,1:T(8,128)(2,1)S(1)}, u32[]{:S(2)}, u32[]{:S(2)}) %collective-permute-start.43) | collective-permute-done | bytes 131104 | tf_op jit(solution)/shard_map/ppermute | solution.py:17
  342.6 5.4 %collective-permute-done.40 = bf16[128,512]{0,1:T(8,128)(2,1)S(1)} collective-permute-done((bf16[128,512]{0,1:T(8,128)(2,1)S(1)}, bf16[128,512]{0,1:T(8,128)(2,1)S(1)}, u32[]{:S(2)}, u32[]{:S(2)}) %collective-permute-start.40) | collective-permute-done | bytes 131104 | tf_op jit(solution)/shard_map/ppermute | solution.py:17
  349.0 5.0 %collective-permute-start.26 = (bf16[128,512]{0,1:T(8,128)(2,1)S(1)}, bf16[128,512]{0,1:T(8,128)(2,1)S(1)}, u32[]{:S(2)}, u32[]{:S(2)}) collective-permute-start(bf16[128,512]{0,1:T(8,128)(2,1)S(1)} %fusion.22), channel_id=1, source_target_pairs={{0,0},{1,10},{2,17},{3,27},{4,4},{5,14},{6,21},{7,31},{8,1},{9,11}... | collective-permute-start | bytes 393224 | tf_op jit(solution)/shard_map/ppermute | solution.py:333
  354.3 4.7 %collective-permute-start.23 = (bf16[128,512]{0,1:T(8,128)(2,1)S(1)}, bf16[128,512]{0,1:T(8,128)(2,1)S(1)}, u32[]{:S(2)}, u32[]{:S(2)}) collective-permute-start(bf16[128,512]{0,1:T(8,128)(2,1)S(1)} %fusion.23), channel_id=1, source_target_pairs={{0,0},{1,10},{2,17},{3,27},{4,4},{5,14},{6,21},{7,31},{8,1},{9,11}... | collective-permute-start | bytes 393224 | tf_op jit(solution)/shard_map/ppermute | solution.py:333
  365.1 5.6 %collective-permute-start.44 = (bf16[128,512]{0,1:T(8,128)(2,1)S(1)}, bf16[128,512]{0,1:T(8,128)(2,1)S(1)}, u32[]{:S(2)}, u32[]{:S(2)}) collective-permute-start(bf16[128,512]{0,1:T(8,128)(2,1)S(1)} %fusion.20), channel_id=1, source_target_pairs={{0,0},{1,10},{2,17},{3,27},{4,4},{5,14},{6,21},{7,31},{8,1},{9,11}... | collective-permute-start | bytes 393224 | tf_op jit(solution)/shard_map/ppermute | solution.py:333
  371.8 5.3 %collective-permute-start.41 = (bf16[128,512]{0,1:T(8,128)(2,1)S(1)}, bf16[128,512]{0,1:T(8,128)(2,1)S(1)}, u32[]{:S(2)}, u32[]{:S(2)}) collective-permute-start(bf16[128,512]{0,1:T(8,128)(2,1)S(1)} %fusion.21), channel_id=1, source_target_pairs={{0,0},{1,10},{2,17},{3,27},{4,4},{5,14},{6,21},{7,31},{8,1},{9,11}... | collective-permute-start | bytes 393224 | tf_op jit(solution)/shard_map/ppermute | solution.py:333
  377.2 3.7 collective-permute-start.62
  386.7 3.8 collective-permute-done.59
  (289 shorter events, 123.3 us)
Async XLA Ops:
  6.1 21.4 %collective-permute-start.9 = (bf16[256,256]{1,0:T(8,128)(2,1)S(1)}, bf16[256,256]{1,0:T(8,128)(2,1)S(1)}, u32[]{:S(2)}, u32[]{:S(2)}) collective-permute-start(bf16[256,256]{1,0:T(8,128)(2,1)S(1)} %get-tuple-element.60), channel_id=1, source_target_pairs={{0,1},{1,0},{2,3},{3,2},{4,5},{5,4},{6,7},{7,6},{8,9},{9,8},{10,11... | collective-permute-start | bytes 393224 | tf_op jit(solution)/shard_map/ppermute | solution.py:17
  6.9 20.6 %collective-permute-start.12 = (bf16[256,256]{1,0:T(8,128)(2,1)S(1)}, bf16[256,256]{1,0:T(8,128)(2,1)S(1)}, u32[]{:S(2)}, u32[]{:S(2)}) collective-permute-start(bf16[256,256]{1,0:T(8,128)(2,1)S(1)} %get-tuple-element.60), channel_id=1, source_target_pairs={{0,2},{1,3},{2,0},{3,1},{4,6},{5,7},{6,4},{7,5},{8,10},{9,11},{10,... | collective-permute-start | bytes 393224 | tf_op jit(solution)/shard_map/ppermute | solution.py:17
  11.7 15.9 %collective-permute-start.13 = (bf16[256,256]{1,0:T(8,128)(2,1)S(1)}, bf16[256,256]{1,0:T(8,128)(2,1)S(1)}, u32[]{:S(2)}, u32[]{:S(2)}) collective-permute-start(bf16[256,256]{1,0:T(8,128)(2,1)S(1)} %get-tuple-element.60), channel_id=1, source_target_pairs={{0,3},{1,2},{2,1},{3,0},{4,7},{5,6},{6,5},{7,4},{8,11},{9,10},{10,... | collective-permute-start | bytes 393224 | tf_op jit(solution)/shard_map/ppermute | solution.py:17
  32.0 27.5 %collective-permute-start.10 = (bf16[512,256]{1,0:T(8,128)(2,1)S(1)}, bf16[512,256]{1,0:T(8,128)(2,1)S(1)}, u32[]{:S(2)}, u32[]{:S(2)}) collective-permute-start(bf16[512,256]{1,0:T(8,128)(2,1)S(1)} %pad_maximum_fusion.8), channel_id=1, source_target_pairs={{0,8},{4,12},{8,0},{12,4},{16,24},{20,28},{24,16},{28,20},{1,9},{5... | collective-permute-start | bytes 786440 | tf_op jit(solution)/shard_map/ppermute | solution.py:17
  33.6 27.3 %collective-permute-start.14 = (bf16[512,256]{1,0:T(8,128)(2,1)S(1)}, bf16[512,256]{1,0:T(8,128)(2,1)S(1)}, u32[]{:S(2)}, u32[]{:S(2)}) collective-permute-start(bf16[512,256]{1,0:T(8,128)(2,1)S(1)} %pad_maximum_fusion.9), channel_id=1, source_target_pairs={{0,16},{4,20},{8,24},{12,28},{16,0},{20,4},{24,8},{28,12},{1,17},{... | collective-permute-start | bytes 786440 | tf_op jit(solution)/shard_map/ppermute | solution.py:17
  58.0 25.9 %collective-permute-start.46 = (bf16[512,256]{1,0:T(8,128)(2,1)S(1)}, bf16[512,256]{1,0:T(8,128)(2,1)S(1)}, u32[]{:S(2)}, u32[]{:S(2)}) collective-permute-start(bf16[512,256]{1,0:T(8,128)(2,1)S(1)} %pad_maximum_fusion.12), channel_id=1, source_target_pairs={{0,8},{4,12},{8,0},{12,4},{16,24},{20,28},{24,16},{28,20},{1,9},{5... | collective-permute-start | bytes 786440 | tf_op jit(solution)/shard_map/ppermute | solution.py:17
  59.5 25.0 %collective-permute-start.50 = (bf16[512,256]{1,0:T(8,128)(2,1)S(1)}, bf16[512,256]{1,0:T(8,128)(2,1)S(1)}, u32[]{:S(2)}, u32[]{:S(2)}) collective-permute-start(bf16[512,256]{1,0:T(8,128)(2,1)S(1)} %pad_maximum_fusion.13), channel_id=1, source_target_pairs={{0,16},{4,20},{8,24},{12,28},{16,0},{20,4},{24,8},{28,12},{1,17},{... | collective-permute-start | bytes 786440 | tf_op jit(solution)/shard_map/ppermute | solution.py:17
  60.9 22.2 %collective-permute-start.11 = (bf16[1024,256]{1,0:T(8,128)(2,1)S(1)}, bf16[1024,256]{1,0:T(8,128)(2,1)S(1)}, u32[]{:S(2)}, u32[]{:S(2)}) collective-permute-start(bf16[1024,256]{1,0:T(8,128)(2,1)S(1)} %pad_maximum_fusion.2), channel_id=1, source_target_pairs={{0,16},{4,20},{8,24},{12,28},{16,0},{20,4},{24,8},{28,12},{1,17},{... | collective-permute-start | bytes 1572872 | tf_op jit(solution)/shard_map/ppermute | solution.py:17
  61.8 21.4 %collective-permute-start.15 = (bf16[1024,256]{1,0:T(8,128)(2,1)S(1)}, bf16[1024,256]{1,0:T(8,128)(2,1)S(1)}, u32[]{:S(2)}, u32[]{:S(2)}) collective-permute-start(bf16[1024,256]{1,0:T(8,128)(2,1)S(1)} %pad_maximum_fusion.3), channel_id=1, source_target_pairs={{0,8},{4,12},{8,0},{12,4},{16,24},{20,28},{24,16},{28,20},{1,9},{5... | collective-permute-start | bytes 1572872 | tf_op jit(solution)/shard_map/ppermute | solution.py:17
  66.5 24.0 %collective-permute-start.29 = (bf16[1024,256]{1,0:T(8,128)(2,1)S(1)}, bf16[1024,256]{1,0:T(8,128)(2,1)S(1)}, u32[]{:S(2)}, u32[]{:S(2)}) collective-permute-start(bf16[1024,256]{1,0:T(8,128)(2,1)S(1)} %pad_maximum_fusion.4), channel_id=1, source_target_pairs={{0,16},{4,20},{8,24},{12,28},{16,0},{20,4},{24,8},{28,12},{1,17},{... | collective-permute-start | bytes 1572872 | tf_op jit(solution)/shard_map/ppermute | solution.py:17
  83.2 25.9 %collective-permute-start.16 = (bf16[2048,256]{1,0:T(8,128)(2,1)S(1)}, bf16[2048,256]{1,0:T(8,128)(2,1)S(1)}, u32[]{:S(2)}, u32[]{:S(2)}) collective-permute-start(bf16[2048,256]{1,0:T(8,128)(2,1)S(1)} %pad_maximum_fusion.p0), channel_id=1, source_target_pairs={{0,4},{4,0},{8,12},{12,8},{16,20},{20,16},{24,28},{28,24},{1,5},{5... | collective-permute-start | bytes 3145736 | tf_op jit(solution)/shard_map/ppermute | solution.py:17
  83.3 26.4 %collective-permute-start.17 = (bf16[2048,256]{1,0:T(8,128)(2,1)S(1)}, bf16[2048,256]{1,0:T(8,128)(2,1)S(1)}, u32[]{:S(2)}, u32[]{:S(2)}) collective-permute-start(bf16[2048,256]{1,0:T(8,128)(2,1)S(1)} %constant_dynamic-update-slice_fusion.10.p1), channel_id=1, source_target_pairs={{0,4},{4,0},{8,12},{12,8},{16,20},{20,16},{24,28},{28,24},{1,5},{5... | collective-permute-start | bytes 3145736 | tf_op jit(solution)/shard_map/ppermute | solution.py:17
  90.5 18.6 %collective-permute-start.51 = (bf16[1024,256]{1,0:T(8,128)(2,1)S(1)}, bf16[1024,256]{1,0:T(8,128)(2,1)S(1)}, u32[]{:S(2)}, u32[]{:S(2)}) collective-permute-start(bf16[1024,256]{1,0:T(8,128)(2,1)S(1)} %pad_maximum_fusion.7), channel_id=1, source_target_pairs={{0,8},{4,12},{8,0},{12,4},{16,24},{20,28},{24,16},{28,20},{1,9},{5... | collective-permute-start | bytes 1572872 | tf_op jit(solution)/shard_map/ppermute | solution.py:17
  98.8 51.0 %collective-permute-start.34 = (bf16[2048,256]{1,0:T(8,128)(2,1)S(1)}, bf16[2048,256]{1,0:T(8,128)(2,1)S(1)}, u32[]{:S(2)}, u32[]{:S(2)}) collective-permute-start(bf16[2048,256]{1,0:T(8,128)(2,1)S(1)} %constant_dynamic-update-slice_fusion.14.p0), channel_id=1, source_target_pairs={{0,4},{4,0},{8,12},{12,8},{16,20},{20,16},{24,28},{28,24},{1,5},{5... | collective-permute-start | bytes 3145736 | tf_op jit(solution)/shard_map/ppermute | solution.py:17
  100.0 49.9 %collective-permute-start.35 = (bf16[2048,256]{1,0:T(8,128)(2,1)S(1)}, bf16[2048,256]{1,0:T(8,128)(2,1)}, u32[]{:S(2)}, u32[]{:S(2)}) collective-permute-start(bf16[2048,256]{1,0:T(8,128)(2,1)S(1)} %constant_dynamic-update-slice_fusion.18.p1), channel_id=1, source_target_pairs={{0,4},{4,0},{8,12},{12,8},{16,20},{20,16},{24,28},{28,24},{1,5},{5... | collective-permute-start | bytes 3145736 | tf_op jit(solution)/shard_map/ppermute | solution.py:17
  109.1 82.1 %collective-permute-start.52 = (bf16[2048,256]{1,0:T(8,128)(2,1)S(1)}, bf16[2048,256]{1,0:T(8,128)(2,1)S(1)}, u32[]{:S(2)}, u32[]{:S(2)}) collective-permute-start(bf16[2048,256]{1,0:T(8,128)(2,1)S(1)} %constant_dynamic-update-slice_fusion.22.p0), channel_id=1, source_target_pairs={{0,4},{4,0},{8,12},{12,8},{16,20},{20,16},{24,28},{28,24},{1,5},{5... | collective-permute-start | bytes 3145736 | tf_op jit(solution)/shard_map/ppermute | solution.py:17
  109.1 82.1 %collective-permute-start.53 = (bf16[2048,256]{1,0:T(8,128)(2,1)S(1)}, bf16[2048,256]{1,0:T(8,128)(2,1)S(1)}, u32[]{:S(2)}, u32[]{:S(2)}) collective-permute-start(bf16[2048,256]{1,0:T(8,128)(2,1)S(1)} %constant_dynamic-update-slice_fusion.26.p1), channel_id=1, source_target_pairs={{0,4},{4,0},{8,12},{12,8},{16,20},{20,16},{24,28},{28,24},{1,5},{5... | collective-permute-start | bytes 3145736 | tf_op jit(solution)/shard_map/ppermute | solution.py:17
  149.7 98.0 %collective-permute-start.18 = (bf16[2,512,256]{2,1,0:T(8,128)(2,1)}, bf16[2,512,256]{2,1,0:T(8,128)(2,1)}, u32[]{:S(2)}, u32[]{:S(2)}) collective-permute-start(bf16[2,512,256]{2,1,0:T(8,128)(2,1)} %get-tuple-element.31), channel_id=1, source_target_pairs={{0,1},{1,0},{2,3},{3,2},{4,5},{5,4},{6,7},{7,6},{8,9},{9,8},{10,11... | collective-permute-start | bytes 1572872 | tf_op jit(solution)/shard_map/ppermute | solution.py:17
  149.7 40.8 %collective-permute-start.63 = (f32[128,256]{1,0:T(8,128)}, f32[128,256]{1,0:T(8,128)S(1)}, u32[]{:S(2)}, u32[]{:S(2)}) collective-permute-start(f32[128,256]{1,0:T(8,128)} %get-tuple-element.49), channel_id=1, source_target_pairs={{0,4},{4,0},{8,12},{12,8},{16,20},{20,16},{24,28},{28,24},{1,5},{5... | collective-permute-start | bytes 393224 | tf_op jit(solution)/shard_map/ppermute | solution.py:17
  190.1 43.2 %collective-permute-start.69 = (f32[128,256]{1,0:T(8,128)}, f32[128,256]{1,0:T(8,128)S(1)}, u32[]{:S(2)}, u32[]{:S(2)}) collective-permute-start(f32[128,256]{1,0:T(8,128)} %get-tuple-element.51), channel_id=1, source_target_pairs={{0,4},{4,0},{8,12},{12,8},{16,20},{20,16},{24,28},{28,24},{1,5},{5... | collective-permute-start | bytes 393224 | tf_op jit(solution)/shard_map/ppermute | solution.py:17
  190.6 44.2 %collective-permute-start.64 = (f32[128,256]{1,0:T(8,128)S(1)}, f32[128,256]{1,0:T(8,128)S(1)}, u32[]{:S(2)}, u32[]{:S(2)}) collective-permute-start(f32[128,256]{1,0:T(8,128)S(1)} %add.186), channel_id=1, source_target_pairs={{0,8},{4,12},{8,0},{12,4},{16,24},{20,28},{24,16},{28,20},{1,9},{5... | collective-permute-start | bytes 393224 | tf_op jit(solution)/shard_map/ppermute | solution.py:17
  231.2 35.6 %collective-permute-start.36 = (bf16[2,512,256]{2,1,0:T(8,128)(2,1)S(1)}, bf16[2,512,256]{2,1,0:T(8,128)(2,1)S(1)}, u32[]{:S(2)}, u32[]{:S(2)}) collective-permute-start(bf16[2,512,256]{2,1,0:T(8,128)(2,1)S(1)} %copy-done.13), channel_id=1, source_target_pairs={{0,1},{1,0},{2,3},{3,2},{4,5},{5,4},{6,7},{7,6},{8,9},{9,8},{10,11... | collective-permute-start | bytes 1572872 | tf_op jit(solution)/shard_map/ppermute | solution.py:17
  242.2 50.7 %collective-permute-start.20 = (bf16[4,256,512]{2,1,0:T(8,128)(2,1)}, bf16[4,256,512]{2,1,0:T(8,128)(2,1)S(1)}, u32[]{:S(2)}, u32[]{:S(2)}) collective-permute-start(bf16[4,256,512]{2,1,0:T(8,128)(2,1)} %get-tuple-element.33), channel_id=1, source_target_pairs={{0,4},{4,0},{8,12},{12,8},{16,20},{20,16},{24,28},{28,24},{1,5},{5... | collective-permute-start | bytes 3145736 | tf_op jit(solution)/shard_map/ppermute | solution.py:17
  242.8 35.8 %collective-permute-start.54 = (bf16[2,512,256]{2,1,0:T(8,128)(2,1)}, bf16[2,512,256]{2,1,0:T(8,128)(2,1)S(1)}, u32[]{:S(2)}, u32[]{:S(2)}) collective-permute-start(bf16[2,512,256]{2,1,0:T(8,128)(2,1)} %get-tuple-element.45), channel_id=1, source_target_pairs={{0,1},{1,0},{2,3},{3,2},{4,5},{5,4},{6,7},{7,6},{8,9},{9,8},{10,11... | collective-permute-start | bytes 1572872 | tf_op jit(solution)/shard_map/ppermute | solution.py:17
  251.5 46.7 %collective-permute-start.38 = (bf16[4,256,512]{2,1,0:T(8,128)(2,1)}, bf16[4,256,512]{2,1,0:T(8,128)(2,1)}, u32[]{:S(2)}, u32[]{:S(2)}) collective-permute-start(bf16[4,256,512]{2,1,0:T(8,128)(2,1)} %get-tuple-element.40), channel_id=1, source_target_pairs={{0,4},{4,0},{8,12},{12,8},{16,20},{20,16},{24,28},{28,24},{1,5},{5... | collective-permute-start | bytes 3145736 | tf_op jit(solution)/shard_map/ppermute | solution.py:17
  289.8 69.4 %collective-permute-start.19 = (bf16[512,256]{1,0:T(8,128)(2,1)}, bf16[512,256]{1,0:T(8,128)(2,1)}, u32[]{:S(2)}, u32[]{:S(2)}) collective-permute-start(bf16[512,256]{1,0:T(8,128)(2,1)} %slice_bitcast_fusion.10), channel_id=1, source_target_pairs={{0,2},{1,3},{2,0},{3,1},{4,6},{5,7},{6,4},{7,5},{8,10},{9,11},{10,... | collective-permute-start | bytes 786440 | tf_op jit(solution)/shard_map/ppermute | solution.py:17
  289.8 91.1 %collective-permute-start.37 = (bf16[512,256]{1,0:T(8,128)(2,1)}, bf16[512,256]{1,0:T(8,128)(2,1)}, u32[]{:S(2)}, u32[]{:S(2)}) collective-permute-start(bf16[512,256]{1,0:T(8,128)(2,1)} %slice_bitcast_fusion.6), channel_id=1, source_target_pairs={{0,2},{1,3},{2,0},{3,1},{4,6},{5,7},{6,4},{7,5},{8,10},{9,11},{10,... | collective-permute-start | bytes 786440 | tf_op jit(solution)/shard_map/ppermute | solution.py:17
  295.3 89.4 %collective-permute-start.55 = (bf16[512,256]{1,0:T(8,128)(2,1)}, bf16[512,256]{1,0:T(8,128)(2,1)}, u32[]{:S(2)}, u32[]{:S(2)}) collective-permute-start(bf16[512,256]{1,0:T(8,128)(2,1)} %slice_bitcast_fusion.2), channel_id=1, source_target_pairs={{0,2},{1,3},{2,0},{3,1},{4,6},{5,7},{6,4},{7,5},{8,10},{9,11},{10,... | collective-permute-start | bytes 786440 | tf_op jit(solution)/shard_map/ppermute | solution.py:17
  298.2 16.9 %collective-permute-start.24 = (bf16[2,128,512]{1,2,0:T(8,128)(2,1)}, bf16[2,128,512]{1,2,0:T(8,128)(2,1)}, u32[]{:S(2)}, u32[]{:S(2)}) collective-permute-start(bf16[2,128,512]{1,2,0:T(8,128)(2,1)} %bitcast.17), channel_id=1, source_target_pairs={{0,16},{4,20},{8,24},{12,28},{16,0},{20,4},{24,8},{28,12},{1,17},{... | collective-permute-start | bytes 786440 | tf_op jit(solution)/shard_map/ppermute | solution.py:17
  321.2 27.8 %collective-permute-start.57 = (bf16[2,128,512]{1,2,0:T(8,128)(2,1)S(1)}, bf16[2,128,512]{1,2,0:T(8,128)(2,1)S(1)}, u32[]{:S(2)}, u32[]{:S(2)}) collective-permute-start(bf16[2,128,512]{1,2,0:T(8,128)(2,1)S(1)} %copy-done.10), channel_id=1, source_target_pairs={{0,8},{4,12},{8,0},{12,4},{16,24},{20,28},{24,16},{28,20},{1,9},{5... | collective-permute-start | bytes 786440 | tf_op jit(solution)/shard_map/ppermute | solution.py:17
  361.6 15.6 %collective-permute-start.58 = (bf16[128,512]{0,1:T(8,128)(2,1)S(1)}, bf16[128,512]{0,1:T(8,128)(2,1)S(1)}, u32[]{:S(2)}, u32[]{:S(2)}) collective-permute-start(bf16[128,512]{0,1:T(8,128)(2,1)S(1)} %slice_bitcast_fusion.14), channel_id=1, source_target_pairs={{0,16},{4,20},{8,24},{12,28},{16,0},{20,4},{24,8},{28,12},{1,17},{... | collective-permute-start | bytes 393224 | tf_op jit(solution)/shard_map/ppermute | solution.py:17
  365.1 18.5 %collective-permute-start.44 = (bf16[128,512]{0,1:T(8,128)(2,1)S(1)}, bf16[128,512]{0,1:T(8,128)(2,1)S(1)}, u32[]{:S(2)}, u32[]{:S(2)}) collective-permute-start(bf16[128,512]{0,1:T(8,128)(2,1)S(1)} %fusion.20), channel_id=1, source_target_pairs={{0,0},{1,10},{2,17},{3,27},{4,4},{5,14},{6,21},{7,31},{8,1},{9,11}... | collective-permute-start | bytes 393224 | tf_op jit(solution)/shard_map/ppermute | solution.py:333
  (63 other events, 647.9 us)

commit v2 on v0

v2 whole, which is shorter than its diff:
```python
import functools

import jax
import jax.numpy as jnp
from jax import lax
from jax.experimental import pallas as pl
from jax.experimental.pallas import tpu as pltpu
from jax.sharding import PartitionSpec as P

LANES = 128
BF = jnp.bfloat16
F32 = jnp.float32


def swap(x, axis, bit):
    count = lax.axis_size(axis)
    return lax.ppermute(x, axis, [(i, i ^ bit) for i in range(count)])


def row_bits(row_count):
    return [b for b in (1 << n for n in range(1, 20)) if b < row_count]


def join_kernel(counts, *refs):
    outs = refs[len(refs) - len(counts) :]
    refs = iter(refs)
    for count, out in zip(counts, outs):
        at = 0
        for _ in range(count):
            ref = next(refs)
            out[at : at + ref.shape[0]] = ref[...]
            at += ref.shape[0]


def join(groups, marks=()):
    flat = [x for group in groups for x in group]
    vmem = pl.BlockSpec(memory_space=pltpu.VMEM)
    size = 2 * sum(x.size for x in flat)
    return pl.pallas_call(
        functools.partial(join_kernel, [len(group) for group in groups]),
        in_specs=[vmem] * (len(flat) + len(marks)),
        out_specs=[vmem] * len(groups),
        out_shape=[
            jax.ShapeDtypeStruct((sum(x.shape[0] for x in group), group[0].shape[1]), BF)
            for group in groups
        ],
        compiler_params=pltpu.CompilerParams(vmem_limit_bytes=24 * 2**20),
        cost_estimate=pl.CostEstimate(flops=0, bytes_accessed=2 * size, transcendentals=0),
    )(*flat, *marks)


def gather(owns, marks):
    col_count = lax.axis_size("col")
    bits = row_bits(lax.axis_size("row"))
    half = col_count // 2
    rounds = len(bits) + 1
    state = [None] * len(owns)
    sent = owns[0]
    for tick in range(rounds + len(owns) - 1):
        groups, places = [], []
        for n in range(len(owns)):
            step = tick - n
            if step == 0:
                line = [sent] + [swap(sent, "col", d) for d in range(1, col_count)]
                state[n] = [line[:half], line[half:]]
            elif 0 < step < rounds:
                first, second = state[n]
                state[n] = [
                    [first, swap(first, "row", bits[step - 1])],
                    [second, swap(second, "row", bits[-step])],
                ]
            else:
                continue
            for side in range(2):
                places.append((n, side))
                groups.append(state[n][side])
        if tick + 1 < len(owns):
            groups.append([owns[tick + 1]])
        joined = join(groups, tuple(marks[tick : tick + 1]))
        if tick + 1 < len(owns):
            sent = joined[-1]
        for (n, side), value in zip(places, joined):
            state[n][side] = value
        done = tick - rounds + 1
        if done >= 0:
            first, second = state[done]
            yield [first, second, swap(first, "row", 1), swap(second, "row", 1)]


def invert_kernel(listed, sibs, p0, p1, p2, p3, out_ref):
    pieces = (p0, p1, p2, p3)
    lines = out_ref.shape[1]
    count, _, wide = p0.shape
    line_ids = lax.broadcasted_iota(jnp.int32, (lines, wide), 0).astype(F32)
    lane_ids = lax.broadcasted_iota(jnp.int32, (LANES, wide), 0).astype(F32)
    for s in range(sibs):
        total = jnp.zeros((lines, 2 * LANES), F32)
        for n, piece in enumerate(pieces):
            left, right = [], []
            for m in range(count):
                code = piece[m, listed:, :].astype(F32)
                place = 1 + (n * count + m) * listed
                place = place + lax.broadcasted_iota(jnp.int32, (1, wide), 1)
                high = (place // LANES).astype(F32)
                low = (place % LANES).astype(F32)
                left.append(jnp.where(line_ids == code[2 * s : 2 * s + 1], 1.0, 0.0))
                on_lane = lane_ids == code[2 * s + 1 : 2 * s + 2]
                right.append(
                    jnp.concatenate(
                        [jnp.where(on_lane, high, 0.0), jnp.where(on_lane, low, 0.0)], 0
                    )
                )
            total += lax.dot_general(
                jnp.concatenate(left, 1).astype(BF),
                jnp.concatenate(right, 1).astype(BF),
                (((1,), (1,)), ((), ())),
                preferred_element_type=F32,
            )
        out_ref[s] = (total[:, :LANES] * LANES + total[:, LANES:]).astype(jnp.int32)


def invert(pieces, chunk, codes, sibs, rows):
    width = pieces[0].shape[1]
    pieces = [p.reshape(-1, chunk + codes, width) for p in pieces]
    vmem = pl.BlockSpec(memory_space=pltpu.VMEM)
    return pl.pallas_call(
        functools.partial(invert_kernel, chunk, sibs),
        in_specs=[vmem] * 4,
        out_specs=pl.BlockSpec(memory_space=pltpu.VMEM),
        out_shape=jax.ShapeDtypeStruct((sibs, rows // LANES, LANES), jnp.int32),
        compiler_params=pltpu.CompilerParams(vmem_limit_bytes=16 * 2**20),
        cost_estimate=pl.CostEstimate(
            flops=4 * 10**9, bytes_accessed=4 * sibs * rows, transcendentals=0
        ),
    )(*pieces)


def tables_kernel(chunk, row_inv, col_inv, p0, p1, p2, p3, *refs):
    row_out, col_out, mark, source, target = refs[-5:]
    mark[...] = jnp.zeros_like(mark)
    step = 256
    width = col_out.shape[1]
    parts = width // LANES
    count = p0.shape[0]
    source[0 : 8 * parts, :] = jnp.zeros((8 * parts, LANES), F32)
    for n, piece in enumerate((p0, p1, p2, p3)):

        def fill(m, unused, n=n, piece=piece):
            values = piece[m, :chunk, :].astype(F32)
            base = parts * (1 + (n * count + m) * chunk)
            for q in range(parts):
                source[pl.ds(base + q, chunk, stride=parts), :] = values[
                    :, q * LANES : (q + 1) * LANES
                ]
            return unused

        lax.fori_loop(0, count, fill, 0)

    def pick(inv):
        batch = 16

        def line(h, unused):
            for first in range(0, LANES, batch):
                found = [
                    source[pl.ds(pl.multiple_of(parts * inv[h, first + u], parts), parts), :]
                    for u in range(batch)
                ]
                for u in range(batch):
                    target[
                        pl.ds(pl.multiple_of(parts * (h * LANES + first + u), parts), parts), :
                    ] = found[u]
            return unused

        lax.fori_loop(0, inv.shape[0], line, 0)

    pick(row_inv)
    for n in range(row_out.shape[1] // step):
        for q in range(parts):
            values = target[pl.ds(parts * n * step + q, step, stride=parts), :]
            row_out[q * LANES : (q + 1) * LANES, n * step : (n + 1) * step] = values.T.astype(BF)
    pick(col_inv)

    def drain(n, unused):
        at = pl.multiple_of(n * step, step)
        for q in range(parts):
            values = target[pl.ds(parts * at + q, step, stride=parts), :]
            col_out[pl.ds(at, step), q * LANES : (q + 1) * LANES] = values.astype(BF)
        return unused

    lax.fori_loop(0, col_out.shape[0] // step, drain, 0)


def tables(pieces, chunk, whole_chunk, row_inv, col_inv, marks):
    width = pieces[0].shape[1]
    pieces = [p.reshape(-1, whole_chunk, width) for p in pieces]
    count = pieces[0].shape[0]
    listed = 4 * count * chunk
    parts = width // LANES
    rows, cols = row_inv.size, col_inv.size
    vmem = pl.BlockSpec(memory_space=pltpu.VMEM)
    smem = pl.BlockSpec(memory_space=pltpu.SMEM)
    return pl.pallas_call(
        functools.partial(tables_kernel, chunk),
        in_specs=[smem, smem] + [vmem] * (4 + len(marks)),
        out_specs=[vmem] * 3,
        out_shape=[
            jax.ShapeDtypeStruct((width, rows), BF),
            jax.ShapeDtypeStruct((cols, width), BF),
            jax.ShapeDtypeStruct((8, LANES), F32),
        ],
        scratch_shapes=[
            pltpu.VMEM((parts * (listed + 8), LANES), F32),
            pltpu.VMEM((parts * max(rows, cols), LANES), F32),
        ],
        compiler_params=pltpu.CompilerParams(vmem_limit_bytes=28 * 2**20),
        cost_estimate=pl.CostEstimate(
            flops=10**10, bytes_accessed=2 * width * (listed + rows + cols), transcendentals=0
        ),
    )(row_inv, col_inv, *pieces, *marks)


def block_kernel(ancestor, lower, diagonal, mark, held, arrived, left):
    mark[...] = jnp.zeros_like(mark)
    rows, cols = lower.shape
    step = 256
    wide = 512 if cols % 512 == 0 else cols
    row_start = lax.axis_index("row") * rows
    col_start = lax.axis_index("col") * cols
    ins, outs = [], []
    for n in range(0, rows, step):
        here = held.at[n : n + step]
        ins.append(pltpu.make_async_copy(ancestor.at[n : n + step], here, arrived.at[n // step]))
        outs.append(pltpu.make_async_copy(here, lower.at[n : n + step], left.at[n // step]))
    for copy in ins:
        copy.start()
    diagonal[...] = jnp.zeros_like(diagonal)
    for n in range(rows // step):
        ins[n].wait()
        row_first = row_start + n * step
        at = slice(n * step, (n + 1) * step)

        def strip(m, unused, row_first=row_first, at=at):
            first = pl.multiple_of(m * wide, wide)
            over = pl.ds(first, wide)
            col_first = col_start + first
            empty = row_first + step <= col_first

            @pl.when(empty)
            def none():
                held[at, over] = jnp.zeros((step, wide), BF)

            @pl.when(jnp.logical_not(empty) & (row_first < col_first + wide))
            def some():
                row_ids = row_first + lax.broadcasted_iota(jnp.int32, (step, wide), 0)
                col_ids = col_first + lax.broadcasted_iota(jnp.int32, (step, wide), 1)
                values = held[at, over].astype(F32)
                on = jnp.where(col_ids == row_ids, values, 0.0)
                diagonal[at, :] += jnp.sum(on, axis=1, keepdims=True)
                held[at, over] = jnp.where(col_ids < row_ids, values, 0.0).astype(BF)

            return unused

        lax.fori_loop(0, cols // wide, strip, 0)
        outs[n].start()
    for copy in outs:
        copy.wait()


def lower_block(ancestor):
    rows, cols = ancestor.shape
    anywhere = pl.BlockSpec(memory_space=pl.ANY)
    return pl.pallas_call(
        block_kernel,
        in_specs=[anywhere],
        out_specs=[pl.BlockSpec(memory_space=pltpu.HBM)] + [pl.BlockSpec(memory_space=pltpu.VMEM)] * 2,
        out_shape=[
            jax.ShapeDtypeStruct((rows, cols), BF),
            jax.ShapeDtypeStruct((rows, 1), F32),
            jax.ShapeDtypeStruct((8, LANES), F32),
        ],
        scratch_shapes=[
            pltpu.VMEM((rows, cols), BF),
            pltpu.SemaphoreType.DMA((rows // 256,)),
            pltpu.SemaphoreType.DMA((rows // 256,)),
        ],
        compiler_params=pltpu.CompilerParams(vmem_limit_bytes=24 * 2**20),
        cost_estimate=pl.CostEstimate(
            flops=rows * cols, bytes_accessed=4 * rows * cols, transcendentals=0
        ),
    )(ancestor)


def terms_kernel(plan, block, diagonal, row_t, col, *refs):
    m_send, m_keep, d_send, d_keep, y_send, y_keep, total, rounded = refs[-8:]
    i = pl.program_id(0)
    steps = pl.num_programs(0)
    rows = block.shape[0]
    owned = m_send.shape[2]
    tile = 2 * owned
    width = row_t.shape[0]
    place, core, swapped, offset = [plan[steps + n] for n in range(4)]
    at_tile = pl.ds(pl.multiple_of(plan[i] * tile, tile), tile)
    values = col[at_tile, :]

    def mirrored(out):
        term = jnp.dot(row_t[...], block[...], preferred_element_type=F32).astype(BF)
        out[swapped] = term[:, :owned]
        out[1 - swapped] = term[:, owned:]

    @pl.when(i < steps // 2)
    def sent():
        mirrored(m_send)

    @pl.when(i >= steps // 2)
    def kept():
        mirrored(m_keep)

    @pl.when(i == 0)
    def first():
        total[...] = jnp.dot(block[...], values, preferred_element_type=F32)

    @pl.when(i > 0)
    def later():
        total[...] += jnp.dot(block[...], values, preferred_element_type=F32)

    @pl.when(i == steps - 1)
    def last():
        cols = col.shape[0]
        for e in range(rows // owned):
            start = pl.multiple_of((e ^ place) * owned, owned)
            at = pl.ds(start, owned)
            back = pl.multiple_of(jnp.clip(start + offset, 0, cols - owned), owned)
            own = diagonal[at, :] * col[pl.ds(back, owned), :].astype(F32)
            term = total[at, :]
            rounded[at, :] = (term + 0.5 * own).astype(BF)
            term = (term + own).astype(BF)
            if e % 2:
                d_send[e // 2] = term
            else:
                d_keep[e // 2] = term
        y = jnp.dot(row_t[...], rounded[...], preferred_element_type=F32)
        y = y + y.T
        half = width // 2

        @pl.when(core == 0)
        def first_core():
            y_keep[0] = y[:half]
            y_send[0] = y[half:]

        @pl.when(core != 0)
        def second_core():
            y_keep[0] = y[half:]
            y_send[0] = y[:half]


def terms(plan, lower, diagonal, row_t, col, owned, marks):
    rows, cols = lower.shape
    width = col.shape[1]
    steps = cols // (2 * owned)
    half = steps // 2
    count = rows // owned
    everything = [
        pl.BlockSpec(x.shape, lambda i, plan, x=x: (0,) * x.ndim) for x in (diagonal, row_t, col)
    ]
    anywhere = pl.BlockSpec(memory_space=pl.ANY)
    d_spec = pl.BlockSpec((count // 2, owned, width), lambda i, plan: (0, 0, 0))
    y_spec = pl.BlockSpec((1, width // 2, width), lambda i, plan: (0, 0, 0))
    grid_spec = pltpu.PrefetchScalarGridSpec(
        num_scalar_prefetch=1,
        grid=(steps,),
        in_specs=[pl.BlockSpec((rows, 2 * owned), lambda i, plan: (0, plan[i]))]
        + everything
        + [anywhere] * len(marks),
        out_specs=[
            pl.BlockSpec((2, width, owned), lambda i, plan: (jnp.minimum(i, half - 1), 0, 0)),
            pl.BlockSpec((2, width, owned), lambda i, plan: (jnp.maximum(i - half, 0), 0, 0)),
            d_spec,
            d_spec,
            y_spec,
            y_spec,
        ],
        scratch_shapes=[pltpu.VMEM((rows, width), F32), pltpu.VMEM((rows, width), BF)],
    )
    return pl.pallas_call(
        terms_kernel,
        grid_spec=grid_spec,
        out_shape=[
            jax.ShapeDtypeStruct((steps, width, owned), BF),
            jax.ShapeDtypeStruct((steps, width, owned), BF),
            jax.ShapeDtypeStruct((count // 2, owned, width), BF),
            jax.ShapeDtypeStruct((count // 2, owned, width), BF),
            jax.ShapeDtypeStruct((1, width // 2, width), F32),
            jax.ShapeDtypeStruct((1, width // 2, width), F32),
        ],
        compiler_params=pltpu.CompilerParams(vmem_limit_bytes=34 * 2**20),
        cost_estimate=pl.CostEstimate(
            flops=5 * rows * cols * width, bytes_accessed=2 * rows * cols, transcendentals=0
        ),
    )(plan, lower, diagonal, row_t, col, *marks)


def tree_sum(values):
    values = [x.astype(F32) for x in values]
    while len(values) > 1:
        values = [a + b for a, b in zip(values[::2], values[1::2])]
    return values[0]


def sums_kernel(counts, outs, *refs):
    ins, outs_refs = refs[: len(refs) - len(outs)], refs[len(refs) - len(outs) :]
    groups, at = [], 0
    for count in counts:
        groups.append(ins[at : at + count])
        at += count
    for ref, pieces in zip(outs_refs, outs):
        for place, group, slot, low, high in pieces:
            ref[place] = tree_sum([x[slot, low:high] for x in groups[group]]).astype(ref.dtype)


def sums(groups, outs):
    flat = [x for group in groups for x in group]
    shapes = []
    for pieces in outs:
        _, group, _, low, high = pieces[0]
        like = groups[group][0]
        shapes.append(
            jax.ShapeDtypeStruct((len(pieces), high - low, like.shape[2]), like.dtype)
        )
    vmem = pl.BlockSpec(memory_space=pltpu.VMEM)
    size = sum(x.size for x in flat)
    return pl.pallas_call(
        functools.partial(sums_kernel, [len(group) for group in groups], outs),
        in_specs=[vmem] * len(flat),
        out_specs=[vmem] * len(outs),
        out_shape=shapes,
        compiler_params=pltpu.CompilerParams(vmem_limit_bytes=16 * 2**20),
        cost_estimate=pl.CostEstimate(flops=size, bytes_accessed=3 * size, transcendentals=0),
    )(*flat)


def mirrored_share(m_send, m_keep, paths):
    col_bits = lax.axis_size("col").bit_length() - 1
    width, owned = m_keep.shape[1:]
    part = width // paths
    bits = row_bits(lax.axis_size("row"))
    slots = [list(range(len(m_keep))) for _ in range(paths)]
    groups = [(m_keep, swap(m_send, "row", 1))]
    for n in range(col_bits):
        outs = []
        chosen_bits = []
        for path in range(paths):
            place = col_bits - 1 - n if path else n
            chosen_bits.append(bits[place])
            low, group = (part * path, 0) if n == 0 else (0, path)
            for send in (True, False):
                chosen = [i for i, e in enumerate(slots[path]) if bool(e >> place & 1) == send]
                outs.append([(p, group, i, low, low + part) for p, i in enumerate(chosen)])
            slots[path] = [e for e in slots[path] if not e >> place & 1]
        made = yield groups, outs
        groups = [
            (made[2 * path + 1], swap(made[2 * path], "row", chosen_bits[path]))
            for path in range(paths)
        ]
    (own,) = yield groups, [[(path, path, 0, 0, part) for path in range(paths)]]
    return to_owner(own.reshape(width, owned))


def direct_share(d_send, d_keep):
    col_bits = lax.axis_size("col").bit_length() - 1
    owned = d_keep.shape[1]
    groups = [(d_keep, swap(d_send, "col", 1))]
    slots = list(range(len(d_keep)))
    for n in range(1, col_bits):
        bit = 1 << (n - 1)
        outs = []
        for send in (True, False):
            chosen = [i for i, e in enumerate(slots) if bool(e & bit) == send]
            outs.append([(p, 0, i, 0, owned) for p, i in enumerate(chosen)])
        slots = [e for e in slots if not e & bit]
        d_send, d_keep = yield groups, outs
        groups = [(d_keep, swap(d_send, "col", bit << 1))]
    return groups[0]


def diagonal_sum(y_send, y_keep, core, direct):
    rows = y_keep.shape[1]
    whole = [[(0, 0, 0, 0, rows)]]
    (y,) = yield [(y_keep, swap(y_send, "row", 1))], whole
    for axis, first in (("row", 2), ("col", 1)):
        size = lax.axis_size(axis)
        if direct:
            steps = [range(first, size, first)]
        else:
            steps = [[first << n] for n in range((size // first).bit_length() - 1)]
        for step in steps:
            (y,) = yield [(y, *[swap(y, axis, bits) for bits in step])], whole
    other = swap(y, "row", 1)[0]
    return jnp.where(
        core == 0, jnp.concatenate([y[0], other], 0), jnp.concatenate([other, y[0]], 0)
    )


class Rounds:
    def __init__(self, *chains):
        self.chains = chains
        self.results = [None] * len(chains)
        self.jobs = {}
        for n, chain in enumerate(chains):
            self.send(n, None)

    def send(self, n, values):
        try:
            self.jobs[n] = self.chains[n].send(values)
        except StopIteration as end:
            self.jobs.pop(n, None)
            self.results[n] = end.value

    def advance(self):
        groups, outs = [], []
        for job_groups, job_outs in self.jobs.values():
            for pieces in job_outs:
                outs.append([(p, group + len(groups), *rest) for p, group, *rest in pieces])
            groups += job_groups
        made = sums(groups, outs)
        at = 0
        for n, (_, job_outs) in list(self.jobs.items()):
            self.send(n, made[at : at + len(job_outs)])
            at += len(job_outs)
        return made[-1]

    def finish(self):
        while self.jobs:
            self.advance()
        return self.results


def reversed_bits(value, bits):
    return sum(((value >> n) & 1) << (bits - 1 - n) for n in range(bits))


def to_owner(x):
    row_count = lax.axis_size("row")
    col_count = lax.axis_size("col")
    bits = col_count.bit_length() - 1
    pairs = []
    for row in range(row_count):
        for col in range(col_count):
            place = (row // 2) ^ reversed_bits(col, bits)
            pairs.append((row * col_count + col, (2 * col + row % 2) * col_count + place))
    return lax.ppermute(x, ("row", "col"), pairs)


def finish_kernel(member, *refs):
    out = refs[-1]
    owned = out.shape[0]
    sibs = member.shape[0]
    width = out.shape[1] // sibs
    s = 0
    for n in range(0, len(refs) - 1, 3):
        kept, got, mirrored = refs[n : n + 3]
        for at in range(0, mirrored.shape[0], width):
            over = slice(at, at + width)
            product = kept[0, :, over].astype(F32) + got[0, :, over].astype(F32)
            product = product + mirrored[over, :].astype(F32).T
            listed = jnp.broadcast_to(member[s : s + 1, :].astype(F32), (LANES, owned)).T
            for q in range(0, width, LANES):
                out[:, s * width + q : s * width + q + LANES] = jnp.where(
                    listed > 0.5, -product[:, q : q + LANES], 0.0
                ).astype(BF)
            s += 1


def finish(member, shares, width):
    sibs, owned = member.shape
    vmem = pl.BlockSpec(memory_space=pltpu.VMEM)
    flat = [x for share in shares for x in share]
    return pl.pallas_call(
        finish_kernel,
        in_specs=[vmem] * (1 + len(flat)),
        out_specs=vmem,
        out_shape=jax.ShapeDtypeStruct((owned, sibs * width), BF),
        compiler_params=pltpu.CompilerParams(vmem_limit_bytes=24 * 2**20),
        cost_estimate=pl.CostEstimate(
            flops=4 * owned * sibs * width,
            bytes_accessed=8 * owned * sibs * width,
            transcendentals=0,
        ),
    )(member, *flat)


def per_device(ancestor, panels, row_index, diag_inverse):
    row_count = lax.axis_size("row")
    col_count = lax.axis_size("col")
    assert row_count == 2 * col_count
    block_rows, block_cols = ancestor.shape
    sib_count, listed, width = panels.shape
    owned = block_rows // col_count
    row_place = lax.axis_index("row")
    col_place = lax.axis_index("col")
    core = row_place % 2
    chip = row_place // 2
    col_bits = col_count.bit_length() - 1
    row_lines, col_lines, own_lines = block_rows // LANES, block_cols // LANES, owned // LANES
    mixed = chip ^ sum(((col_place >> n) & 1) << (col_bits - 1 - n) for n in range(col_bits))
    pairs = [(2 * n ^ mixed) // 2 for n in range(col_count // 2)]
    plan = jnp.stack(
        [n + (1 - core) * (col_count // 2) for n in pairs]
        + [n + core * (col_count // 2) for n in pairs]
        + [col_place, core, mixed % 2, row_place * block_rows - col_place * block_cols]
    ).astype(jnp.int32)

    codes = jnp.stack([row_index // LANES, row_index % LANES], 1).astype(BF)
    codes = codes.reshape(-1, listed)
    code_rows = -(-len(codes) // 16) * 16
    codes = jnp.pad(
        codes, ((0, code_rows - len(codes)), (0, width - listed)), constant_values=-1
    )
    owns = [jnp.concatenate([panels[0], codes], 0)] + [panels[s] for s in range(1, sib_count)]
    chunks = [listed + code_rows] + [listed] * (sib_count - 1)

    lower, diagonal, mark = lower_block(ancestor)
    marks = [mark] * (len(row_bits(row_count)) + 1)
    gathered = gather(owns, marks)
    both, direct = [], []
    tables_marks, terms_marks = [()] * 2, [()] * 2
    row_inv = col_inv = member = None
    for s in range(sib_count):
        pieces = next(gathered)
        if s == 0:
            inverse = invert(pieces, listed, code_rows, sib_count, block_rows * row_count)
            row_inv = lax.dynamic_slice_in_dim(inverse, row_place * row_lines, row_lines, 1)
            col_inv = lax.dynamic_slice_in_dim(inverse, col_place * col_lines, col_lines, 1)
            own_inv = lax.dynamic_slice_in_dim(
                inverse, row_place * row_lines + col_place * own_lines, own_lines, 1
            )
            member = own_inv.reshape(sib_count, owned)
        last = s == sib_count - 1
        before = ()
        if s > 1:
            before = tuple(chain.advance() for chain in both[:-1] + direct[:-1] if chain.jobs)
        row_t, col, mark = tables(pieces, listed, chunks[s], row_inv[s], col_inv[s], before)
        before = tuple(chain.advance() for chain in both if chain.jobs)
        m_send, m_keep, d_send, d_keep, y_send, y_keep = terms(
            plan, lower, diagonal, row_t, col, owned, before
        )
        marks.append(mark)
        both.append(
            Rounds(
                mirrored_share(m_send, m_keep, 2 if last else 1),
                diagonal_sum(y_send, y_keep, core, last),
            )
        )
        direct.append(Rounds(direct_share(d_send, d_keep)))
    shares, diags = [], []
    for s in range(sib_count):
        mirrored, diag = both[s].finish()
        shares.append((*direct[s].finish()[0], mirrored))
        diags.append(diag)
    return finish(member, shares, width), diag_inverse + jnp.stack(diags)


def solution(mesh):
    in_specs = (P("row", "col"), P(None, ("row", "col"), None), P(None, ("row", "col")), P())
    out_specs = (P(("row", "col"), None), P())
    return jax.shard_map(
        per_device, mesh=mesh, in_specs=in_specs, out_specs=out_specs, check_vma=False
    )
```

time: 851 us -> 293 us (0.34)
  local copies, waits for them, and re-layouts: 380 us -> 8.42 us
  waiting for transfers between devices: 312 us -> 98.2 us
  Pallas kernels: 0 us -> 90.3 us
  starting transfers between devices: 5.4 us -> 92.1 us
  blocking collectives: 70.1 us -> 0 us
  matrix products: 40 us -> 0 us
  other arithmetic: 26.2 us -> 2.75 us
  between operations: 13.9 us -> 1.27 us
    unnamed x16 -> x22, local copies, waits for them, and re-layouts: 306 us -> 7.23 us
    all_to_all x1 -> x0, waiting for transfers between devices: 185 us -> none  [per_device(): lax.all_to_all(mirrored, 'col', split_axis=0, concat_axis=0, tiled=True)]
    ppermute x0 -> x67, waiting for transfers between devices: none -> 98.2 us  [the longest x64 97.8 us: swap(): return lax.ppermute(x, axis, [(i, i ^ bit) for i in range(count)])]
    ppermute x0 -> x67, starting transfers between devices: none -> 92.1 us  [the longest x64 82.9 us: swap(): return lax.ppermute(x, axis, [(i, i ^ bit) for i in range(count)])]
    pallas_call x0 -> x30, Pallas kernels: none -> 90.3 us  [the longest x3 43.2 us: terms(): pl.pallas_call(terms_kernel, grid_spec=grid_spec, out_shape=[jax.ShapeDty...]
    all_gather x1 -> x0, blocking collectives: 70.1 us -> none  [per_device(): targets = lax.all_gather(row_index, ('row', 'col'), axis=1, tiled=True)]
    reduce_scatter x2 -> x0, waiting for transfers between devices: 57.5 us -> none  [the longest x1 57.5 us: per_device(): lax.psum_scatter(stacked, 'row', scatter_dimension=0, tiled=True)]
    psum x1 -> x0, waiting for transfers between devices: 40.2 us -> none  [per_device(): diag_block = diag_inverse + lax.psum(partial_value, ('row', 'col'))]
  transfers between devices with their start and end apart: 5 -> 67, of which waited for: 4 -> 19; matrix products, arithmetic and copies ran while one was open for 13% -> 1% of each run, Pallas kernels for 0% -> 25%
where the time goes in v2:
time: 293 us
  waiting for transfers between devices  98.2 us (34%)
  starting transfers between devices  92.1 us (31%)
  Pallas kernels  90.3 us (31%)
  local copies, waits for them, and re-layouts  8.42 us (3%)
    ppermute x64, waiting for transfers between devices, swap(): return lax.ppermute(x, axis, [(i, i ^ bit) for i in range(count)])  97.8 us
    ppermute x64, starting transfers between devices, swap(): return lax.ppermute(x, axis, [(i, i ^ bit) for i in range(count)])  82.9 us
    pallas_call x3, Pallas kernels, terms(): pl.pallas_call(terms_kernel, grid_spec=grid_spec, out_shape=[jax.ShapeDty...  43.2 us
    pallas_call x3, Pallas kernels, tables(): pl.pallas_call(functools.partial(tables_kernel, chunk), in_specs=[smem, s...  28.8 us
    ppermute x3, starting transfers between devices, to_owner(): return lax.ppermute(x, ('row', 'col'), pairs)  9.19 us
    unnamed x22, local copies, waits for them, and re-layouts  7.23 us
    pallas_call x1, Pallas kernels, lower_block(): pl.pallas_call(block_kernel, in_specs=[anywhere], out_specs=[pl.BlockSpec...  6.15 us
    pallas_call x1, Pallas kernels, invert(): pl.pallas_call(functools.partial(invert_kernel, chunk, sibs), in_specs=[v...  6.13 us
  transfers between devices with their start and end apart: 67, of which 19 were waited for; matrix products, arithmetic and copies ran while one was open for 1% of the time, Pallas kernels for 25%

profile of v2, /device:TPU:4, one launch (start us, length us, event | category | flops | bytes accessed | tf_op | source)
XLA Modules:
  0.0 293.1 jit_solution(17384203403402797920)
XLA Ops:
  4.1 2.6 collective-permute-start.1
  6.9 6.1 %shard_map.59 = (bf16[2048,4096]{1,0:T(8,128)(2,1)S(1)}, f32[2048,1]{1,0:T(8,128)S(1)}, f32[8,128]{1,0:T(8,128)S(1)}) custom-call(bf16[2048,4096]{1,0:T(8,128)(2,1)} %ancestor.1), custom_call_target="tpu_custom_call" | custom-call | flops 8388608 | bytes 33554432 | tf_op jit(solution)/shard_map/pallas_call | solution.py:272
  13.1 5.8 %copy-done.1 = bf16[2048,4096]{1,0:T(8,128)(2,1)} copy-done((bf16[2048,4096]{1,0:T(8,128)(2,1)}, bf16[2048,4096]{1,0:T(8,128)(2,1)S(1)}, u32[]{:S(2)}) %copy-start.1) | copy-done | bytes 16777240
  22.0 3.4 %collective-permute-start.6 = (bf16[256,256]{1,0:T(8,128)(2,1)S(1)}, bf16[256,256]{1,0:T(8,128)(2,1)S(1)}, u32[]{:S(2)}, u32[]{:S(2)}) collective-permute-start(bf16[256,256]{1,0:T(8,128)(2,1)S(1)} %get-tuple-element.88.refs_4_), channel_id=1, source_target_pairs={{0,2},{1,3},{2,0},{3,1},{4,6},{5,7},{6,4},{7,5},{8,10},{9,11},{10,... | collective-permute-start | bytes 393224 | tf_op jit(solution)/shard_map/ppermute | solution.py:17
  27.3 7.0 %collective-permute-done.6.refs_6_ = bf16[256,256]{1,0:T(8,128)(2,1)S(1)} collective-permute-done((bf16[256,256]{1,0:T(8,128)(2,1)S(1)}, bf16[256,256]{1,0:T(8,128)(2,1)S(1)}, u32[]{:S(2)}, u32[]{:S(2)}) %collective-permute-start.6) | collective-permute-done | bytes 131104 | tf_op jit(solution)/shard_map/ppermute | solution.py:17
  42.3 3.9 %collective-permute-done.13.refs_10_ = bf16[256,256]{1,0:T(8,128)(2,1)S(1)} collective-permute-done((bf16[256,256]{1,0:T(8,128)(2,1)S(1)}, bf16[256,256]{1,0:T(8,128)(2,1)S(1)}, u32[]{:S(2)}, u32[]{:S(2)}) %collective-permute-start.13) | collective-permute-done | bytes 131104 | tf_op jit(solution)/shard_map/ppermute | solution.py:17
  46.1 4.7 %collective-permute-start.14 = (bf16[256,256]{1,0:T(8,128)(2,1)S(1)}, bf16[256,256]{1,0:T(8,128)(2,1)S(1)}, u32[]{:S(2)}, u32[]{:S(2)}) collective-permute-start(bf16[256,256]{1,0:T(8,128)(2,1)S(1)} %get-tuple-element.93.refs_8_), channel_id=1, source_target_pairs={{0,3},{1,2},{2,1},{3,0},{4,7},{5,6},{6,5},{7,4},{8,11},{9,10},{10,... | collective-permute-start | bytes 393224 | tf_op jit(solution)/shard_map/ppermute | solution.py:17
  50.8 2.9 %collective-permute-done.14.refs_11_ = bf16[256,256]{1,0:T(8,128)(2,1)S(1)} collective-permute-done((bf16[256,256]{1,0:T(8,128)(2,1)S(1)}, bf16[256,256]{1,0:T(8,128)(2,1)S(1)}, u32[]{:S(2)}, u32[]{:S(2)}) %collective-permute-start.14) | collective-permute-done | bytes 131104 | tf_op jit(solution)/shard_map/ppermute | solution.py:17
  60.0 6.1 %shard_map.63 = s32[3,128,128]{2,1,0:T(8,128)S(1)} custom-call(bf16[8,272,256]{2,1,0:T(8,128)(2,1)S(1)} %bitcast.51, bf16[8,272,256]{2,1,0:T(8,128)(2,1)} %bitcast.6.p1, bf16[8,272,256]{2,1,0:T(8,128)(2,1)} %bitcast.7.p2, bf16[8,272,256]{2,1,0:T(8,128)(2,1)} %bitcast.8.p3), custom_call_target="tpu_custom_call" | custom-call | flops 4000000000 | bytes 196608 | tf_op jit(solution)/shard_map/pallas_call | solution.py:126
  66.8 10.1 %shard_map.64 = (bf16[256,2048]{1,0:T(8,128)(2,1)S(1)}, bf16[4096,256]{1,0:T(8,128)(2,1)S(1)}, f32[8,128]{1,0:T(8,128)S(1)}) custom-call(s32[16,128]{1,0:T(8,128)S(1)} %get-tuple-element.176.row_inv, s32[32,128]{1,0:T(8,128)S(1)} %get-tuple-element.173.col_inv, bf16[8,272,256]{2,1,0:T(8,128)(2,1)S(1)} %bitcast.52, bf16[8,272,256]{2,1,0:T(8,128)(2,1)} %bitcast.6.p1, ...), custom_call_target="tpu_custom_call" | custom-call | flops 10000000000 | bytes 7340032 | tf_op jit(solution)/shard_map/pallas_call | solution.py:202
  77.0 14.2 %shard_map.65 = (bf16[4,256,512]{2,1,0:T(8,128)(2,1)S(1)}, bf16[4,256,512]{2,1,0:T(8,128)(2,1)S(1)}, bf16[2,512,256]{2,1,0:T(8,128)(2,1)S(1)}, bf16[2,512,256]{2...) custom-call(s32[8]{0:T(128)S(1)} %stack.56.plan, bf16[2048,4096]{1,0:T(8,128)(2,1)} %copy-done.1, ...), custom_call_target="tpu_custom_call" | custom-call | flops 10737418240 | bytes 16777216 | tf_op jit(solution)/shard_map/pallas_call | solution.py:384
  92.6 2.4 collective-permute-start.17
  102.4 9.0 %shard_map.71 = (bf16[256,2048]{1,0:T(8,128)(2,1)S(1)}, bf16[4096,256]{1,0:T(8,128)(2,1)S(1)}, f32[8,128]{1,0:T(8,128)S(1)}) custom-call(s32[16,128]{1,0:T(8,128)S(1)} %get-tuple-element.175.row_inv, s32[32,128]{1,0:T(8,128)S(1)} %get-tuple-element.172.col_inv, bf16[8,256,256]{2,1,0:T(8,128)(2,1)S(1)} %bitcast.57, bf16[8,256,256]{2,1,0:T(8,128)(2,1)S(1)} %bitcast.58, ...), custom_call_target="tpu_custom_call" | custom-call | flops 10000000000 | bytes 7340032 | tf_op jit(solution)/shard_map/pallas_call | solution.py:202
  114.2 12.2 %collective-permute-done.22.refs_3_ = f32[1,128,256]{2,1,0:T(8,128)S(1)} collective-permute-done((f32[1,128,256]{2,1,0:T(8,128)S(1)}, f32[1,128,256]{2,1,0:T(8,128)S(1)}, u32[]{:S(2)}, u32[]{:S(2)}) %collective-permute-start.22) | collective-permute-done | bytes 131104 | tf_op jit(solution)/shard_map/ppermute | solution.py:17
  128.6 14.0 %shard_map.72 = (bf16[4,256,512]{2,1,0:T(8,128)(2,1)S(1)}, bf16[4,256,512]{2,1,0:T(8,128)(2,1)S(1)}, bf16[2,512,256]{2,1,0:T(8,128)(2,1)S(1)}, bf16[2,512,256]{2...) custom-call(s32[8]{0:T(128)S(1)} %stack.56.plan, bf16[2048,4096]{1,0:T(8,128)(2,1)} %copy-done.1, ...), custom_call_target="tpu_custom_call" | custom-call | flops 10737418240 | bytes 16777216 | tf_op jit(solution)/shard_map/pallas_call | solution.py:384
  143.5 9.6 %shard_map.78 = (bf16[256,2048]{1,0:T(8,128)(2,1)S(1)}, bf16[4096,256]{1,0:T(8,128)(2,1)S(1)}, f32[8,128]{1,0:T(8,128)}) custom-call(s32[16,128]{1,0:T(8,128)S(1)} %get-tuple-element.174.row_inv, s32[32,128]{1,0:T(8,128)S(1)} %get-tuple-element.171.col_inv, bf16[8,256,256]{2,1,0:T(8,128)(2,1)S(1)} %bitcast.53, bf16[8,256,256]{2,1,0:T(8,128)(2,1)S(1)} %bitcast.54, ...), custom_call_target="tpu_custom_call" | custom-call | flops 10000000000 | bytes 7340032 | tf_op jit(solution)/shard_map/pallas_call | solution.py:202
  153.5 15.0 %shard_map.79 = (bf16[4,256,512]{2,1,0:T(8,128)(2,1)S(1)}, bf16[4,256,512]{2,1,0:T(8,128)(2,1)S(1)}, bf16[2,512,256]{2,1,0:T(8,128)(2,1)}, bf16[2,512,256]{2,1,0...) custom-call(s32[8]{0:T(128)S(1)} %stack.56.plan, bf16[2048,4096]{1,0:T(8,128)(2,1)} %copy-done.1, ...), custom_call_target="tpu_custom_call" | custom-call | flops 10737418240 | bytes 16777216 | tf_op jit(solution)/shard_map/pallas_call | solution.py:384
  170.5 15.1 %collective-permute-done.37.refs_3_ = f32[1,128,256]{2,1,0:T(8,128)S(1)} collective-permute-done((f32[1,128,256]{2,1,0:T(8,128)S(1)}, f32[1,128,256]{2,1,0:T(8,128)S(1)}, u32[]{:S(2)}, u32[]{:S(2)}) %collective-permute-start.37) | collective-permute-done | bytes 131104 | tf_op jit(solution)/shard_map/ppermute | solution.py:17
  190.2 6.3 %collective-permute-done.39.refs_3_ = f32[1,128,256]{2,1,0:T(8,128)S(1)} collective-permute-done((f32[1,128,256]{2,1,0:T(8,128)S(1)}, f32[1,128,256]{2,1,0:T(8,128)S(1)}, u32[]{:S(2)}, u32[]{:S(2)}) %collective-permute-start.39) | collective-permute-done | bytes 131104 | tf_op jit(solution)/shard_map/ppermute | solution.py:17
  196.5 2.4 collective-permute-start.60
  201.0 4.6 %collective-permute-done.60.refs_1_ = f32[1,128,256]{2,1,0:T(8,128)S(1)} collective-permute-done((f32[1,128,256]{2,1,0:T(8,128)S(1)}, f32[1,128,256]{2,1,0:T(8,128)S(1)}, u32[]{:S(2)}, u32[]{:S(2)}) %collective-permute-start.60) | collective-permute-done | bytes 131104 | tf_op jit(solution)/shard_map/ppermute | solution.py:17
  210.9 4.0 %collective-permute-done.53.refs_7_ = f32[1,128,256]{2,1,0:T(8,128)S(1)} collective-permute-done((f32[1,128,256]{2,1,0:T(8,128)S(1)}, f32[1,128,256]{2,1,0:T(8,128)S(1)}, u32[]{:S(2)}, u32[]{:S(2)}) %collective-permute-start.53) | collective-permute-done | bytes 131104 | tf_op jit(solution)/shard_map/ppermute | solution.py:17
  220.3 4.7 %collective-permute-done.61.refs_1_ = f32[1,128,256]{2,1,0:T(8,128)S(1)} collective-permute-done((f32[1,128,256]{2,1,0:T(8,128)S(1)}, f32[1,128,256]{2,1,0:T(8,128)S(1)}, u32[]{:S(2)}, u32[]{:S(2)}) %collective-permute-start.61) | collective-permute-done | bytes 131104 | tf_op jit(solution)/shard_map/ppermute | solution.py:17
  224.9 4.7 %collective-permute-start.56 = (f32[1,128,256]{2,1,0:T(8,128)S(1)}, f32[1,128,256]{2,1,0:T(8,128)S(1)}, u32[]{:S(2)}, u32[]{:S(2)}) collective-permute-start(f32[1,128,256]{2,1,0:T(8,128)S(1)} %get-tuple-element.164.refs_4_), channel_id=1, source_target_pairs={{0,1},{1,0},{2,3},{3,2},{4,5},{5,4},{6,7},{7,6},{8,9},{9,8},{10,11... | collective-permute-start | bytes 393224 | tf_op jit(solution)/shard_map/ppermute | solution.py:17
  231.1 3.4 %collective-permute-start.58 = (f32[1,128,256]{2,1,0:T(8,128)S(1)}, f32[1,128,256]{2,1,0:T(8,128)}, u32[]{:S(2)}, u32[]{:S(2)}) collective-permute-start(f32[1,128,256]{2,1,0:T(8,128)S(1)} %get-tuple-element.164.refs_4_), channel_id=1, source_target_pairs={{0,3},{1,2},{2,1},{3,0},{4,7},{5,6},{6,5},{7,4},{8,11},{9,10},{10,... | collective-permute-start | bytes 393224 | tf_op jit(solution)/shard_map/ppermute | solution.py:17
  236.1 3.2 %collective-permute-done.57.refs_6_ = f32[1,128,256]{2,1,0:T(8,128)} collective-permute-done((f32[1,128,256]{2,1,0:T(8,128)S(1)}, f32[1,128,256]{2,1,0:T(8,128)}, u32[]{:S(2)}, u32[]{:S(2)}) %collective-permute-start.57) | collective-permute-done | bytes 131104 | tf_op jit(solution)/shard_map/ppermute | solution.py:17
  239.3 10.9 %collective-permute-start.33 = (bf16[1,512,256]{2,1,0:T(8,128)(2,1)S(1)}, bf16[1,512,256]{2,1,0:T(8,128)(2,1)S(1)}, u32[]{:S(2)}, u32[]{:S(2)}) collective-permute-start(bf16[1,512,256]{2,1,0:T(8,128)(2,1)S(1)} %get-tuple-element.127), channel_id=1, source_target_pairs={{0,2},{1,3},{2,0},{3,1},{4,6},{5,7},{6,4},{7,5},{8,10},{9,11},{10,... | collective-permute-start | bytes 786440 | tf_op jit(solution)/shard_map/ppermute | solution.py:17
  252.3 2.4 collective-permute-start.25
  254.9 3.3 %collective-permute-start.46 = (bf16[1,512,256]{2,1,0:T(8,128)(2,1)S(1)}, bf16[1,512,256]{2,1,0:T(8,128)(2,1)S(1)}, u32[]{:S(2)}, u32[]{:S(2)}) collective-permute-start(bf16[1,512,256]{2,1,0:T(8,128)(2,1)S(1)} %get-tuple-element.150), channel_id=1, source_target_pairs={{0,2},{1,3},{2,0},{3,1},{4,6},{5,7},{6,4},{7,5},{8,10},{9,11},{10,... | collective-permute-start | bytes 786440 | tf_op jit(solution)/shard_map/ppermute | solution.py:17
  260.2 4.9 %collective-permute-start.59 = (bf16[256,512]{1,0:T(8,128)(2,1)S(1)}, bf16[256,512]{1,0:T(8,128)(2,1)S(1)}, u32[]{:S(2)}, u32[]{:S(2)}) collective-permute-start(bf16[256,512]{1,0:T(8,128)(2,1)S(1)} %bitcast.63), channel_id=1, source_target_pairs={{0,0},{1,10},{2,17},{3,27},{4,4},{5,14},{6,21},{7,31},{8,1},{9,11}... | collective-permute-start | bytes 786440 | tf_op jit(solution)/shard_map/ppermute | solution.py:550
  266.1 20.8 %collective-permute-done.33.refs_4_ = bf16[1,512,256]{2,1,0:T(8,128)(2,1)S(1)} collective-permute-done((bf16[1,512,256]{2,1,0:T(8,128)(2,1)S(1)}, bf16[1,512,256]{2,1,0:T(8,128)(2,1)S(1)}, u32[]{:S(2)}, u32[]{:S(2)}) %collective-permute-start.33) | collective-permute-done | bytes 262176 | tf_op jit(solution)/shard_map/ppermute | solution.py:17
  286.8 4.3 %collective-permute-done.46.refs_7_ = bf16[1,512,256]{2,1,0:T(8,128)(2,1)S(1)} collective-permute-done((bf16[1,512,256]{2,1,0:T(8,128)(2,1)S(1)}, bf16[1,512,256]{2,1,0:T(8,128)(2,1)S(1)}, u32[]{:S(2)}, u32[]{:S(2)}) %collective-permute-start.46) | collective-permute-done | bytes 262176 | tf_op jit(solution)/shard_map/ppermute | solution.py:17
  (167 shorter events, 67.7 us)
Async XLA Ops:
  2.5 16.4 %collective-permute-start = (bf16[272,256]{1,0:T(8,128)(2,1)S(1)}, bf16[272,256]{1,0:T(8,128)(2,1)S(1)}, u32[]{:S(2)}, u32[]{:S(2)}) collective-permute-start(bf16[272,256]{1,0:T(8,128)(2,1)S(1)} %fusion.1.refs_0_), channel_id=1, source_target_pairs={{0,1},{1,0},{2,3},{3,2},{4,5},{5,4},{6,7},{7,6},{8,9},{9,8},{10,11... | collective-permute-start | bytes 417800 | tf_op jit(solution)/shard_map/ppermute | solution.py:17
  4.1 14.8 %collective-permute-start.1 = (bf16[272,256]{1,0:T(8,128)(2,1)S(1)}, bf16[272,256]{1,0:T(8,128)(2,1)S(1)}, u32[]{:S(2)}, u32[]{:S(2)}) collective-permute-start(bf16[272,256]{1,0:T(8,128)(2,1)S(1)} %fusion.1.refs_0_), channel_id=1, source_target_pairs={{0,2},{1,3},{2,0},{3,1},{4,6},{5,7},{6,4},{7,5},{8,10},{9,11},{10,... | collective-permute-start | bytes 417800 | tf_op jit(solution)/shard_map/ppermute | solution.py:17
  19.0 15.3 %collective-permute-start.3 = (bf16[544,256]{1,0:T(8,128)(2,1)S(1)}, bf16[544,256]{1,0:T(8,128)(2,1)S(1)}, u32[]{:S(2)}, u32[]{:S(2)}) collective-permute-start(bf16[544,256]{1,0:T(8,128)(2,1)S(1)} %get-tuple-element.86.refs_0_), channel_id=1, source_target_pairs={{0,8},{4,12},{8,0},{12,4},{16,24},{20,28},{24,16},{28,20},{1,9},{5... | collective-permute-start | bytes 835592 | tf_op jit(solution)/shard_map/ppermute | solution.py:17
  34.4 19.3 %collective-permute-start.8 = (bf16[1088,256]{1,0:T(8,128)(2,1)S(1)}, bf16[1088,256]{1,0:T(8,128)(2,1)S(1)}, u32[]{:S(2)}, u32[]{:S(2)}) collective-permute-start(bf16[1088,256]{1,0:T(8,128)(2,1)S(1)} %get-tuple-element.89.refs_0_), channel_id=1, source_target_pairs={{0,16},{4,20},{8,24},{12,28},{16,0},{20,4},{24,8},{28,12},{1,17},{... | collective-permute-start | bytes 1671176 | tf_op jit(solution)/shard_map/ppermute | solution.py:17
  36.0 17.8 %collective-permute-start.9 = (bf16[1088,256]{1,0:T(8,128)(2,1)S(1)}, bf16[1088,256]{1,0:T(8,128)(2,1)S(1)}, u32[]{:S(2)}, u32[]{:S(2)}) collective-permute-start(bf16[1088,256]{1,0:T(8,128)(2,1)S(1)} %get-tuple-element.90.refs_2_), channel_id=1, source_target_pairs={{0,8},{4,12},{8,0},{12,4},{16,24},{20,28},{24,16},{28,20},{1,9},{5... | collective-permute-start | bytes 1671176 | tf_op jit(solution)/shard_map/ppermute | solution.py:17
  55.6 35.7 %collective-permute-start.26 = (bf16[1024,256]{1,0:T(8,128)(2,1)S(1)}, bf16[1024,256]{1,0:T(8,128)(2,1)S(1)}, u32[]{:S(2)}, u32[]{:S(2)}) collective-permute-start(bf16[1024,256]{1,0:T(8,128)(2,1)S(1)} %get-tuple-element.115.refs_0_), channel_id=1, source_target_pairs={{0,16},{4,20},{8,24},{12,28},{16,0},{20,4},{24,8},{28,12},{1,17},{... | collective-permute-start | bytes 1572872 | tf_op jit(solution)/shard_map/ppermute | solution.py:17
  56.2 35.2 %collective-permute-start.27 = (bf16[1024,256]{1,0:T(8,128)(2,1)S(1)}, bf16[1024,256]{1,0:T(8,128)(2,1)S(1)}, u32[]{:S(2)}, u32[]{:S(2)}) collective-permute-start(bf16[1024,256]{1,0:T(8,128)(2,1)S(1)} %get-tuple-element.116.refs_2_), channel_id=1, source_target_pairs={{0,8},{4,12},{8,0},{12,4},{16,24},{20,28},{24,16},{28,20},{1,9},{5... | collective-permute-start | bytes 1572872 | tf_op jit(solution)/shard_map/ppermute | solution.py:17
  57.6 33.6 %collective-permute-start.28 = (bf16[512,256]{1,0:T(8,128)(2,1)S(1)}, bf16[512,256]{1,0:T(8,128)(2,1)S(1)}, u32[]{:S(2)}, u32[]{:S(2)}) collective-permute-start(bf16[512,256]{1,0:T(8,128)(2,1)S(1)} %get-tuple-element.117.refs_4_), channel_id=1, source_target_pairs={{0,8},{4,12},{8,0},{12,4},{16,24},{20,28},{24,16},{28,20},{1,9},{5... | collective-permute-start | bytes 786440 | tf_op jit(solution)/shard_map/ppermute | solution.py:17
  59.5 31.8 %collective-permute-start.29 = (bf16[512,256]{1,0:T(8,128)(2,1)S(1)}, bf16[512,256]{1,0:T(8,128)(2,1)S(1)}, u32[]{:S(2)}, u32[]{:S(2)}) collective-permute-start(bf16[512,256]{1,0:T(8,128)(2,1)S(1)} %get-tuple-element.118.refs_6_), channel_id=1, source_target_pairs={{0,16},{4,20},{8,24},{12,28},{16,0},{20,4},{24,8},{28,12},{1,17},{... | collective-permute-start | bytes 786440 | tf_op jit(solution)/shard_map/ppermute | solution.py:17
  92.6 50.0 %collective-permute-start.17 = (bf16[2,512,256]{2,1,0:T(8,128)(2,1)S(1)}, bf16[2,512,256]{2,1,0:T(8,128)(2,1)S(1)}, u32[]{:S(2)}, u32[]{:S(2)}) collective-permute-start(bf16[2,512,256]{2,1,0:T(8,128)(2,1)S(1)} %get-tuple-element.101), channel_id=1, source_target_pairs={{0,1},{1,0},{2,3},{3,2},{4,5},{5,4},{6,7},{7,6},{8,9},{9,8},{10,11... | collective-permute-start | bytes 1572872 | tf_op jit(solution)/shard_map/ppermute | solution.py:17
  97.1 14.4 %collective-permute-start.41 = (bf16[1024,256]{1,0:T(8,128)(2,1)S(1)}, bf16[1024,256]{1,0:T(8,128)(2,1)S(1)}, u32[]{:S(2)}, u32[]{:S(2)}) collective-permute-start(bf16[1024,256]{1,0:T(8,128)(2,1)S(1)} %get-tuple-element.139.refs_0_), channel_id=1, source_target_pairs={{0,16},{4,20},{8,24},{12,28},{16,0},{20,4},{24,8},{28,12},{1,17},{... | collective-permute-start | bytes 1572872 | tf_op jit(solution)/shard_map/ppermute | solution.py:17
  98.6 14.8 %collective-permute-start.42 = (bf16[1024,256]{1,0:T(8,128)(2,1)S(1)}, bf16[1024,256]{1,0:T(8,128)(2,1)S(1)}, u32[]{:S(2)}, u32[]{:S(2)}) collective-permute-start(bf16[1024,256]{1,0:T(8,128)(2,1)S(1)} %get-tuple-element.140.refs_2_), channel_id=1, source_target_pairs={{0,8},{4,12},{8,0},{12,4},{16,24},{20,28},{24,16},{28,20},{1,9},{5... | collective-permute-start | bytes 1572872 | tf_op jit(solution)/shard_map/ppermute | solution.py:17
  100.3 26.0 %collective-permute-start.21 = (bf16[2,256,512]{2,1,0:T(8,128)(2,1)S(1)}, bf16[2,256,512]{2,1,0:T(8,128)(2,1)S(1)}, u32[]{:S(2)}, u32[]{:S(2)}) collective-permute-start(bf16[2,256,512]{2,1,0:T(8,128)(2,1)S(1)} %get-tuple-element.109), channel_id=1, source_target_pairs={{0,8},{4,12},{8,0},{12,4},{16,24},{20,28},{24,16},{28,20},{1,9},{5... | collective-permute-start | bytes 1572872 | tf_op jit(solution)/shard_map/ppermute | solution.py:17
  101.0 25.4 %collective-permute-start.22 = (f32[1,128,256]{2,1,0:T(8,128)S(1)}, f32[1,128,256]{2,1,0:T(8,128)S(1)}, u32[]{:S(2)}, u32[]{:S(2)}) collective-permute-start(f32[1,128,256]{2,1,0:T(8,128)S(1)} %get-tuple-element.110.refs_2_.refs_0_), channel_id=1, source_target_pairs={{0,8},{4,12},{8,0},{12,4},{16,24},{20,28},{24,16},{28,20},{1,9},{5... | collective-permute-start | bytes 393224 | tf_op jit(solution)/shard_map/ppermute | solution.py:17
  113.6 29.9 %collective-permute-start.43 = (bf16[2048,256]{1,0:T(8,128)(2,1)S(1)}, bf16[2048,256]{1,0:T(8,128)(2,1)S(1)}, u32[]{:S(2)}, u32[]{:S(2)}) collective-permute-start(bf16[2048,256]{1,0:T(8,128)(2,1)S(1)} %get-tuple-element.142), channel_id=1, source_target_pairs={{0,4},{4,0},{8,12},{12,8},{16,20},{20,16},{24,28},{28,24},{1,5},{5... | collective-permute-start | bytes 3145736 | tf_op jit(solution)/shard_map/ppermute | solution.py:17
  113.7 29.9 %collective-permute-start.44 = (bf16[2048,256]{1,0:T(8,128)(2,1)S(1)}, bf16[2048,256]{1,0:T(8,128)(2,1)S(1)}, u32[]{:S(2)}, u32[]{:S(2)}) collective-permute-start(bf16[2048,256]{1,0:T(8,128)(2,1)S(1)} %get-tuple-element.143), channel_id=1, source_target_pairs={{0,4},{4,0},{8,12},{12,8},{16,20},{20,16},{24,28},{28,24},{1,5},{5... | collective-permute-start | bytes 3145736 | tf_op jit(solution)/shard_map/ppermute | solution.py:17
  126.5 16.9 %collective-permute-start.23 = (bf16[1,256,512]{2,1,0:T(8,128)(2,1)S(1)}, bf16[1,256,512]{2,1,0:T(8,128)(2,1)S(1)}, u32[]{:S(2)}, u32[]{:S(2)}) collective-permute-start(bf16[1,256,512]{2,1,0:T(8,128)(2,1)S(1)} %get-tuple-element.112), channel_id=1, source_target_pairs={{0,16},{4,20},{8,24},{12,28},{16,0},{20,4},{24,8},{28,12},{1,17},{... | collective-permute-start | bytes 786440 | tf_op jit(solution)/shard_map/ppermute | solution.py:17
  127.1 15.8 %collective-permute-start.24 = (f32[1,128,256]{2,1,0:T(8,128)S(1)}, f32[1,128,256]{2,1,0:T(8,128)S(1)}, u32[]{:S(2)}, u32[]{:S(2)}) collective-permute-start(f32[1,128,256]{2,1,0:T(8,128)S(1)} %get-tuple-element.113.refs_2_.refs_0_), channel_id=1, source_target_pairs={{0,16},{4,20},{8,24},{12,28},{16,0},{20,4},{24,8},{28,12},{1,17},{... | collective-permute-start | bytes 393224 | tf_op jit(solution)/shard_map/ppermute | solution.py:17
  168.5 30.6 %collective-permute-start.47 = (bf16[4,256,512]{2,1,0:T(8,128)(2,1)S(1)}, bf16[4,256,512]{2,1,0:T(8,128)(2,1)S(1)}, u32[]{:S(2)}, u32[]{:S(2)}) collective-permute-start(bf16[4,256,512]{2,1,0:T(8,128)(2,1)S(1)} %get-tuple-element.152), channel_id=1, source_target_pairs={{0,4},{4,0},{8,12},{12,8},{16,20},{20,16},{24,28},{28,24},{1,5},{5... | collective-permute-start | bytes 3145736 | tf_op jit(solution)/shard_map/ppermute | solution.py:17
  168.5 17.1 %collective-permute-start.36 = (bf16[2,256,512]{2,1,0:T(8,128)(2,1)S(1)}, bf16[2,256,512]{2,1,0:T(8,128)(2,1)S(1)}, u32[]{:S(2)}, u32[]{:S(2)}) collective-permute-start(bf16[2,256,512]{2,1,0:T(8,128)(2,1)S(1)} %get-tuple-element.133), channel_id=1, source_target_pairs={{0,8},{4,12},{8,0},{12,4},{16,24},{20,28},{24,16},{28,20},{1,9},{5... | collective-permute-start | bytes 1572872 | tf_op jit(solution)/shard_map/ppermute | solution.py:17
  170.0 15.7 %collective-permute-start.37 = (f32[1,128,256]{2,1,0:T(8,128)S(1)}, f32[1,128,256]{2,1,0:T(8,128)S(1)}, u32[]{:S(2)}, u32[]{:S(2)}) collective-permute-start(f32[1,128,256]{2,1,0:T(8,128)S(1)} %get-tuple-element.134.refs_2_.refs_1_), channel_id=1, source_target_pairs={{0,8},{4,12},{8,0},{12,4},{16,24},{20,28},{24,16},{28,20},{1,9},{5... | collective-permute-start | bytes 393224 | tf_op jit(solution)/shard_map/ppermute | solution.py:17
  187.8 31.8 %collective-permute-start.32 = (bf16[2,512,256]{2,1,0:T(8,128)(2,1)S(1)}, bf16[2,512,256]{2,1,0:T(8,128)(2,1)S(1)}, u32[]{:S(2)}, u32[]{:S(2)}) collective-permute-start(bf16[2,512,256]{2,1,0:T(8,128)(2,1)S(1)} %get-tuple-element.125), channel_id=1, source_target_pairs={{0,1},{1,0},{2,3},{3,2},{4,5},{5,4},{6,7},{7,6},{8,9},{9,8},{10,11... | collective-permute-start | bytes 1572872 | tf_op jit(solution)/shard_map/ppermute | solution.py:17
  209.3 43.0 %collective-permute-start.45 = (bf16[2,512,256]{2,1,0:T(8,128)(2,1)}, bf16[2,512,256]{2,1,0:T(8,128)(2,1)S(1)}, u32[]{:S(2)}, u32[]{:S(2)}) collective-permute-start(bf16[2,512,256]{2,1,0:T(8,128)(2,1)} %get-tuple-element.148), channel_id=1, source_target_pairs={{0,1},{1,0},{2,3},{3,2},{4,5},{5,4},{6,7},{7,6},{8,9},{9,8},{10,11... | collective-permute-start | bytes 1572872 | tf_op jit(solution)/shard_map/ppermute | solution.py:17
  219.6 15.0 %collective-permute-start.55 = (bf16[1,128,512]{2,1,0:T(8,128)(2,1)S(1)}, bf16[1,128,512]{2,1,0:T(8,128)(2,1)S(1)}, u32[]{:S(2)}, u32[]{:S(2)}) collective-permute-start(bf16[1,128,512]{2,1,0:T(8,128)(2,1)S(1)} %get-tuple-element.163), channel_id=1, source_target_pairs={{0,8},{4,12},{8,0},{12,4},{16,24},{20,28},{24,16},{28,20},{1,9},{5... | collective-permute-start | bytes 393224 | tf_op jit(solution)/shard_map/ppermute | solution.py:17
  234.6 16.6 %collective-permute-start.62 = (f32[1,128,256]{2,1,0:T(8,128)S(1)}, f32[1,128,256]{2,1,0:T(8,128)}, u32[]{:S(2)}, u32[]{:S(2)}) collective-permute-start(f32[1,128,256]{2,1,0:T(8,128)S(1)} %shard_map.86), channel_id=1, source_target_pairs={{0,4},{4,0},{8,12},{12,8},{16,20},{20,16},{24,28},{28,24},{1,5},{5... | collective-permute-start | bytes 393224 | tf_op jit(solution)/shard_map/ppermute | solution.py:17
  234.7 20.2 %collective-permute-start.65 = (f32[1,128,256]{2,1,0:T(8,128)S(1)}, f32[1,128,256]{2,1,0:T(8,128)S(1)}, u32[]{:S(2)}, u32[]{:S(2)}) collective-permute-start(f32[1,128,256]{2,1,0:T(8,128)S(1)} %shard_map.88), channel_id=1, source_target_pairs={{0,4},{4,0},{8,12},{12,8},{16,20},{20,16},{24,28},{28,24},{1,5},{5... | collective-permute-start | bytes 393224 | tf_op jit(solution)/shard_map/ppermute | solution.py:17
  239.3 20.9 %collective-permute-start.18 = (bf16[1,512,256]{2,1,0:T(8,128)(2,1)}, bf16[1,512,256]{2,1,0:T(8,128)(2,1)S(1)}, u32[]{:S(2)}, u32[]{:S(2)}) collective-permute-start(bf16[1,512,256]{2,1,0:T(8,128)(2,1)} %copy-done.4), channel_id=1, source_target_pairs={{0,2},{1,3},{2,0},{3,1},{4,6},{5,7},{6,4},{7,5},{8,10},{9,11},{10,... | collective-permute-start | bytes 786440 | tf_op jit(solution)/shard_map/ppermute | solution.py:17
  239.3 47.5 %collective-permute-start.33 = (bf16[1,512,256]{2,1,0:T(8,128)(2,1)S(1)}, bf16[1,512,256]{2,1,0:T(8,128)(2,1)S(1)}, u32[]{:S(2)}, u32[]{:S(2)}) collective-permute-start(bf16[1,512,256]{2,1,0:T(8,128)(2,1)S(1)} %get-tuple-element.127), channel_id=1, source_target_pairs={{0,2},{1,3},{2,0},{3,1},{4,6},{5,7},{6,4},{7,5},{8,10},{9,11},{10,... | collective-permute-start | bytes 786440 | tf_op jit(solution)/shard_map/ppermute | solution.py:17
  252.3 34.5 %collective-permute-start.25 = (bf16[256,512]{1,0:T(8,128)(2,1)S(1)}, bf16[256,512]{1,0:T(8,128)(2,1)S(1)}, u32[]{:S(2)}, u32[]{:S(2)}) collective-permute-start(bf16[256,512]{1,0:T(8,128)(2,1)S(1)} %bitcast.61), channel_id=1, source_target_pairs={{0,0},{1,10},{2,17},{3,27},{4,4},{5,14},{6,21},{7,31},{8,1},{9,11}... | collective-permute-start | bytes 786440 | tf_op jit(solution)/shard_map/ppermute | solution.py:550
  254.9 36.3 %collective-permute-start.46 = (bf16[1,512,256]{2,1,0:T(8,128)(2,1)S(1)}, bf16[1,512,256]{2,1,0:T(8,128)(2,1)S(1)}, u32[]{:S(2)}, u32[]{:S(2)}) collective-permute-start(bf16[1,512,256]{2,1,0:T(8,128)(2,1)S(1)} %get-tuple-element.150), channel_id=1, source_target_pairs={{0,2},{1,3},{2,0},{3,1},{4,6},{5,7},{6,4},{7,5},{8,10},{9,11},{10,... | collective-permute-start | bytes 786440 | tf_op jit(solution)/shard_map/ppermute | solution.py:17
  258.2 32.9 %collective-permute-start.40 = (bf16[256,512]{1,0:T(8,128)(2,1)S(1)}, bf16[256,512]{1,0:T(8,128)(2,1)S(1)}, u32[]{:S(2)}, u32[]{:S(2)}) collective-permute-start(bf16[256,512]{1,0:T(8,128)(2,1)S(1)} %bitcast.62), channel_id=1, source_target_pairs={{0,0},{1,10},{2,17},{3,27},{4,4},{5,14},{6,21},{7,31},{8,1},{9,11}... | collective-permute-start | bytes 786440 | tf_op jit(solution)/shard_map/ppermute | solution.py:550
  260.2 31.4 %collective-permute-start.59 = (bf16[256,512]{1,0:T(8,128)(2,1)S(1)}, bf16[256,512]{1,0:T(8,128)(2,1)S(1)}, u32[]{:S(2)}, u32[]{:S(2)}) collective-permute-start(bf16[256,512]{1,0:T(8,128)(2,1)S(1)} %bitcast.63), channel_id=1, source_target_pairs={{0,0},{1,10},{2,17},{3,27},{4,4},{5,14},{6,21},{7,31},{8,1},{9,11}... | collective-permute-start | bytes 786440 | tf_op jit(solution)/shard_map/ppermute | solution.py:550
  (45 other events, 487.7 us)

commit v3 on v2

--- a/solution.py
+++ b/solution.py
@@ -71,6 +71,10 @@
                 ]
             else:
                 continue
+            if step == rounds - 1:
+                places.append((n, 0))
+                groups.append(state[n][0] + state[n][1])
+                continue
             for side in range(2):
                 places.append((n, side))
                 groups.append(state[n][side])
@@ -83,12 +87,11 @@
             state[n][side] = value
         done = tick - rounds + 1
         if done >= 0:
-            first, second = state[done]
-            yield [first, second, swap(first, "row", 1), swap(second, "row", 1)]
-
-
-def invert_kernel(listed, sibs, p0, p1, p2, p3, out_ref):
-    pieces = (p0, p1, p2, p3)
+            yield [state[done][0], swap(state[done][0], "row", 1)]
+
+
+def invert_kernel(listed, sibs, p0, p1, out_ref):
+    pieces = (p0, p1)
     lines = out_ref.shape[1]
     count, _, wide = p0.shape
     line_ids = lax.broadcasted_iota(jnp.int32, (lines, wide), 0).astype(F32)
@@ -125,7 +128,7 @@
     vmem = pl.BlockSpec(memory_space=pltpu.VMEM)
     return pl.pallas_call(
         functools.partial(invert_kernel, chunk, sibs),
-        in_specs=[vmem] * 4,
+        in_specs=[vmem] * 2,
         out_specs=pl.BlockSpec(memory_space=pltpu.VMEM),
         out_shape=jax.ShapeDtypeStruct((sibs, rows // LANES, LANES), jnp.int32),
         compiler_params=pltpu.CompilerParams(vmem_limit_bytes=16 * 2**20),
@@ -135,7 +138,7 @@
     )(*pieces)
 
 
-def tables_kernel(chunk, row_inv, col_inv, p0, p1, p2, p3, *refs):
+def tables_kernel(chunk, row_inv, col_inv, p0, p1, *refs):
     row_out, col_out, mark, source, target = refs[-5:]
     mark[...] = jnp.zeros_like(mark)
     step = 256
@@ -143,7 +146,7 @@
     parts = width // LANES
     count = p0.shape[0]
     source[0 : 8 * parts, :] = jnp.zeros((8 * parts, LANES), F32)
-    for n, piece in enumerate((p0, p1, p2, p3)):
+    for n, piece in enumerate((p0, p1)):
 
         def fill(m, unused, n=n, piece=piece):
             values = piece[m, :chunk, :].astype(F32)
@@ -194,14 +197,14 @@
     width = pieces[0].shape[1]
     pieces = [p.reshape(-1, whole_chunk, width) for p in pieces]
     count = pieces[0].shape[0]
-    listed = 4 * count * chunk
+    listed = 2 * count * chunk
     parts = width // LANES
     rows, cols = row_inv.size, col_inv.size
     vmem = pl.BlockSpec(memory_space=pltpu.VMEM)
     smem = pl.BlockSpec(memory_space=pltpu.SMEM)
     return pl.pallas_call(
         functools.partial(tables_kernel, chunk),
-        in_specs=[smem, smem] + [vmem] * (4 + len(marks)),
+        in_specs=[smem, smem] + [vmem] * (2 + len(marks)),
         out_specs=[vmem] * 3,
         out_shape=[
             jax.ShapeDtypeStruct((width, rows), BF),
@@ -290,30 +293,45 @@
     )(ancestor)
 
 
+def encode(values, lanes):
+    high = values.astype(BF)
+    low = (values - high.astype(F32)).astype(BF)
+    both = jnp.concatenate([high, low], 1)
+    return jnp.concatenate([both[:, n : n + lanes] for n in range(0, both.shape[1], lanes)], 0)
+
+
+def decode(codes, width):
+    rows = codes.shape[0] * codes.shape[1] // (2 * width)
+    both = jnp.concatenate([codes[n : n + rows] for n in range(0, codes.shape[0], rows)], 1)
+    both = both.astype(F32)
+    return both[:, :width] + both[:, width:]
+
+
 def terms_kernel(plan, block, diagonal, row_t, col, *refs):
-    m_send, m_keep, d_send, d_keep, y_send, y_keep, total, rounded = refs[-8:]
+    m_send, m_keep, direct, total, rounded, y = refs[-6:]
     i = pl.program_id(0)
     steps = pl.num_programs(0)
     rows = block.shape[0]
     owned = m_send.shape[2]
     tile = 2 * owned
     width = row_t.shape[0]
-    place, core, swapped, offset = [plan[steps + n] for n in range(4)]
+    coded = m_send.shape[1] - width
+    core, swapped, offset, chip = [plan[steps + n] for n in range(4)]
     at_tile = pl.ds(pl.multiple_of(plan[i] * tile, tile), tile)
     values = col[at_tile, :]
 
-    def mirrored(out):
+    def mirrored(out, slot):
         term = jnp.dot(row_t[...], block[...], preferred_element_type=F32).astype(BF)
-        out[swapped] = term[:, :owned]
-        out[1 - swapped] = term[:, owned:]
+        out[slot + swapped, coded:, :] = term[:, :owned]
+        out[slot + 1 - swapped, coded:, :] = term[:, owned:]
 
     @pl.when(i < steps // 2)
     def sent():
-        mirrored(m_send)
+        mirrored(m_send, 2 * i)
 
     @pl.when(i >= steps // 2)
     def kept():
-        mirrored(m_keep)
+        mirrored(m_keep, 2 * i - steps)
 
     @pl.when(i == 0)
     def first():
@@ -327,70 +345,54 @@
     def last():
         cols = col.shape[0]
         for e in range(rows // owned):
-            start = pl.multiple_of((e ^ place) * owned, owned)
-            at = pl.ds(start, owned)
-            back = pl.multiple_of(jnp.clip(start + offset, 0, cols - owned), owned)
+            at = slice(e * owned, (e + 1) * owned)
+            back = pl.multiple_of(jnp.clip(e * owned + offset, 0, cols - owned), owned)
             own = diagonal[at, :] * col[pl.ds(back, owned), :].astype(F32)
             term = total[at, :]
             rounded[at, :] = (term + 0.5 * own).astype(BF)
-            term = (term + own).astype(BF)
-            if e % 2:
-                d_send[e // 2] = term
-            else:
-                d_keep[e // 2] = term
-        y = jnp.dot(row_t[...], rounded[...], preferred_element_type=F32)
-        y = y + y.T
-        half = width // 2
-
-        @pl.when(core == 0)
-        def first_core():
-            y_keep[0] = y[:half]
-            y_send[0] = y[half:]
-
-        @pl.when(core != 0)
-        def second_core():
-            y_keep[0] = y[half:]
-            y_send[0] = y[:half]
+            direct[e] = (term + own).astype(BF)
+        half = jnp.dot(row_t[...], rounded[...], preferred_element_type=F32)
+        y[...] = half + half.T
+        slots = m_send.shape[0]
+        share = width // (2 * slots)
+        for out, side in ((m_send, 1 - core), (m_keep, core)):
+            for e in range(slots):
+                start = pl.multiple_of((2 * (e ^ chip) + side) * share, share)
+                out[e, :coded, :] = encode(y[pl.ds(start, share), :], owned)
 
 
 def terms(plan, lower, diagonal, row_t, col, owned, marks):
     rows, cols = lower.shape
     width = col.shape[1]
     steps = cols // (2 * owned)
-    half = steps // 2
     count = rows // owned
     everything = [
         pl.BlockSpec(x.shape, lambda i, plan, x=x: (0,) * x.ndim) for x in (diagonal, row_t, col)
     ]
     anywhere = pl.BlockSpec(memory_space=pl.ANY)
-    d_spec = pl.BlockSpec((count // 2, owned, width), lambda i, plan: (0, 0, 0))
-    y_spec = pl.BlockSpec((1, width // 2, width), lambda i, plan: (0, 0, 0))
+    d_spec = pl.BlockSpec((count, owned, width), lambda i, plan: (0, 0, 0))
+    coded = 2 * width * width // cols
+    m_spec = pl.BlockSpec((steps, coded + width, owned), lambda i, plan: (0, 0, 0))
     grid_spec = pltpu.PrefetchScalarGridSpec(
         num_scalar_prefetch=1,
         grid=(steps,),
         in_specs=[pl.BlockSpec((rows, 2 * owned), lambda i, plan: (0, plan[i]))]
         + everything
         + [anywhere] * len(marks),
-        out_specs=[
-            pl.BlockSpec((2, width, owned), lambda i, plan: (jnp.minimum(i, half - 1), 0, 0)),
-            pl.BlockSpec((2, width, owned), lambda i, plan: (jnp.maximum(i - half, 0), 0, 0)),
-            d_spec,
-            d_spec,
-            y_spec,
-            y_spec,
+        out_specs=[m_spec, m_spec, d_spec],
+        scratch_shapes=[
+            pltpu.VMEM((rows, width), F32),
+            pltpu.VMEM((rows, width), BF),
+            pltpu.VMEM((width, width), F32),
         ],
-        scratch_shapes=[pltpu.VMEM((rows, width), F32), pltpu.VMEM((rows, width), BF)],
     )
     return pl.pallas_call(
         terms_kernel,
         grid_spec=grid_spec,
         out_shape=[
-            jax.ShapeDtypeStruct((steps, width, owned), BF),
-            jax.ShapeDtypeStruct((steps, width, owned), BF),
-            jax.ShapeDtypeStruct((count // 2, owned, width), BF),
-            jax.ShapeDtypeStruct((count // 2, owned, width), BF),
-            jax.ShapeDtypeStruct((1, width // 2, width), F32),
-            jax.ShapeDtypeStruct((1, width // 2, width), F32),
+            jax.ShapeDtypeStruct((steps, coded + width, owned), BF),
+            jax.ShapeDtypeStruct((steps, coded + width, owned), BF),
+            jax.ShapeDtypeStruct((count, owned, width), BF),
         ],
         compiler_params=pltpu.CompilerParams(vmem_limit_bytes=34 * 2**20),
         cost_estimate=pl.CostEstimate(
@@ -406,42 +408,52 @@
     return values[0]
 
 
-def sums_kernel(counts, outs, *refs):
-    ins, outs_refs = refs[: len(refs) - len(outs)], refs[len(refs) - len(outs) :]
+def sums_kernel(width, counts, outs, marks, *refs):
+    ins, outs_refs = refs[: len(refs) - len(outs) - marks], refs[len(refs) - len(outs) :]
     groups, at = [], 0
     for count in counts:
         groups.append(ins[at : at + count])
         at += count
     for ref, pieces in zip(outs_refs, outs):
-        for place, group, slot, low, high in pieces:
-            ref[place] = tree_sum([x[slot, low:high] for x in groups[group]]).astype(ref.dtype)
-
-
-def sums(groups, outs):
+        for place, group, slot, low, high, coded in pieces:
+            addends = [x[slot, low:high] for x in groups[group]]
+            if ref.dtype == F32 and coded:
+                ref[place] = tree_sum([decode(x, ref.shape[2]) for x in addends])
+                continue
+            if coded:
+                total = tree_sum([decode(x[:coded], width) for x in addends])
+                ref[place, :coded] = encode(total, ref.shape[2])
+            ref[place, coded:] = tree_sum([x[coded:] for x in addends]).astype(ref.dtype)
+
+
+def sums(groups, outs, width, marks=()):
     flat = [x for group in groups for x in group]
     shapes = []
     for pieces in outs:
-        _, group, _, low, high = pieces[0]
+        _, group, _, low, high, coded = pieces[0]
         like = groups[group][0]
-        shapes.append(
-            jax.ShapeDtypeStruct((len(pieces), high - low, like.shape[2]), like.dtype)
-        )
+        rows, lanes, dtype = high - low, like.shape[2], like.dtype
+        if coded == rows:
+            rows, lanes, dtype = rows * lanes // (2 * width), width, F32
+        shapes.append(jax.ShapeDtypeStruct((len(pieces), rows, lanes), dtype))
     vmem = pl.BlockSpec(memory_space=pltpu.VMEM)
     size = sum(x.size for x in flat)
     return pl.pallas_call(
-        functools.partial(sums_kernel, [len(group) for group in groups], outs),
-        in_specs=[vmem] * len(flat),
+        functools.partial(sums_kernel, width, [len(group) for group in groups], outs, len(marks)),
+        in_specs=[vmem] * len(flat) + [pl.BlockSpec(memory_space=pl.ANY)] * len(marks),
         out_specs=[vmem] * len(outs),
         out_shape=shapes,
         compiler_params=pltpu.CompilerParams(vmem_limit_bytes=16 * 2**20),
         cost_estimate=pl.CostEstimate(flops=size, bytes_accessed=3 * size, transcendentals=0),
-    )(*flat)
-
-
-def mirrored_share(m_send, m_keep, paths):
+    )(*flat, *marks)
+
+
+def mirrored_share(m_send, m_keep, paths, width):
     col_bits = lax.axis_size("col").bit_length() - 1
-    width, owned = m_keep.shape[1:]
+    rows, owned = m_keep.shape[1:]
+    coded = rows - width
     part = width // paths
+    cuts = [0] + [coded + part * (path + 1) for path in range(paths)]
     bits = row_bits(lax.axis_size("row"))
     slots = [list(range(len(m_keep))) for _ in range(paths)]
     groups = [(m_keep, swap(m_send, "row", 1))]
@@ -451,57 +463,48 @@
         for path in range(paths):
             place = col_bits - 1 - n if path else n
             chosen_bits.append(bits[place])
-            low, group = (part * path, 0) if n == 0 else (0, path)
+            low, high = cuts[path : path + 2]
+            group = 0 if n == 0 else path
+            if n:
+                low, high = 0, high - low
+            codes = 0 if path else coded
             for send in (True, False):
                 chosen = [i for i, e in enumerate(slots[path]) if bool(e >> place & 1) == send]
-                outs.append([(p, group, i, low, low + part) for p, i in enumerate(chosen)])
+                outs.append([(p, group, i, low, high, codes) for p, i in enumerate(chosen)])
             slots[path] = [e for e in slots[path] if not e >> place & 1]
         made = yield groups, outs
         groups = [
             (made[2 * path + 1], swap(made[2 * path], "row", chosen_bits[path]))
             for path in range(paths)
         ]
-    (own,) = yield groups, [[(path, path, 0, 0, part) for path in range(paths)]]
-    return to_owner(own.reshape(width, owned))
-
-
-def direct_share(d_send, d_keep):
-    col_bits = lax.axis_size("col").bit_length() - 1
-    owned = d_keep.shape[1]
-    groups = [(d_keep, swap(d_send, "col", 1))]
-    slots = list(range(len(d_keep)))
-    for n in range(1, col_bits):
-        bit = 1 << (n - 1)
-        outs = []
-        for send in (True, False):
-            chosen = [i for i, e in enumerate(slots) if bool(e & bit) == send]
-            outs.append([(p, 0, i, 0, owned) for p, i in enumerate(chosen)])
-        slots = [e for e in slots if not e & bit]
-        d_send, d_keep = yield groups, outs
-        groups = [(d_keep, swap(d_send, "col", bit << 1))]
-    return groups[0]
-
-
-def diagonal_sum(y_send, y_keep, core, direct):
-    rows = y_keep.shape[1]
-    whole = [[(0, 0, 0, 0, rows)]]
-    (y,) = yield [(y_keep, swap(y_send, "row", 1))], whole
-    for axis, first in (("row", 2), ("col", 1)):
-        size = lax.axis_size(axis)
-        if direct:
-            steps = [range(first, size, first)]
-        else:
-            steps = [[first << n] for n in range((size // first).bit_length() - 1)]
-        for step in steps:
-            (y,) = yield [(y, *[swap(y, axis, bits) for bits in step])], whole
-    other = swap(y, "row", 1)[0]
-    return jnp.where(
-        core == 0, jnp.concatenate([y[0], other], 0), jnp.concatenate([other, y[0]], 0)
-    )
+    own = []
+    for path in range(paths):
+        first = 0 if path else coded
+        own.append((path, path, 0, first, first + part, 0))
+    own, y = yield groups, [own, [(0, 0, 0, 0, coded, coded)]]
+    return to_owner(own.reshape(width, owned)), y
+
+
+def diagonal_sum(ys):
+    y = jnp.concatenate(ys, 0)
+    bit = 1
+    while bit < lax.axis_size("col"):
+        y = y + swap(y, "col", bit)
+        bit *= 2
+    y = y[:, None]
+    bit = lax.axis_size("row") // 2
+    while bit:
+        other = swap(y, "row", bit)
+        low = (lax.axis_index("row") & bit) == 0
+        both = [jnp.where(low, y, other), jnp.where(low, other, y)]
+        y = jnp.stack(both, 2).reshape(y.shape[0], -1, *y.shape[2:])
+        bit //= 2
+    return y.reshape(y.shape[0], -1, y.shape[3])
 
 
 class Rounds:
-    def __init__(self, *chains):
+    def __init__(self, width, *chains):
+        self.width = width
         self.chains = chains
         self.results = [None] * len(chains)
         self.jobs = {}
@@ -515,13 +518,13 @@
             self.jobs.pop(n, None)
             self.results[n] = end.value
 
-    def advance(self):
+    def advance(self, *marks):
         groups, outs = [], []
         for job_groups, job_outs in self.jobs.values():
             for pieces in job_outs:
                 outs.append([(p, group + len(groups), *rest) for p, group, *rest in pieces])
             groups += job_groups
-        made = sums(groups, outs)
+        made = sums(groups, outs, self.width, marks)
         at = 0
         for n, (_, job_outs) in list(self.jobs.items()):
             self.send(n, made[at : at + len(job_outs)])
@@ -556,12 +559,13 @@
     sibs = member.shape[0]
     width = out.shape[1] // sibs
     s = 0
-    for n in range(0, len(refs) - 1, 3):
-        kept, got, mirrored = refs[n : n + 3]
+    for n in range(0, len(refs) - 1, 2):
+        parts, mirrored = refs[n : n + 2]
         for at in range(0, mirrored.shape[0], width):
             over = slice(at, at + width)
-            product = kept[0, :, over].astype(F32) + got[0, :, over].astype(F32)
-            product = product + mirrored[over, :].astype(F32).T
+            product = mirrored[over, :].astype(F32).T
+            for m in range(parts.shape[0]):
+                product = product + parts[m, :, over].astype(F32)
             listed = jnp.broadcast_to(member[s : s + 1, :].astype(F32), (LANES, owned)).T
             for q in range(0, width, LANES):
                 out[:, s * width + q : s * width + q + LANES] = jnp.where(
@@ -606,7 +610,7 @@
     plan = jnp.stack(
         [n + (1 - core) * (col_count // 2) for n in pairs]
         + [n + core * (col_count // 2) for n in pairs]
-        + [col_place, core, mixed % 2, row_place * block_rows - col_place * block_cols]
+        + [core, mixed % 2, row_place * block_rows - col_place * block_cols, chip]
     ).astype(jnp.int32)
 
     codes = jnp.stack([row_index // LANES, row_index % LANES], 1).astype(BF)
@@ -622,7 +626,6 @@
     marks = [mark] * (len(row_bits(row_count)) + 1)
     gathered = gather(owns, marks)
     both, direct = [], []
-    tables_marks, terms_marks = [()] * 2, [()] * 2
     row_inv = col_inv = member = None
     for s in range(sib_count):
         pieces = next(gathered)
@@ -634,29 +637,28 @@
                 inverse, row_place * row_lines + col_place * own_lines, own_lines, 1
             )
             member = own_inv.reshape(sib_count, owned)
-        last = s == sib_count - 1
-        before = ()
-        if s > 1:
-            before = tuple(chain.advance() for chain in both[:-1] + direct[:-1] if chain.jobs)
+        before = [chain.advance() for chain in both[-1:]] + direct[:-1]
         row_t, col, mark = tables(pieces, listed, chunks[s], row_inv[s], col_inv[s], before)
-        before = tuple(chain.advance() for chain in both if chain.jobs)
-        m_send, m_keep, d_send, d_keep, y_send, y_keep = terms(
-            plan, lower, diagonal, row_t, col, owned, before
-        )
         marks.append(mark)
-        both.append(
-            Rounds(
-                mirrored_share(m_send, m_keep, 2 if last else 1),
-                diagonal_sum(y_send, y_keep, core, last),
-            )
-        )
-        direct.append(Rounds(direct_share(d_send, d_keep)))
-    shares, diags = [], []
+        before = [chain.advance(mark) for chain in both if chain.jobs]
+        m_send, m_keep, parts = terms(plan, lower, diagonal, row_t, col, owned, before)
+        paths = 2 if s == sib_count - 1 else 1
+        both.append(Rounds(width, mirrored_share(m_send, m_keep, paths, width)))
+        direct.append(lax.all_to_all(parts, "col", 0, 0, tiled=True))
+    both[-1].advance(*direct[-2:-1])
+    mark = both[-1].advance()
+    for chain in both[:-1]:
+        while chain.jobs:
+            chain.advance(mark)
+    while both[-1].jobs:
+        both[-1].advance(*direct[-1:])
+    shares, ys = [], []
     for s in range(sib_count):
-        mirrored, diag = both[s].finish()
-        shares.append((*direct[s].finish()[0], mirrored))
-        diags.append(diag)
-    return finish(member, shares, width), diag_inverse + jnp.stack(diags)
+        mirrored, y = both[s].results[0]
+        shares.append((direct[s], mirrored))
+        ys.append(y)
+    diags = jnp.concatenate([diagonal_sum(ys[:-1]), diagonal_sum(ys[-1:])], 0)
+    return finish(member, shares, width), diag_inverse + diags
 
 
 def solution(mesh):

time: 293 us -> 260 us (0.89)
  waiting for transfers between devices: 98.2 us -> 68.9 us
  starting transfers between devices: 92.1 us -> 65.7 us
  Pallas kernels: 90.3 us -> 104 us
  local copies, waits for them, and re-layouts: 8.42 us -> 13.9 us
    ppermute x64 -> x45, starting transfers between devices: 82.9 us -> 43.7 us  [swap(): return lax.ppermute(x, axis, [(i, i ^ bit) for i in range(count)])]
    ppermute x64 -> x45, waiting for transfers between devices: 97.8 us -> 68.9 us  [swap(): return lax.ppermute(x, axis, [(i, i ^ bit) for i in range(count)])]
    all_to_all x0 -> x3, starting transfers between devices: none -> 13.4 us  [per_device(): direct.append(lax.all_to_all(parts, 'col', 0, 0, tiled=True))]
    pallas_call x16 -> x8, Pallas kernels: 2.76 us -> 8.59 us  [sums(): pl.pallas_call(functools.partial(sums_kernel, width, [len(group) for grou...]
    unnamed x22 -> x49, local copies, waits for them, and re-layouts: 7.23 us -> 10.8 us
    pallas_call x5, Pallas kernels: 1.77 us -> 4.79 us  [join(): pl.pallas_call(functools.partial(join_kernel, [len(group) for group in gr...]
  transfers between devices with their start and end apart: 67 -> 51, of which waited for: 19 -> 16; matrix products, arithmetic and copies ran while one was open for 1% -> 2% of each run, Pallas kernels for 25% -> 39%
where the time goes in v3:
time: 260 us; the launch traced here: 258 us
  Pallas kernels  104 us (40%)
  waiting for transfers between devices  68.9 us (27%)
  starting transfers between devices  65.7 us (25%)
  local copies, waits for them, and re-layouts  13.9 us (5%)
  other arithmetic  4.48 us (2%)
    ppermute x45, waiting for transfers between devices, swap(): return lax.ppermute(x, axis, [(i, i ^ bit) for i in range(count)])  68.9 us
    pallas_call x3, Pallas kernels, terms(): pl.pallas_call(terms_kernel, grid_spec=grid_spec, out_shape=[jax.ShapeDty...  44.8 us
    ppermute x45, starting transfers between devices, swap(): return lax.ppermute(x, axis, [(i, i ^ bit) for i in range(count)])  43.7 us
    pallas_call x3, Pallas kernels, tables(): pl.pallas_call(functools.partial(tables_kernel, chunk), in_specs=[smem, s...  31.2 us
    all_to_all x3, starting transfers between devices, per_device(): direct.append(lax.all_to_all(parts, 'col', 0, 0, tiled=True))  13.4 us
    unnamed x49, local copies, waits for them, and re-layouts  10.8 us
    pallas_call x8, Pallas kernels, sums(): pl.pallas_call(functools.partial(sums_kernel, width, [len(group) for grou...  8.59 us
    ppermute x3, starting transfers between devices, to_owner(): return lax.ppermute(x, ('row', 'col'), pairs)  8.58 us
  transfers between devices with their start and end apart: 51, of which 16 were waited for; matrix products, arithmetic and copies ran while one was open for 2% of the time, Pallas kernels for 39%

profile of v3, /device:TPU:4, one launch (start us, length us, event | category | flops | bytes accessed | tf_op | source)
XLA Modules:
  0.0 257.9 jit_solution(5046819230701558755)
XLA Ops:
  2.5 3.7 %collective-permute-start.2 = (bf16[272,256]{1,0:T(8,128)(2,1)S(1)}, bf16[272,256]{1,0:T(8,128)(2,1)S(1)}, u32[]{:S(2)}, u32[]{:S(2)}) collective-permute-start(bf16[272,256]{1,0:T(8,128)(2,1)S(1)} %fusion.1.refs_0_), channel_id=1, source_target_pairs={{0,3},{1,2},{2,1},{3,0},{4,7},{5,6},{6,5},{7,4},{8,11},{9,10},{10,... | collective-permute-start | bytes 417800 | tf_op jit(solution)/shard_map/ppermute | solution.py:17
  6.9 6.1 %shard_map.59 = (bf16[2048,4096]{1,0:T(8,128)(2,1)S(1)}, f32[2048,1]{1,0:T(8,128)S(1)}, f32[8,128]{1,0:T(8,128)S(1)}) custom-call(bf16[2048,4096]{1,0:T(8,128)(2,1)} %ancestor.1), custom_call_target="tpu_custom_call" | custom-call | flops 8388608 | bytes 33554432 | tf_op jit(solution)/shard_map/pallas_call | solution.py:275
  13.1 5.8 %copy-done.15 = bf16[2048,4096]{1,0:T(8,128)(2,1)} copy-done((bf16[2048,4096]{1,0:T(8,128)(2,1)}, bf16[2048,4096]{1,0:T(8,128)(2,1)S(1)}, u32[]{:S(2)}) %copy-start.15) | copy-done | bytes 16777240
  21.0 3.9 %collective-permute-start.7 = (bf16[256,256]{1,0:T(8,128)(2,1)S(1)}, bf16[256,256]{1,0:T(8,128)(2,1)S(1)}, u32[]{:S(2)}, u32[]{:S(2)}) collective-permute-start(bf16[256,256]{1,0:T(8,128)(2,1)S(1)} %get-tuple-element.64.refs_4_), channel_id=1, source_target_pairs={{0,3},{1,2},{2,1},{3,0},{4,7},{5,6},{6,5},{7,4},{8,11},{9,10},{10,... | collective-permute-start | bytes 393224 | tf_op jit(solution)/shard_map/ppermute | solution.py:17
  25.5 3.7 %collective-permute-done.7.refs_7_ = bf16[256,256]{1,0:T(8,128)(2,1)S(1)} collective-permute-done((bf16[256,256]{1,0:T(8,128)(2,1)S(1)}, bf16[256,256]{1,0:T(8,128)(2,1)S(1)}, u32[]{:S(2)}, u32[]{:S(2)}) %collective-permute-start.7) | collective-permute-done | bytes 131104 | tf_op jit(solution)/shard_map/ppermute | solution.py:17
  29.1 5.3 %collective-permute-done.6.refs_6_ = bf16[256,256]{1,0:T(8,128)(2,1)S(1)} collective-permute-done((bf16[256,256]{1,0:T(8,128)(2,1)S(1)}, bf16[256,256]{1,0:T(8,128)(2,1)S(1)}, u32[]{:S(2)}, u32[]{:S(2)}) %collective-permute-start.6) | collective-permute-done | bytes 131104 | tf_op jit(solution)/shard_map/ppermute | solution.py:17
  36.5 2.6 collective-permute-start.14
  40.4 3.1 %collective-permute-done.14.refs_11_ = bf16[256,256]{1,0:T(8,128)(2,1)S(1)} collective-permute-done((bf16[256,256]{1,0:T(8,128)(2,1)S(1)}, bf16[256,256]{1,0:T(8,128)(2,1)S(1)}, u32[]{:S(2)}, u32[]{:S(2)}) %collective-permute-start.14) | collective-permute-done | bytes 131104 | tf_op jit(solution)/shard_map/ppermute | solution.py:17
  44.5 3.6 %collective-permute-done.13.refs_10_ = bf16[256,256]{1,0:T(8,128)(2,1)S(1)} collective-permute-done((bf16[256,256]{1,0:T(8,128)(2,1)S(1)}, bf16[256,256]{1,0:T(8,128)(2,1)S(1)}, u32[]{:S(2)}, u32[]{:S(2)}) %collective-permute-start.13) | collective-permute-done | bytes 131104 | tf_op jit(solution)/shard_map/ppermute | solution.py:17
  48.2 4.8 %collective-permute-done.12.refs_9_ = bf16[256,256]{1,0:T(8,128)(2,1)S(1)} collective-permute-done((bf16[256,256]{1,0:T(8,128)(2,1)S(1)}, bf16[256,256]{1,0:T(8,128)(2,1)S(1)}, u32[]{:S(2)}, u32[]{:S(2)}) %collective-permute-start.12) | collective-permute-done | bytes 131104 | tf_op jit(solution)/shard_map/ppermute | solution.py:17
  61.1 6.5 %shard_map.63 = s32[3,128,128]{2,1,0:T(8,128)S(1)} custom-call(bf16[16,272,256]{2,1,0:T(8,128)(2,1)} %bitcast.5.p0, bf16[16,272,256]{2,1,0:T(8,128)(2,1)} %bitcast.6.p1), custom_call_target="tpu_custom_call" | custom-call | flops 4000000000 | bytes 196608 | tf_op jit(solution)/shard_map/pallas_call | solution.py:129
  68.9 10.5 %shard_map.64 = (bf16[256,2048]{1,0:T(8,128)(2,1)S(1)}, bf16[4096,256]{1,0:T(8,128)(2,1)S(1)}, f32[8,128]{1,0:T(8,128)S(1)}) custom-call(s32[16,128]{1,0:T(8,128)S(1)} %get-tuple-element.138.row_inv, s32[32,128]{1,0:T(8,128)S(1)} %get-tuple-element.135.col_inv, bf16[16,272,256]{2,1,0:T(8,128)(2,1)} %bitcast.5.p0, bf16[16,272,256]{2,1,0:T(8,128)(2,1)} %bitcast.6.p1), custom_call_target="tpu_custom_call" | custom-call | flops 10000000000 | bytes 7340032 | tf_op jit(solution)/shard_map/pallas_call | solution.py:205
  81.1 15.2 %shard_map.65 = (bf16[4,288,512]{2,1,0:T(8,128)(2,1)}, bf16[4,288,512]{2,1,0:T(8,128)(2,1)S(1)}, bf16[4,512,256]{2,1,0:T(8,128)(2,1)}) custom-call(s32[8]{0:T(128)S(1)} %copy-done.13, bf16[2048,4096]{1,0:T(8,128)(2,1)} %copy-done.15, f32[2048,1]{1,0:T(8,128)S(1)} %copy-done.17, bf16[256,2048]{1,0:T(8,128)(2,1)S(1)} %get-tuple-element.73.row_t, ...), custom_call_target="tpu_custom_call" | custom-call | flops 10737418240 | bytes 16777216 | tf_op jit(solution)/shard_map/pallas_call | solution.py:389
  96.7 3.8 %all-to-all-start = ((bf16[4,512,256]{2,1,0:T(8,128)(2,1)}), bf16[4,512,256]{2,1,0:T(8,128)(2,1)S(1)}, u32[]{:S(2)}, u32[]{:S(2)}) async-start(bf16[4,512,256]{2,1,0:T(8,128)(2,1)} %get-tuple-element.75), calls=%async_computation | async-start | bytes 2097152 | tf_op jit(solution)/shard_map/all_to_all | solution.py:647
  105.1 10.3 %shard_map.68 = (bf16[256,2048]{1,0:T(8,128)(2,1)S(1)}, bf16[4096,256]{1,0:T(8,128)(2,1)S(1)}, f32[8,128]{1,0:T(8,128)S(1)}) custom-call(s32[16,128]{1,0:T(8,128)S(1)} %copy-done.12, s32[32,128]{1,0:T(8,128)S(1)} %copy-done.10, bf16[16,256,256]{2,1,0:T(8,128)(2,1)} %bitcast.19.p0, bf16[16,256,256]{2,1,0:T(8,128)(2,1)} %bitcast.20.p1, ...), custom_call_target="tpu_custom_call" | custom-call | flops 10000000000 | bytes 7340032 | tf_op jit(solution)/shard_map/pallas_call | solution.py:205
  117.7 10.0 %collective-permute-done.17.refs_1_ = bf16[2,288,512]{2,1,0:T(8,128)(2,1)S(1)} collective-permute-done((bf16[2,288,512]{2,1,0:T(8,128)(2,1)S(1)}, bf16[2,288,512]{2,1,0:T(8,128)(2,1)S(1)}, u32[]{:S(2)}, u32[]{:S(2)}) %collective-permute-start.17) | collective-permute-done | bytes 589856 | tf_op jit(solution)/shard_map/ppermute | solution.py:17
  128.5 14.8 %shard_map.71 = (bf16[4,288,512]{2,1,0:T(8,128)(2,1)S(1)}, bf16[4,288,512]{2,1,0:T(8,128)(2,1)S(1)}, bf16[4,512,256]{2,1,0:T(8,128)(2,1)}) custom-call(s32[8]{0:T(128)S(1)} %copy-done.14, bf16[2048,4096]{1,0:T(8,128)(2,1)} %copy-done.15, f32[2048,1]{1,0:T(8,128)S(1)} %copy-done.18, bf16[256,2048]{1,0:T(8,128)(2,1)S(1)} %get-tuple-element.91.row_t, ...), custom_call_target="tpu_custom_call" | custom-call | flops 10737418240 | bytes 16777216 | tf_op jit(solution)/shard_map/pallas_call | solution.py:389
  147.7 4.5 %all-to-all-start.1 = ((bf16[4,512,256]{2,1,0:T(8,128)(2,1)}), bf16[4,512,256]{2,1,0:T(8,128)(2,1)S(1)}, u32[]{:S(2)}, u32[]{:S(2)}) async-start(bf16[4,512,256]{2,1,0:T(8,128)(2,1)} %get-tuple-element.98), calls=%async_computation.1 | async-start | bytes 2097152 | tf_op jit(solution)/shard_map/all_to_all | solution.py:647
  152.3 10.4 %shard_map.73 = (bf16[256,2048]{1,0:T(8,128)(2,1)S(1)}, bf16[4096,256]{1,0:T(8,128)(2,1)S(1)}, f32[8,128]{1,0:T(8,128)S(1)}) custom-call(s32[16,128]{1,0:T(8,128)S(1)} %copy-done.11, s32[32,128]{1,0:T(8,128)S(1)} %get-tuple-element.133.col_inv, bf16[16,256,256]{2,1,0:T(8,128)(2,1)} %bitcast.23.p0, bf16[16,256,256]{2,1,0:T(8,128)(2,1)} %bitcast.24.p1, ...), custom_call_target="tpu_custom_call" | custom-call | flops 10000000000 | bytes 7340032 | tf_op jit(solution)/shard_map/pallas_call | solution.py:205
  164.6 14.8 %shard_map.76 = (bf16[4,288,512]{2,1,0:T(8,128)(2,1)}, bf16[4,288,512]{2,1,0:T(8,128)(2,1)S(1)}, bf16[4,512,256]{2,1,0:T(8,128)(2,1)S(1)}) custom-call(s32[8]{0:T(128)S(1)} %copy-done.14, bf16[2048,4096]{1,0:T(8,128)(2,1)} %copy-done.15, f32[2048,1]{1,0:T(8,128)S(1)} %copy-done.19, bf16[256,2048]{1,0:T(8,128)(2,1)S(1)} %get-tuple-element.102.row_t, ...), custom_call_target="tpu_custom_call" | custom-call | flops 10737418240 | bytes 16777216 | tf_op jit(solution)/shard_map/pallas_call | solution.py:389
  181.5 5.1 %all-to-all-start.2 = ((bf16[4,512,256]{2,1,0:T(8,128)(2,1)}), bf16[4,512,256]{2,1,0:T(8,128)(2,1)S(1)}, u32[]{:S(2)}, u32[]{:S(2)}) async-start(bf16[4,512,256]{2,1,0:T(8,128)(2,1)} %copy-done.2), calls=%async_computation.2 | async-start | bytes 2097152 | tf_op jit(solution)/shard_map/all_to_all | solution.py:647
  192.9 7.2 %collective-permute-done.33.refs_3_ = bf16[2,128,512]{2,1,0:T(8,128)(2,1)S(1)} collective-permute-done((bf16[2,128,512]{2,1,0:T(8,128)(2,1)S(1)}, bf16[2,128,512]{2,1,0:T(8,128)(2,1)S(1)}, u32[]{:S(2)}, u32[]{:S(2)}) %collective-permute-start.33) | collective-permute-done | bytes 262176 | tf_op jit(solution)/shard_map/ppermute | solution.py:17
  202.7 3.7 %collective-permute-done.30 = bf16[1,288,512]{2,1,0:T(8,128)(2,1)S(1)} collective-permute-done((bf16[1,288,512]{2,1,0:T(8,128)(2,1)}, bf16[1,288,512]{2,1,0:T(8,128)(2,1)S(1)}, u32[]{:S(2)}, u32[]{:S(2)}) %collective-permute-start.30) | collective-permute-done | bytes 294944 | tf_op jit(solution)/shard_map/ppermute | solution.py:17
  207.2 2.1 collective-permute-start.38
  209.3 4.7 %collective-permute-done.38 = f32[2,32,256]{2,1,0:T(8,128)} collective-permute-done((f32[2,32,256]{2,1,0:T(8,128)S(1)}, f32[2,32,256]{2,1,0:T(8,128)}, u32[]{:S(2)}, u32[]{:S(2)}) %collective-permute-start.38) | collective-permute-done | bytes 65568 | tf_op jit(solution)/shard_map/ppermute | solution.py:17
  219.3 3.0 %collective-permute-start.28 = (bf16[256,512]{1,0:T(8,128)(2,1)}, bf16[256,512]{1,0:T(8,128)(2,1)S(1)}, u32[]{:S(2)}, u32[]{:S(2)}) collective-permute-start(bf16[256,512]{1,0:T(8,128)(2,1)} %bitcast.89), channel_id=1, source_target_pairs={{0,0},{1,10},{2,17},{3,27},{4,4},{5,14},{6,21},{7,31},{8,1},{9,11}... | collective-permute-start | bytes 786440 | tf_op jit(solution)/shard_map/ppermute | solution.py:553
  222.2 3.3 %collective-permute-start.34 = (bf16[256,512]{1,0:T(8,128)(2,1)}, bf16[256,512]{1,0:T(8,128)(2,1)S(1)}, u32[]{:S(2)}, u32[]{:S(2)}) collective-permute-start(bf16[256,512]{1,0:T(8,128)(2,1)} %bitcast.97), channel_id=1, source_target_pairs={{0,0},{1,10},{2,17},{3,27},{4,4},{5,14},{6,21},{7,31},{8,1},{9,11}... | collective-permute-start | bytes 786440 | tf_op jit(solution)/shard_map/ppermute | solution.py:553
  227.8 2.7 %collective-permute-start.40 = (f32[2,1,32,256]{3,2,0,1:T(8,128)S(1)}, f32[2,1,32,256]{3,2,0,1:T(8,128)S(1)}, u32[]{:S(2)}, u32[]{:S(2)}) collective-permute-start(f32[2,1,32,256]{3,2,0,1:T(8,128)S(1)} %add_bitcast_fusion), channel_id=1, source_target_pairs={{0,16},{4,20},{8,24},{12,28},{16,0},{20,4},{24,8},{28,12},{1,17},{... | collective-permute-start | bytes 196616 | tf_op jit(solution)/shard_map/ppermute | solution.py:17
  230.5 2.3 collective-permute-start.37
  232.8 10.3 %collective-permute-done.44 = f32[1,32,256]{2,1,0:T(8,128)S(1)} collective-permute-done((f32[1,32,256]{2,1,0:T(8,128)S(1)}, f32[1,32,256]{2,1,0:T(8,128)S(1)}, u32[]{:S(2)}, u32[]{:S(2)}) %collective-permute-start.44) | collective-permute-done | bytes 32800 | tf_op jit(solution)/shard_map/ppermute | solution.py:17
  243.2 3.9 %collective-permute-done.45 = f32[1,1,32,256]{3,2,1,0:T(8,128)S(1)} collective-permute-done((f32[1,1,32,256]{3,2,1,0:T(8,128)S(1)}, f32[1,1,32,256]{3,2,1,0:T(8,128)S(1)}, u32[]{:S(2)}, u32[]{:S(2)}) %collective-permute-start.45) | collective-permute-done | bytes 32800 | tf_op jit(solution)/shard_map/ppermute | solution.py:17
  249.3 2.8 %collective-permute-done.46 = f32[1,2,32,256]{3,2,1,0:T(8,128)S(1)} collective-permute-done((f32[1,2,32,256]{3,2,1,0:T(8,128)S(1)}, f32[1,2,32,256]{3,2,1,0:T(8,128)S(1)}, u32[]{:S(2)}, u32[]{:S(2)}) %collective-permute-start.46) | collective-permute-done | bytes 65568 | tf_op jit(solution)/shard_map/ppermute | solution.py:17
  (172 shorter events, 62.4 us)
Async XLA Ops:
  2.5 16.4 %collective-permute-start.2 = (bf16[272,256]{1,0:T(8,128)(2,1)S(1)}, bf16[272,256]{1,0:T(8,128)(2,1)S(1)}, u32[]{:S(2)}, u32[]{:S(2)}) collective-permute-start(bf16[272,256]{1,0:T(8,128)(2,1)S(1)} %fusion.1.refs_0_), channel_id=1, source_target_pairs={{0,3},{1,2},{2,1},{3,0},{4,7},{5,6},{6,5},{7,4},{8,11},{9,10},{10,... | collective-permute-start | bytes 417800 | tf_op jit(solution)/shard_map/ppermute | solution.py:17
  6.1 12.8 %collective-permute-start.1 = (bf16[272,256]{1,0:T(8,128)(2,1)S(1)}, bf16[272,256]{1,0:T(8,128)(2,1)S(1)}, u32[]{:S(2)}, u32[]{:S(2)}) collective-permute-start(bf16[272,256]{1,0:T(8,128)(2,1)S(1)} %fusion.1.refs_0_), channel_id=1, source_target_pairs={{0,2},{1,3},{2,0},{3,1},{4,6},{5,7},{6,4},{7,5},{8,10},{9,11},{10,... | collective-permute-start | bytes 417800 | tf_op jit(solution)/shard_map/ppermute | solution.py:17
  6.1 12.8 %collective-permute-start = (bf16[272,256]{1,0:T(8,128)(2,1)S(1)}, bf16[272,256]{1,0:T(8,128)(2,1)S(1)}, u32[]{:S(2)}, u32[]{:S(2)}) collective-permute-start(bf16[272,256]{1,0:T(8,128)(2,1)S(1)} %fusion.1.refs_0_), channel_id=1, source_target_pairs={{0,1},{1,0},{2,3},{3,2},{4,5},{5,4},{6,7},{7,6},{8,9},{9,8},{10,11... | collective-permute-start | bytes 417800 | tf_op jit(solution)/shard_map/ppermute | solution.py:17
  19.0 15.5 %collective-permute-start.3 = (bf16[544,256]{1,0:T(8,128)(2,1)S(1)}, bf16[544,256]{1,0:T(8,128)(2,1)S(1)}, u32[]{:S(2)}, u32[]{:S(2)}) collective-permute-start(bf16[544,256]{1,0:T(8,128)(2,1)S(1)} %get-tuple-element.62.refs_0_), channel_id=1, source_target_pairs={{0,8},{4,12},{8,0},{12,4},{16,24},{20,28},{24,16},{28,20},{1,9},{5... | collective-permute-start | bytes 835592 | tf_op jit(solution)/shard_map/ppermute | solution.py:17
  20.5 13.9 %collective-permute-start.4 = (bf16[544,256]{1,0:T(8,128)(2,1)S(1)}, bf16[544,256]{1,0:T(8,128)(2,1)S(1)}, u32[]{:S(2)}, u32[]{:S(2)}) collective-permute-start(bf16[544,256]{1,0:T(8,128)(2,1)S(1)} %get-tuple-element.63.refs_2_), channel_id=1, source_target_pairs={{0,16},{4,20},{8,24},{12,28},{16,0},{20,4},{24,8},{28,12},{1,17},{... | collective-permute-start | bytes 835592 | tf_op jit(solution)/shard_map/ppermute | solution.py:17
  34.6 20.1 %collective-permute-start.8 = (bf16[1088,256]{1,0:T(8,128)(2,1)S(1)}, bf16[1088,256]{1,0:T(8,128)(2,1)S(1)}, u32[]{:S(2)}, u32[]{:S(2)}) collective-permute-start(bf16[1088,256]{1,0:T(8,128)(2,1)S(1)} %get-tuple-element.65.refs_0_), channel_id=1, source_target_pairs={{0,16},{4,20},{8,24},{12,28},{16,0},{20,4},{24,8},{28,12},{1,17},{... | collective-permute-start | bytes 1671176 | tf_op jit(solution)/shard_map/ppermute | solution.py:17
  36.0 18.7 %collective-permute-start.9 = (bf16[1088,256]{1,0:T(8,128)(2,1)S(1)}, bf16[1088,256]{1,0:T(8,128)(2,1)S(1)}, u32[]{:S(2)}, u32[]{:S(2)}) collective-permute-start(bf16[1088,256]{1,0:T(8,128)(2,1)S(1)} %get-tuple-element.66.refs_2_), channel_id=1, source_target_pairs={{0,8},{4,12},{8,0},{12,4},{16,24},{20,28},{24,16},{28,20},{1,9},{5... | collective-permute-start | bytes 1671176 | tf_op jit(solution)/shard_map/ppermute | solution.py:17
  39.1 15.6 %collective-permute-start.10 = (bf16[512,256]{1,0:T(8,128)(2,1)S(1)}, bf16[512,256]{1,0:T(8,128)(2,1)S(1)}, u32[]{:S(2)}, u32[]{:S(2)}) collective-permute-start(bf16[512,256]{1,0:T(8,128)(2,1)S(1)} %get-tuple-element.67.refs_4_), channel_id=1, source_target_pairs={{0,8},{4,12},{8,0},{12,4},{16,24},{20,28},{24,16},{28,20},{1,9},{5... | collective-permute-start | bytes 786440 | tf_op jit(solution)/shard_map/ppermute | solution.py:17
  43.5 11.2 %collective-permute-start.11 = (bf16[512,256]{1,0:T(8,128)(2,1)S(1)}, bf16[512,256]{1,0:T(8,128)(2,1)S(1)}, u32[]{:S(2)}, u32[]{:S(2)}) collective-permute-start(bf16[512,256]{1,0:T(8,128)(2,1)S(1)} %get-tuple-element.68.refs_6_), channel_id=1, source_target_pairs={{0,16},{4,20},{8,24},{12,28},{16,0},{20,4},{24,8},{28,12},{1,17},{... | collective-permute-start | bytes 786440 | tf_op jit(solution)/shard_map/ppermute | solution.py:17
  57.0 22.4 %collective-permute-start.20 = (bf16[512,256]{1,0:T(8,128)(2,1)S(1)}, bf16[512,256]{1,0:T(8,128)(2,1)S(1)}, u32[]{:S(2)}, u32[]{:S(2)}) collective-permute-start(bf16[512,256]{1,0:T(8,128)(2,1)S(1)} %get-tuple-element.82.refs_4_), channel_id=1, source_target_pairs={{0,8},{4,12},{8,0},{12,4},{16,24},{20,28},{24,16},{28,20},{1,9},{5... | collective-permute-start | bytes 786440 | tf_op jit(solution)/shard_map/ppermute | solution.py:17
  57.5 21.9 %collective-permute-start.21 = (bf16[512,256]{1,0:T(8,128)(2,1)S(1)}, bf16[512,256]{1,0:T(8,128)(2,1)S(1)}, u32[]{:S(2)}, u32[]{:S(2)}) collective-permute-start(bf16[512,256]{1,0:T(8,128)(2,1)S(1)} %get-tuple-element.83.refs_6_), channel_id=1, source_target_pairs={{0,16},{4,20},{8,24},{12,28},{16,0},{20,4},{24,8},{28,12},{1,17},{... | collective-permute-start | bytes 786440 | tf_op jit(solution)/shard_map/ppermute | solution.py:17
  58.5 20.9 %collective-permute-start.18 = (bf16[1024,256]{1,0:T(8,128)(2,1)S(1)}, bf16[1024,256]{1,0:T(8,128)(2,1)S(1)}, u32[]{:S(2)}, u32[]{:S(2)}) collective-permute-start(bf16[1024,256]{1,0:T(8,128)(2,1)S(1)} %get-tuple-element.80.refs_0_), channel_id=1, source_target_pairs={{0,16},{4,20},{8,24},{12,28},{16,0},{20,4},{24,8},{28,12},{1,17},{... | collective-permute-start | bytes 1572872 | tf_op jit(solution)/shard_map/ppermute | solution.py:17
  59.5 19.9 %collective-permute-start.19 = (bf16[1024,256]{1,0:T(8,128)(2,1)S(1)}, bf16[1024,256]{1,0:T(8,128)(2,1)S(1)}, u32[]{:S(2)}, u32[]{:S(2)}) collective-permute-start(bf16[1024,256]{1,0:T(8,128)(2,1)S(1)} %get-tuple-element.81.refs_2_), channel_id=1, source_target_pairs={{0,8},{4,12},{8,0},{12,4},{16,24},{20,28},{24,16},{28,20},{1,9},{5... | collective-permute-start | bytes 1572872 | tf_op jit(solution)/shard_map/ppermute | solution.py:17
  81.0 24.1 %collective-permute-start.22 = (bf16[4096,256]{1,0:T(8,128)(2,1)}, bf16[4096,256]{1,0:T(8,128)(2,1)}, u32[]{:S(2)}, u32[]{:S(2)}) collective-permute-start(bf16[4096,256]{1,0:T(8,128)(2,1)} %get-tuple-element.85), channel_id=1, source_target_pairs={{0,4},{4,0},{8,12},{12,8},{16,20},{20,16},{24,28},{28,24},{1,5},{5... | collective-permute-start | bytes 6291464 | tf_op jit(solution)/shard_map/ppermute | solution.py:17
  96.7 51.0 %all-to-all-start = ((bf16[4,512,256]{2,1,0:T(8,128)(2,1)}), bf16[4,512,256]{2,1,0:T(8,128)(2,1)S(1)}, u32[]{:S(2)}, u32[]{:S(2)}) async-start(bf16[4,512,256]{2,1,0:T(8,128)(2,1)} %get-tuple-element.75), calls=%async_computation | async-start | bytes 2097152 | tf_op jit(solution)/shard_map/all_to_all | solution.py:647
  100.5 14.9 %collective-permute-start.24 = (bf16[1024,256]{1,0:T(8,128)(2,1)S(1)}, bf16[1024,256]{1,0:T(8,128)(2,1)S(1)}, u32[]{:S(2)}, u32[]{:S(2)}) collective-permute-start(bf16[1024,256]{1,0:T(8,128)(2,1)S(1)} %get-tuple-element.89.refs_0_), channel_id=1, source_target_pairs={{0,16},{4,20},{8,24},{12,28},{16,0},{20,4},{24,8},{28,12},{1,17},{... | collective-permute-start | bytes 1572872 | tf_op jit(solution)/shard_map/ppermute | solution.py:17
  101.4 14.8 %collective-permute-start.25 = (bf16[1024,256]{1,0:T(8,128)(2,1)S(1)}, bf16[1024,256]{1,0:T(8,128)(2,1)S(1)}, u32[]{:S(2)}, u32[]{:S(2)}) collective-permute-start(bf16[1024,256]{1,0:T(8,128)(2,1)S(1)} %get-tuple-element.90.refs_2_), channel_id=1, source_target_pairs={{0,8},{4,12},{8,0},{12,4},{16,24},{20,28},{24,16},{28,20},{1,9},{5... | collective-permute-start | bytes 1572872 | tf_op jit(solution)/shard_map/ppermute | solution.py:17
  103.6 24.1 %collective-permute-start.17 = (bf16[2,288,512]{2,1,0:T(8,128)(2,1)S(1)}, bf16[2,288,512]{2,1,0:T(8,128)(2,1)S(1)}, u32[]{:S(2)}, u32[]{:S(2)}) collective-permute-start(bf16[2,288,512]{2,1,0:T(8,128)(2,1)S(1)} %get-tuple-element.79), channel_id=1, source_target_pairs={{0,8},{4,12},{8,0},{12,4},{16,24},{20,28},{24,16},{28,20},{1,9},{5... | collective-permute-start | bytes 1769480 | tf_op jit(solution)/shard_map/ppermute | solution.py:17
  117.7 34.5 %collective-permute-start.26 = (bf16[4096,256]{1,0:T(8,128)(2,1)}, bf16[4096,256]{1,0:T(8,128)(2,1)}, u32[]{:S(2)}, u32[]{:S(2)}) collective-permute-start(bf16[4096,256]{1,0:T(8,128)(2,1)} %shard_map.70), channel_id=1, source_target_pairs={{0,4},{4,0},{8,12},{12,8},{16,20},{20,16},{24,28},{28,24},{1,5},{5... | collective-permute-start | bytes 6291464 | tf_op jit(solution)/shard_map/ppermute | solution.py:17
  143.3 19.5 %collective-permute-start.23 = (bf16[1,288,512]{2,1,0:T(8,128)(2,1)}, bf16[1,288,512]{2,1,0:T(8,128)(2,1)}, u32[]{:S(2)}, u32[]{:S(2)}) collective-permute-start(bf16[1,288,512]{2,1,0:T(8,128)(2,1)} %get-tuple-element.88), channel_id=1, source_target_pairs={{0,16},{4,20},{8,24},{12,28},{16,0},{20,4},{24,8},{28,12},{1,17},{... | collective-permute-start | bytes 884744 | tf_op jit(solution)/shard_map/ppermute | solution.py:17
  147.1 16.7 %collective-permute-start.29 = (bf16[2,288,512]{2,1,0:T(8,128)(2,1)}, bf16[2,288,512]{2,1,0:T(8,128)(2,1)S(1)}, u32[]{:S(2)}, u32[]{:S(2)}) collective-permute-start(bf16[2,288,512]{2,1,0:T(8,128)(2,1)} %get-tuple-element.99), channel_id=1, source_target_pairs={{0,8},{4,12},{8,0},{12,4},{16,24},{20,28},{24,16},{28,20},{1,9},{5... | collective-permute-start | bytes 1769480 | tf_op jit(solution)/shard_map/ppermute | solution.py:17
  147.7 33.7 %all-to-all-start.1 = ((bf16[4,512,256]{2,1,0:T(8,128)(2,1)}), bf16[4,512,256]{2,1,0:T(8,128)(2,1)S(1)}, u32[]{:S(2)}, u32[]{:S(2)}) async-start(bf16[4,512,256]{2,1,0:T(8,128)(2,1)} %get-tuple-element.98), calls=%async_computation.1 | async-start | bytes 2097152 | tf_op jit(solution)/shard_map/all_to_all | solution.py:647
  181.5 34.0 %all-to-all-start.2 = ((bf16[4,512,256]{2,1,0:T(8,128)(2,1)}), bf16[4,512,256]{2,1,0:T(8,128)(2,1)S(1)}, u32[]{:S(2)}, u32[]{:S(2)}) async-start(bf16[4,512,256]{2,1,0:T(8,128)(2,1)} %copy-done.2), calls=%async_computation.2 | async-start | bytes 2097152 | tf_op jit(solution)/shard_map/all_to_all | solution.py:647
  192.1 14.3 %collective-permute-start.30 = (bf16[1,288,512]{2,1,0:T(8,128)(2,1)}, bf16[1,288,512]{2,1,0:T(8,128)(2,1)S(1)}, u32[]{:S(2)}, u32[]{:S(2)}) collective-permute-start(bf16[1,288,512]{2,1,0:T(8,128)(2,1)} %get-tuple-element.101), channel_id=1, source_target_pairs={{0,16},{4,20},{8,24},{12,28},{16,0},{20,4},{24,8},{28,12},{1,17},{... | collective-permute-start | bytes 884744 | tf_op jit(solution)/shard_map/ppermute | solution.py:17
  200.9 14.6 %collective-permute-start.36 = (bf16[1,128,512]{2,1,0:T(8,128)(2,1)}, bf16[1,128,512]{2,1,0:T(8,128)(2,1)}, u32[]{:S(2)}, u32[]{:S(2)}) collective-permute-start(bf16[1,128,512]{2,1,0:T(8,128)(2,1)} %get-tuple-element.116), channel_id=1, source_target_pairs={{0,8},{4,12},{8,0},{12,4},{16,24},{20,28},{24,16},{28,20},{1,9},{5... | collective-permute-start | bytes 393224 | tf_op jit(solution)/shard_map/ppermute | solution.py:17
  201.5 14.0 %collective-permute-start.35 = (bf16[1,160,512]{2,1,0:T(8,128)(2,1)}, bf16[1,160,512]{2,1,0:T(8,128)(2,1)}, u32[]{:S(2)}, u32[]{:S(2)}) collective-permute-start(bf16[1,160,512]{2,1,0:T(8,128)(2,1)} %get-tuple-element.115), channel_id=1, source_target_pairs={{0,16},{4,20},{8,24},{12,28},{16,0},{20,4},{24,8},{28,12},{1,17},{... | collective-permute-start | bytes 491528 | tf_op jit(solution)/shard_map/ppermute | solution.py:17
  214.8 12.1 %collective-permute-start.39 = (f32[2,32,256]{2,1,0:T(8,128)S(1)}, f32[2,32,256]{2,1,0:T(8,128)}, u32[]{:S(2)}, u32[]{:S(2)}) collective-permute-start(f32[2,32,256]{2,1,0:T(8,128)S(1)} %add.73), channel_id=1, source_target_pairs={{0,2},{1,3},{2,0},{3,1},{4,6},{5,7},{6,4},{7,5},{8,10},{9,11},{10,... | collective-permute-start | bytes 196616 | tf_op jit(solution)/shard_map/ppermute | solution.py:17
  219.3 34.8 %collective-permute-start.28 = (bf16[256,512]{1,0:T(8,128)(2,1)}, bf16[256,512]{1,0:T(8,128)(2,1)S(1)}, u32[]{:S(2)}, u32[]{:S(2)}) collective-permute-start(bf16[256,512]{1,0:T(8,128)(2,1)} %bitcast.89), channel_id=1, source_target_pairs={{0,0},{1,10},{2,17},{3,27},{4,4},{5,14},{6,21},{7,31},{8,1},{9,11}... | collective-permute-start | bytes 786440 | tf_op jit(solution)/shard_map/ppermute | solution.py:553
  222.2 31.9 %collective-permute-start.34 = (bf16[256,512]{1,0:T(8,128)(2,1)}, bf16[256,512]{1,0:T(8,128)(2,1)S(1)}, u32[]{:S(2)}, u32[]{:S(2)}) collective-permute-start(bf16[256,512]{1,0:T(8,128)(2,1)} %bitcast.97), channel_id=1, source_target_pairs={{0,0},{1,10},{2,17},{3,27},{4,4},{5,14},{6,21},{7,31},{8,1},{9,11}... | collective-permute-start | bytes 786440 | tf_op jit(solution)/shard_map/ppermute | solution.py:553
  225.6 17.6 %collective-permute-start.44 = (f32[1,32,256]{2,1,0:T(8,128)S(1)}, f32[1,32,256]{2,1,0:T(8,128)S(1)}, u32[]{:S(2)}, u32[]{:S(2)}) collective-permute-start(f32[1,32,256]{2,1,0:T(8,128)S(1)} %add.75), channel_id=1, source_target_pairs={{0,2},{1,3},{2,0},{3,1},{4,6},{5,7},{6,4},{7,5},{8,10},{9,11},{10,... | collective-permute-start | bytes 98312 | tf_op jit(solution)/shard_map/ppermute | solution.py:17
  227.8 15.3 %collective-permute-start.40 = (f32[2,1,32,256]{3,2,0,1:T(8,128)S(1)}, f32[2,1,32,256]{3,2,0,1:T(8,128)S(1)}, u32[]{:S(2)}, u32[]{:S(2)}) collective-permute-start(f32[2,1,32,256]{3,2,0,1:T(8,128)S(1)} %add_bitcast_fusion), channel_id=1, source_target_pairs={{0,16},{4,20},{8,24},{12,28},{16,0},{20,4},{24,8},{28,12},{1,17},{... | collective-permute-start | bytes 196616 | tf_op jit(solution)/shard_map/ppermute | solution.py:17
  230.5 23.6 %collective-permute-start.37 = (bf16[256,512]{1,0:T(8,128)(2,1)S(1)}, bf16[256,512]{1,0:T(8,128)(2,1)S(1)}, u32[]{:S(2)}, u32[]{:S(2)}) collective-permute-start(bf16[256,512]{1,0:T(8,128)(2,1)S(1)} %bitcast.90), channel_id=1, source_target_pairs={{0,0},{1,10},{2,17},{3,27},{4,4},{5,14},{6,21},{7,31},{8,1},{9,11}... | collective-permute-start | bytes 786440 | tf_op jit(solution)/shard_map/ppermute | solution.py:553
  (42 other events, 327.6 us)

commit v4 on v3

--- a/solution.py
+++ b/solution.py
@@ -90,13 +90,14 @@
             yield [state[done][0], swap(state[done][0], "row", 1)]
 
 
-def invert_kernel(listed, sibs, p0, p1, out_ref):
+def invert_kernel(listed, lists, p0, p1, *refs):
+    out_ref = refs[-1]
     pieces = (p0, p1)
     lines = out_ref.shape[1]
     count, _, wide = p0.shape
     line_ids = lax.broadcasted_iota(jnp.int32, (lines, wide), 0).astype(F32)
     lane_ids = lax.broadcasted_iota(jnp.int32, (LANES, wide), 0).astype(F32)
-    for s in range(sibs):
+    for at, s in enumerate(lists):
         total = jnp.zeros((lines, 2 * LANES), F32)
         for n, piece in enumerate(pieces):
             left, right = [], []
@@ -119,23 +120,23 @@
                 (((1,), (1,)), ((), ())),
                 preferred_element_type=F32,
             )
-        out_ref[s] = (total[:, :LANES] * LANES + total[:, LANES:]).astype(jnp.int32)
-
-
-def invert(pieces, chunk, codes, sibs, rows):
+        out_ref[at] = (total[:, :LANES] * LANES + total[:, LANES:]).astype(jnp.int32)
+
+
+def invert(pieces, chunk, codes, lists, rows, marks):
     width = pieces[0].shape[1]
     pieces = [p.reshape(-1, chunk + codes, width) for p in pieces]
     vmem = pl.BlockSpec(memory_space=pltpu.VMEM)
     return pl.pallas_call(
-        functools.partial(invert_kernel, chunk, sibs),
-        in_specs=[vmem] * 2,
+        functools.partial(invert_kernel, chunk, lists),
+        in_specs=[vmem] * 2 + [pl.BlockSpec(memory_space=pl.ANY)] * len(marks),
         out_specs=pl.BlockSpec(memory_space=pltpu.VMEM),
-        out_shape=jax.ShapeDtypeStruct((sibs, rows // LANES, LANES), jnp.int32),
+        out_shape=jax.ShapeDtypeStruct((len(lists), rows // LANES, LANES), jnp.int32),
         compiler_params=pltpu.CompilerParams(vmem_limit_bytes=16 * 2**20),
         cost_estimate=pl.CostEstimate(
-            flops=4 * 10**9, bytes_accessed=4 * sibs * rows, transcendentals=0
+            flops=10**9 * len(lists), bytes_accessed=4 * len(lists) * rows, transcendentals=0
         ),
-    )(*pieces)
+    )(*pieces, *marks)
 
 
 def tables_kernel(chunk, row_inv, col_inv, p0, p1, *refs):
@@ -485,20 +486,23 @@
     return to_owner(own.reshape(width, owned)), y
 
 
-def diagonal_sum(ys):
-    y = jnp.concatenate(ys, 0)
-    bit = 1
-    while bit < lax.axis_size("col"):
-        y = y + swap(y, "col", bit)
-        bit *= 2
-    y = y[:, None]
+def diagonal_sum(ys, early):
+    y = jnp.concatenate(ys, 0)[:, None]
+    bits = []
     bit = lax.axis_size("row") // 2
     while bit:
+        bits.append(bit)
+        bit //= 2
+    for n, bit in enumerate(bits):
+        if n == (0 if early else len(bits) - 1):
+            along = 1
+            while along < lax.axis_size("col"):
+                y = y + swap(y, "col", along)
+                along *= 2
         other = swap(y, "row", bit)
         low = (lax.axis_index("row") & bit) == 0
         both = [jnp.where(low, y, other), jnp.where(low, other, y)]
         y = jnp.stack(both, 2).reshape(y.shape[0], -1, *y.shape[2:])
-        bit //= 2
     return y.reshape(y.shape[0], -1, y.shape[3])
 
 
@@ -626,23 +630,31 @@
     marks = [mark] * (len(row_bits(row_count)) + 1)
     gathered = gather(owns, marks)
     both, direct = [], []
-    row_inv = col_inv = member = None
+    row_inv = col_inv = None
+    members = []
     for s in range(sib_count):
         pieces = next(gathered)
         if s == 0:
-            inverse = invert(pieces, listed, code_rows, sib_count, block_rows * row_count)
+            coded = pieces
+            inverse = invert(coded, listed, code_rows, [0], block_rows * row_count, [])
+        elif s == 1:
+            rest = list(range(1, sib_count))
+            inverse = invert(coded, listed, code_rows, rest, block_rows * row_count, [mark])
+        if s < 2:
             row_inv = lax.dynamic_slice_in_dim(inverse, row_place * row_lines, row_lines, 1)
             col_inv = lax.dynamic_slice_in_dim(inverse, col_place * col_lines, col_lines, 1)
             own_inv = lax.dynamic_slice_in_dim(
                 inverse, row_place * row_lines + col_place * own_lines, own_lines, 1
             )
-            member = own_inv.reshape(sib_count, owned)
-        before = [chain.advance() for chain in both[-1:]] + direct[:-1]
-        row_t, col, mark = tables(pieces, listed, chunks[s], row_inv[s], col_inv[s], before)
+            members.append(own_inv.reshape(-1, owned))
+        at = max(s - 1, 0)
+        before = [chain.advance() for chain in both if chain.jobs] + direct[:-1]
+        row_t, col, mark = tables(pieces, listed, chunks[s], row_inv[at], col_inv[at], before)
         marks.append(mark)
-        before = [chain.advance(mark) for chain in both if chain.jobs]
+        before = [chain.advance(mark) for chain in both[-1:] if chain.jobs]
+        before += [chain.results[0][0] for chain in both if not chain.jobs]
         m_send, m_keep, parts = terms(plan, lower, diagonal, row_t, col, owned, before)
-        paths = 2 if s == sib_count - 1 else 1
+        paths = 2
         both.append(Rounds(width, mirrored_share(m_send, m_keep, paths, width)))
         direct.append(lax.all_to_all(parts, "col", 0, 0, tiled=True))
     both[-1].advance(*direct[-2:-1])
@@ -657,8 +669,8 @@
         mirrored, y = both[s].results[0]
         shares.append((direct[s], mirrored))
         ys.append(y)
-    diags = jnp.concatenate([diagonal_sum(ys[:-1]), diagonal_sum(ys[-1:])], 0)
-    return finish(member, shares, width), diag_inverse + diags
+    diags = jnp.concatenate([diagonal_sum(ys[:-1], True), diagonal_sum(ys[-1:], False)], 0)
+    return finish(jnp.concatenate(members, 0), shares, width), diag_inverse + diags
 
 
 def solution(mesh):

time: 260 us -> 257 us (0.988)
  waiting for transfers between devices: 68.9 us -> 41.4 us
  starting transfers between devices: 65.7 us -> 87.3 us
  local copies, waits for them, and re-layouts: 13.9 us -> 16.8 us
    ppermute x45 -> x49, waiting for transfers between devices: 68.9 us -> 41.4 us  [swap(): return lax.ppermute(x, axis, [(i, i ^ bit) for i in range(count)])]
    ppermute x45 -> x49, starting transfers between devices: 43.7 us -> 59.9 us  [swap(): return lax.ppermute(x, axis, [(i, i ^ bit) for i in range(count)])]
    ppermute x3, starting transfers between devices: 8.58 us -> 13.7 us  [to_owner(): return lax.ppermute(x, ('row', 'col'), pairs)]
    unnamed x49 -> x56, local copies, waits for them, and re-layouts: 10.8 us -> 14.8 us
    pallas_call x1 -> x2, Pallas kernels: 6.51 us -> 7.61 us  [invert(): pl.pallas_call(functools.partial(invert_kernel, chunk, lists), in_specs=[...]
    pallas_call x8 -> x9, Pallas kernels: 8.59 us -> 8.64 us  [sums(): pl.pallas_call(functools.partial(sums_kernel, width, [len(group) for grou...]
  transfers between devices with their start and end apart: 51 -> 55, of which waited for: 16 -> 18; matrix products, arithmetic and copies ran while one was open for 2% -> 1% of each run, Pallas kernels for 39% -> 40%
where the time goes in v4:
time: 257 us; the launch traced here: 254 us
  Pallas kernels  104 us (40%)
  starting transfers between devices  87.3 us (34%)
  waiting for transfers between devices  41.4 us (16%)
  local copies, waits for them, and re-layouts  16.8 us (7%)
  other arithmetic  3.5 us (1%)
    ppermute x49, starting transfers between devices, swap(): return lax.ppermute(x, axis, [(i, i ^ bit) for i in range(count)])  59.9 us
    pallas_call x3, Pallas kernels, terms(): pl.pallas_call(terms_kernel, grid_spec=grid_spec, out_shape=[jax.ShapeDty...  44.8 us
    ppermute x49, waiting for transfers between devices, swap(): return lax.ppermute(x, axis, [(i, i ^ bit) for i in range(count)])  41.4 us
    pallas_call x3, Pallas kernels, tables(): pl.pallas_call(functools.partial(tables_kernel, chunk), in_specs=[smem, s...  30.6 us
    unnamed x56, local copies, waits for them, and re-layouts  14.8 us
    ppermute x3, starting transfers between devices, to_owner(): return lax.ppermute(x, ('row', 'col'), pairs)  13.7 us
    all_to_all x3, starting transfers between devices, per_device(): direct.append(lax.all_to_all(parts, 'col', 0, 0, tiled=True))  13.7 us
    pallas_call x9, Pallas kernels, sums(): pl.pallas_call(functools.partial(sums_kernel, width, [len(group) for grou...  8.64 us
  transfers between devices with their start and end apart: 55, of which 18 were waited for; matrix products, arithmetic and copies ran while one was open for 1% of the time, Pallas kernels for 40%

profile of v4, /device:TPU:4, one launch (start us, length us, event | category | flops | bytes accessed | tf_op | source)
XLA Modules:
  0.0 254.2 jit_solution(5722656172204980752)
XLA Ops:
  4.1 2.6 %collective-permute-start.1 = (bf16[272,256]{1,0:T(8,128)(2,1)S(1)}, bf16[272,256]{1,0:T(8,128)(2,1)S(1)}, u32[]{:S(2)}, u32[]{:S(2)}) collective-permute-start(bf16[272,256]{1,0:T(8,128)(2,1)S(1)} %fusion.1.refs_0_), channel_id=1, source_target_pairs={{0,2},{1,3},{2,0},{3,1},{4,6},{5,7},{6,4},{7,5},{8,10},{9,11},{10,... | collective-permute-start | bytes 417800 | tf_op jit(solution)/shard_map/ppermute | solution.py:17
  6.9 6.1 %shard_map.59 = (bf16[2048,4096]{1,0:T(8,128)(2,1)S(1)}, f32[2048,1]{1,0:T(8,128)S(1)}, f32[8,128]{1,0:T(8,128)S(1)}) custom-call(bf16[2048,4096]{1,0:T(8,128)(2,1)} %ancestor.1), custom_call_target="tpu_custom_call" | custom-call | flops 8388608 | bytes 33554432 | tf_op jit(solution)/shard_map/pallas_call | solution.py:276
  13.1 5.8 %copy-done.19 = bf16[2048,4096]{1,0:T(8,128)(2,1)} copy-done((bf16[2048,4096]{1,0:T(8,128)(2,1)}, bf16[2048,4096]{1,0:T(8,128)(2,1)S(1)}, u32[]{:S(2)}) %copy-start.19) | copy-done | bytes 16777240
  22.0 3.4 %collective-permute-start.6 = (bf16[256,256]{1,0:T(8,128)(2,1)S(1)}, bf16[256,256]{1,0:T(8,128)(2,1)S(1)}, u32[]{:S(2)}, u32[]{:S(2)}) collective-permute-start(bf16[256,256]{1,0:T(8,128)(2,1)S(1)} %get-tuple-element.72.refs_4_), channel_id=1, source_target_pairs={{0,2},{1,3},{2,0},{3,1},{4,6},{5,7},{6,4},{7,5},{8,10},{9,11},{10,... | collective-permute-start | bytes 393224 | tf_op jit(solution)/shard_map/ppermute | solution.py:17
  27.3 7.0 %collective-permute-done.6.refs_6_ = bf16[256,256]{1,0:T(8,128)(2,1)S(1)} collective-permute-done((bf16[256,256]{1,0:T(8,128)(2,1)S(1)}, bf16[256,256]{1,0:T(8,128)(2,1)S(1)}, u32[]{:S(2)}, u32[]{:S(2)}) %collective-permute-start.6) | collective-permute-done | bytes 131104 | tf_op jit(solution)/shard_map/ppermute | solution.py:17
  42.3 3.8 %collective-permute-done.13.refs_10_ = bf16[256,256]{1,0:T(8,128)(2,1)S(1)} collective-permute-done((bf16[256,256]{1,0:T(8,128)(2,1)S(1)}, bf16[256,256]{1,0:T(8,128)(2,1)S(1)}, u32[]{:S(2)}, u32[]{:S(2)}) %collective-permute-start.13) | collective-permute-done | bytes 131104 | tf_op jit(solution)/shard_map/ppermute | solution.py:17
  46.2 4.7 %collective-permute-start.14 = (bf16[256,256]{1,0:T(8,128)(2,1)S(1)}, bf16[256,256]{1,0:T(8,128)(2,1)S(1)}, u32[]{:S(2)}, u32[]{:S(2)}) collective-permute-start(bf16[256,256]{1,0:T(8,128)(2,1)S(1)} %get-tuple-element.77.refs_8_), channel_id=1, source_target_pairs={{0,3},{1,2},{2,1},{3,0},{4,7},{5,6},{6,5},{7,4},{8,11},{9,10},{10,... | collective-permute-start | bytes 393224 | tf_op jit(solution)/shard_map/ppermute | solution.py:17
  50.8 2.9 %collective-permute-done.14.refs_11_ = bf16[256,256]{1,0:T(8,128)(2,1)S(1)} collective-permute-done((bf16[256,256]{1,0:T(8,128)(2,1)S(1)}, bf16[256,256]{1,0:T(8,128)(2,1)S(1)}, u32[]{:S(2)}, u32[]{:S(2)}) %collective-permute-start.14) | collective-permute-done | bytes 131104 | tf_op jit(solution)/shard_map/ppermute | solution.py:17
  59.3 3.1 %shard_map.63 = s32[1,128,128]{2,1,0:T(8,128)S(1)} custom-call(bf16[16,272,256]{2,1,0:T(8,128)(2,1)S(1)} %bitcast.94, bf16[16,272,256]{2,1,0:T(8,128)(2,1)} %bitcast.6.p1), custom_call_target="tpu_custom_call" | custom-call | flops 1000000000 | bytes 65536 | tf_op jit(solution)/shard_map/pallas_call | solution.py:130
  63.1 9.9 %shard_map.64 = (bf16[256,2048]{1,0:T(8,128)(2,1)S(1)}, bf16[4096,256]{1,0:T(8,128)(2,1)S(1)}, f32[8,128]{1,0:T(8,128)S(1)}) custom-call(s32[16,128]{1,0:T(8,128)S(1)} %dynamic-slice_bitcast_fusion.5.row_inv, s32[32,128]{1,0:T(8,128)S(1)} %dynamic-slice_bitcast_fusion.2.col_inv, bf16[16,272,256]{2,1,0:T(8,128)(2,1)S(1)} %bitcast.95, ...), custom_call_target="tpu_custom_call" | custom-call | flops 10000000000 | bytes 7340032 | tf_op jit(solution)/shard_map/pallas_call | solution.py:206
  73.0 2.1 collective-permute-done.21.refs_5_
  76.7 15.2 %shard_map.66 = (bf16[4,288,512]{2,1,0:T(8,128)(2,1)}, bf16[4,288,512]{2,1,0:T(8,128)(2,1)S(1)}, bf16[4,512,256]{2,1,0:T(8,128)(2,1)}) custom-call(s32[8]{0:T(128)S(1)} %stack.104.plan, bf16[2048,4096]{1,0:T(8,128)(2,1)} %copy-done.19, f32[2048,1]{1,0:T(8,128)S(1)} %copy-done.21, bf16[256,2048]{1,0:T(8,128)(2,1)S(1)} %get-tuple-element.82.row_t, ...), custom_call_target="tpu_custom_call" | custom-call | flops 10737418240 | bytes 16777216 | tf_op jit(solution)/shard_map/pallas_call | solution.py:390
  92.4 5.1 %all-to-all-start = ((bf16[4,512,256]{2,1,0:T(8,128)(2,1)}), bf16[4,512,256]{2,1,0:T(8,128)(2,1)S(1)}, u32[]{:S(2)}, u32[]{:S(2)}) async-start(bf16[4,512,256]{2,1,0:T(8,128)(2,1)} %get-tuple-element.84), calls=%async_computation | async-start | bytes 2097152 | tf_op jit(solution)/shard_map/all_to_all | solution.py:659
  102.0 4.5 %shard_map.65 = s32[2,128,128]{2,1,0:T(8,128)S(1)} custom-call(bf16[16,272,256]{2,1,0:T(8,128)(2,1)S(1)} %bitcast.96, bf16[16,272,256]{2,1,0:T(8,128)(2,1)} %bitcast.6.p1, f32[8,128]{1,0:T(8,128)S(1)} %get-tuple-element.79.refs_0_.refs_8_), custom_call_target="tpu_custom_call" | custom-call | flops 2000000000 | bytes 131072 | tf_op jit(solution)/shard_map/pallas_call | solution.py:130
  109.3 10.3 %shard_map.69 = (bf16[256,2048]{1,0:T(8,128)(2,1)S(1)}, bf16[4096,256]{1,0:T(8,128)(2,1)S(1)}, f32[8,128]{1,0:T(8,128)S(1)}) custom-call(s32[16,128]{1,0:T(8,128)S(1)} %get-tuple-element.152.row_inv, s32[32,128]{1,0:T(8,128)S(1)} %get-tuple-element.150.col_inv, bf16[16,256,256]{2,1,0:T(8,128)(2,1)} %bitcast.20.p0, bf16[16,256,256]{2,1,0:T(8,128)(2,1)} %bitcast.21.p1, ...), custom_call_target="tpu_custom_call" | custom-call | flops 10000000000 | bytes 7340032 | tf_op jit(solution)/shard_map/pallas_call | solution.py:206
  121.3 14.8 %shard_map.72 = (bf16[4,288,512]{2,1,0:T(8,128)(2,1)S(1)}, bf16[4,288,512]{2,1,0:T(8,128)(2,1)S(1)}, bf16[4,512,256]{2,1,0:T(8,128)(2,1)}) custom-call(s32[8]{0:T(128)S(1)} %stack.104.plan, bf16[2048,4096]{1,0:T(8,128)(2,1)} %copy-done.19, f32[2048,1]{1,0:T(8,128)S(1)} %copy-done.22, bf16[256,2048]{1,0:T(8,128)(2,1)S(1)} %get-tuple-element.102.row_t, ...), custom_call_target="tpu_custom_call" | custom-call | flops 10737418240 | bytes 16777216 | tf_op jit(solution)/shard_map/pallas_call | solution.py:390
  139.5 3.7 %collective-permute-done.25.refs_3_ = bf16[1,128,512]{2,1,0:T(8,128)(2,1)S(1)} collective-permute-done((bf16[1,128,512]{2,1,0:T(8,128)(2,1)S(1)}, bf16[1,128,512]{2,1,0:T(8,128)(2,1)S(1)}, u32[]{:S(2)}, u32[]{:S(2)}) %collective-permute-start.25) | collective-permute-done | bytes 131104 | tf_op jit(solution)/shard_map/ppermute | solution.py:17
  144.0 5.2 %collective-permute-start.26 = (bf16[256,512]{1,0:T(8,128)(2,1)}, bf16[256,512]{1,0:T(8,128)(2,1)S(1)}, u32[]{:S(2)}, u32[]{:S(2)}) collective-permute-start(bf16[256,512]{1,0:T(8,128)(2,1)} %bitcast.22), channel_id=1, source_target_pairs={{0,0},{1,10},{2,17},{3,27},{4,4},{5,14},{6,21},{7,31},{8,1},{9,11}... | collective-permute-start | bytes 786440 | tf_op jit(solution)/shard_map/ppermute | solution.py:557
  150.2 2.4 collective-permute-start.28
  152.6 3.7 %all-to-all-start.1 = ((bf16[4,512,256]{2,1,0:T(8,128)(2,1)}), bf16[4,512,256]{2,1,0:T(8,128)(2,1)S(1)}, u32[]{:S(2)}, u32[]{:S(2)}) async-start(bf16[4,512,256]{2,1,0:T(8,128)(2,1)} %get-tuple-element.104), calls=%async_computation.1 | async-start | bytes 2097152 | tf_op jit(solution)/shard_map/all_to_all | solution.py:659
  156.3 10.4 %shard_map.75 = (bf16[256,2048]{1,0:T(8,128)(2,1)S(1)}, bf16[4096,256]{1,0:T(8,128)(2,1)S(1)}, f32[8,128]{1,0:T(8,128)S(1)}) custom-call(s32[16,128]{1,0:T(8,128)S(1)} %get-tuple-element.151.row_inv, s32[32,128]{1,0:T(8,128)S(1)} %get-tuple-element.149.col_inv, bf16[16,256,256]{2,1,0:T(8,128)(2,1)} %bitcast.25.p0, bf16[16,256,256]{2,1,0:T(8,128)(2,1)} %bitcast.26.p1, ...), custom_call_target="tpu_custom_call" | custom-call | flops 10000000000 | bytes 7340032 | tf_op jit(solution)/shard_map/pallas_call | solution.py:206
  169.2 14.8 %shard_map.77 = (bf16[4,288,512]{2,1,0:T(8,128)(2,1)}, bf16[4,288,512]{2,1,0:T(8,128)(2,1)S(1)}, bf16[4,512,256]{2,1,0:T(8,128)(2,1)S(1)}) custom-call(s32[8]{0:T(128)S(1)} %stack.104.plan, bf16[2048,4096]{1,0:T(8,128)(2,1)} %copy-done.19, f32[2048,1]{1,0:T(8,128)S(1)} %copy-done.23, bf16[256,2048]{1,0:T(8,128)(2,1)S(1)} %get-tuple-element.119.row_t, ...), custom_call_target="tpu_custom_call" | custom-call | flops 10737418240 | bytes 16777216 | tf_op jit(solution)/shard_map/pallas_call | solution.py:390
  186.0 4.8 %all-to-all-start.2 = ((bf16[4,512,256]{2,1,0:T(8,128)(2,1)}), bf16[4,512,256]{2,1,0:T(8,128)(2,1)S(1)}, u32[]{:S(2)}, u32[]{:S(2)}) async-start(bf16[4,512,256]{2,1,0:T(8,128)(2,1)} %copy-done.4), calls=%async_computation.2 | async-start | bytes 2097152 | tf_op jit(solution)/shard_map/all_to_all | solution.py:659
  197.8 5.9 %collective-permute-done.37.refs_3_ = bf16[2,128,512]{2,1,0:T(8,128)(2,1)S(1)} collective-permute-done((bf16[2,128,512]{2,1,0:T(8,128)(2,1)S(1)}, bf16[2,128,512]{2,1,0:T(8,128)(2,1)S(1)}, u32[]{:S(2)}, u32[]{:S(2)}) %collective-permute-start.37) | collective-permute-done | bytes 262176 | tf_op jit(solution)/shard_map/ppermute | solution.py:17
  213.3 6.2 %collective-permute-start.43 = (f32[2,1,32,256]{3,2,0,1:T(8,128)}, f32[2,1,32,256]{3,2,0,1:T(8,128)}, u32[]{:S(2)}, u32[]{:S(2)}) collective-permute-start(f32[2,1,32,256]{3,2,0,1:T(8,128)} %fusion.7), channel_id=1, source_target_pairs={{0,2},{1,3},{2,0},{3,1},{4,6},{5,7},{6,4},{7,5},{8,10},{9,11},{10,... | collective-permute-start | bytes 196616 | tf_op jit(solution)/shard_map/ppermute | solution.py:17
  219.4 3.4 %collective-permute-start.38 = (bf16[256,512]{1,0:T(8,128)(2,1)}, bf16[256,512]{1,0:T(8,128)(2,1)}, u32[]{:S(2)}, u32[]{:S(2)}) collective-permute-start(bf16[256,512]{1,0:T(8,128)(2,1)} %bitcast.98), channel_id=1, source_target_pairs={{0,0},{1,10},{2,17},{3,27},{4,4},{5,14},{6,21},{7,31},{8,1},{9,11}... | collective-permute-start | bytes 786440 | tf_op jit(solution)/shard_map/ppermute | solution.py:557
  223.9 2.3 collective-permute-start.47
  227.2 5.2 %collective-permute-start.41 = (bf16[256,512]{1,0:T(8,128)(2,1)S(1)}, bf16[256,512]{1,0:T(8,128)(2,1)S(1)}, u32[]{:S(2)}, u32[]{:S(2)}) collective-permute-start(bf16[256,512]{1,0:T(8,128)(2,1)S(1)} %bitcast.99), channel_id=1, source_target_pairs={{0,0},{1,10},{2,17},{3,27},{4,4},{5,14},{6,21},{7,31},{8,1},{9,11}... | collective-permute-start | bytes 786440 | tf_op jit(solution)/shard_map/ppermute | solution.py:557
  235.9 2.1 collective-permute-done.48
  243.2 3.0 %collective-permute-start.50 = (f32[1,4,32,256]{3,2,1,0:T(8,128)S(1)}, f32[1,4,32,256]{3,2,1,0:T(8,128)S(1)}, u32[]{:S(2)}, u32[]{:S(2)}) collective-permute-start(f32[1,4,32,256]{3,2,1,0:T(8,128)S(1)} %add.79), channel_id=1, source_target_pairs={{0,2},{1,3},{2,0},{3,1},{4,6},{5,7},{6,4},{7,5},{8,10},{9,11},{10,... | collective-permute-start | bytes 393224 | tf_op jit(solution)/shard_map/ppermute | solution.py:17
  246.9 2.6 %shard_map.82 = bf16[512,768]{1,0:T(8,128)(2,1)} custom-call(s32[3,512]{1,0:T(4,128)S(1)} %pad_add_fusion.member, bf16[4,512,256]{2,1,0:T(8,128)(2,1)S(1)} %all-to-all-done.refs_2_.refs_0_, bf16[256,512]{1,0:T(8,128)(2,1)S(1)} %copy-done.10, bf16[4,512,256]{2,1,0:T(8,128)(2,1)S(1)} %all-to-all-done.1.refs_2_, ...), custom_call_target="tpu_custom_call" | custom-call | flops 1572864 | bytes 3145728 | tf_op jit(solution)/shard_map/pallas_call | solution.py:585
  249.6 2.1 collective-permute-done.50
  (193 shorter events, 73.5 us)
Async XLA Ops:
  2.5 16.5 %collective-permute-start = (bf16[272,256]{1,0:T(8,128)(2,1)S(1)}, bf16[272,256]{1,0:T(8,128)(2,1)S(1)}, u32[]{:S(2)}, u32[]{:S(2)}) collective-permute-start(bf16[272,256]{1,0:T(8,128)(2,1)S(1)} %fusion.1.refs_0_), channel_id=1, source_target_pairs={{0,1},{1,0},{2,3},{3,2},{4,5},{5,4},{6,7},{7,6},{8,9},{9,8},{10,11... | collective-permute-start | bytes 417800 | tf_op jit(solution)/shard_map/ppermute | solution.py:17
  4.1 14.8 %collective-permute-start.1 = (bf16[272,256]{1,0:T(8,128)(2,1)S(1)}, bf16[272,256]{1,0:T(8,128)(2,1)S(1)}, u32[]{:S(2)}, u32[]{:S(2)}) collective-permute-start(bf16[272,256]{1,0:T(8,128)(2,1)S(1)} %fusion.1.refs_0_), channel_id=1, source_target_pairs={{0,2},{1,3},{2,0},{3,1},{4,6},{5,7},{6,4},{7,5},{8,10},{9,11},{10,... | collective-permute-start | bytes 417800 | tf_op jit(solution)/shard_map/ppermute | solution.py:17
  6.7 12.2 %collective-permute-start.2 = (bf16[272,256]{1,0:T(8,128)(2,1)S(1)}, bf16[272,256]{1,0:T(8,128)(2,1)S(1)}, u32[]{:S(2)}, u32[]{:S(2)}) collective-permute-start(bf16[272,256]{1,0:T(8,128)(2,1)S(1)} %fusion.1.refs_0_), channel_id=1, source_target_pairs={{0,3},{1,2},{2,1},{3,0},{4,7},{5,6},{6,5},{7,4},{8,11},{9,10},{10,... | collective-permute-start | bytes 417800 | tf_op jit(solution)/shard_map/ppermute | solution.py:17
  19.0 15.3 %collective-permute-start.3 = (bf16[544,256]{1,0:T(8,128)(2,1)S(1)}, bf16[544,256]{1,0:T(8,128)(2,1)S(1)}, u32[]{:S(2)}, u32[]{:S(2)}) collective-permute-start(bf16[544,256]{1,0:T(8,128)(2,1)S(1)} %get-tuple-element.70.refs_0_), channel_id=1, source_target_pairs={{0,8},{4,12},{8,0},{12,4},{16,24},{20,28},{24,16},{28,20},{1,9},{5... | collective-permute-start | bytes 835592 | tf_op jit(solution)/shard_map/ppermute | solution.py:17
  20.5 13.8 %collective-permute-start.4 = (bf16[544,256]{1,0:T(8,128)(2,1)S(1)}, bf16[544,256]{1,0:T(8,128)(2,1)S(1)}, u32[]{:S(2)}, u32[]{:S(2)}) collective-permute-start(bf16[544,256]{1,0:T(8,128)(2,1)S(1)} %get-tuple-element.71.refs_2_), channel_id=1, source_target_pairs={{0,16},{4,20},{8,24},{12,28},{16,0},{20,4},{24,8},{28,12},{1,17},{... | collective-permute-start | bytes 835592 | tf_op jit(solution)/shard_map/ppermute | solution.py:17
  22.0 12.3 %collective-permute-start.6 = (bf16[256,256]{1,0:T(8,128)(2,1)S(1)}, bf16[256,256]{1,0:T(8,128)(2,1)S(1)}, u32[]{:S(2)}, u32[]{:S(2)}) collective-permute-start(bf16[256,256]{1,0:T(8,128)(2,1)S(1)} %get-tuple-element.72.refs_4_), channel_id=1, source_target_pairs={{0,2},{1,3},{2,0},{3,1},{4,6},{5,7},{6,4},{7,5},{8,10},{9,11},{10,... | collective-permute-start | bytes 393224 | tf_op jit(solution)/shard_map/ppermute | solution.py:17
  34.4 19.3 %collective-permute-start.8 = (bf16[1088,256]{1,0:T(8,128)(2,1)S(1)}, bf16[1088,256]{1,0:T(8,128)(2,1)S(1)}, u32[]{:S(2)}, u32[]{:S(2)}) collective-permute-start(bf16[1088,256]{1,0:T(8,128)(2,1)S(1)} %get-tuple-element.73.refs_0_), channel_id=1, source_target_pairs={{0,16},{4,20},{8,24},{12,28},{16,0},{20,4},{24,8},{28,12},{1,17},{... | collective-permute-start | bytes 1671176 | tf_op jit(solution)/shard_map/ppermute | solution.py:17
  36.0 17.8 %collective-permute-start.9 = (bf16[1088,256]{1,0:T(8,128)(2,1)S(1)}, bf16[1088,256]{1,0:T(8,128)(2,1)S(1)}, u32[]{:S(2)}, u32[]{:S(2)}) collective-permute-start(bf16[1088,256]{1,0:T(8,128)(2,1)S(1)} %get-tuple-element.74.refs_2_), channel_id=1, source_target_pairs={{0,8},{4,12},{8,0},{12,4},{16,24},{20,28},{24,16},{28,20},{1,9},{5... | collective-permute-start | bytes 1671176 | tf_op jit(solution)/shard_map/ppermute | solution.py:17
  39.5 14.2 %collective-permute-start.10 = (bf16[512,256]{1,0:T(8,128)(2,1)S(1)}, bf16[512,256]{1,0:T(8,128)(2,1)S(1)}, u32[]{:S(2)}, u32[]{:S(2)}) collective-permute-start(bf16[512,256]{1,0:T(8,128)(2,1)S(1)} %get-tuple-element.75.refs_4_), channel_id=1, source_target_pairs={{0,8},{4,12},{8,0},{12,4},{16,24},{20,28},{24,16},{28,20},{1,9},{5... | collective-permute-start | bytes 786440 | tf_op jit(solution)/shard_map/ppermute | solution.py:17
  41.9 11.9 %collective-permute-start.11 = (bf16[512,256]{1,0:T(8,128)(2,1)S(1)}, bf16[512,256]{1,0:T(8,128)(2,1)S(1)}, u32[]{:S(2)}, u32[]{:S(2)}) collective-permute-start(bf16[512,256]{1,0:T(8,128)(2,1)S(1)} %get-tuple-element.76.refs_6_), channel_id=1, source_target_pairs={{0,16},{4,20},{8,24},{12,28},{16,0},{20,4},{24,8},{28,12},{1,17},{... | collective-permute-start | bytes 786440 | tf_op jit(solution)/shard_map/ppermute | solution.py:17
  55.0 20.1 %collective-permute-start.19 = (bf16[1024,256]{1,0:T(8,128)(2,1)S(1)}, bf16[1024,256]{1,0:T(8,128)(2,1)S(1)}, u32[]{:S(2)}, u32[]{:S(2)}) collective-permute-start(bf16[1024,256]{1,0:T(8,128)(2,1)S(1)} %get-tuple-element.91.refs_0_), channel_id=1, source_target_pairs={{0,16},{4,20},{8,24},{12,28},{16,0},{20,4},{24,8},{28,12},{1,17},{... | collective-permute-start | bytes 1572872 | tf_op jit(solution)/shard_map/ppermute | solution.py:17
  55.5 19.6 %collective-permute-start.20 = (bf16[1024,256]{1,0:T(8,128)(2,1)S(1)}, bf16[1024,256]{1,0:T(8,128)(2,1)S(1)}, u32[]{:S(2)}, u32[]{:S(2)}) collective-permute-start(bf16[1024,256]{1,0:T(8,128)(2,1)S(1)} %get-tuple-element.92.refs_2_), channel_id=1, source_target_pairs={{0,8},{4,12},{8,0},{12,4},{16,24},{20,28},{24,16},{28,20},{1,9},{5... | collective-permute-start | bytes 1572872 | tf_op jit(solution)/shard_map/ppermute | solution.py:17
  57.0 18.1 %collective-permute-start.21 = (bf16[512,256]{1,0:T(8,128)(2,1)S(1)}, bf16[512,256]{1,0:T(8,128)(2,1)S(1)}, u32[]{:S(2)}, u32[]{:S(2)}) collective-permute-start(bf16[512,256]{1,0:T(8,128)(2,1)S(1)} %get-tuple-element.93.refs_4_), channel_id=1, source_target_pairs={{0,8},{4,12},{8,0},{12,4},{16,24},{20,28},{24,16},{28,20},{1,9},{5... | collective-permute-start | bytes 786440 | tf_op jit(solution)/shard_map/ppermute | solution.py:17
  57.5 17.6 %collective-permute-start.22 = (bf16[512,256]{1,0:T(8,128)(2,1)}, bf16[512,256]{1,0:T(8,128)(2,1)S(1)}, u32[]{:S(2)}, u32[]{:S(2)}) collective-permute-start(bf16[512,256]{1,0:T(8,128)(2,1)} %copy-done.11), channel_id=1, source_target_pairs={{0,16},{4,20},{8,24},{12,28},{16,0},{20,4},{24,8},{28,12},{1,17},{... | collective-permute-start | bytes 786440 | tf_op jit(solution)/shard_map/ppermute | solution.py:17
  76.7 32.6 %collective-permute-start.23 = (bf16[4096,256]{1,0:T(8,128)(2,1)}, bf16[4096,256]{1,0:T(8,128)(2,1)}, u32[]{:S(2)}, u32[]{:S(2)}) collective-permute-start(bf16[4096,256]{1,0:T(8,128)(2,1)} %get-tuple-element.95), channel_id=1, source_target_pairs={{0,4},{4,0},{8,12},{12,8},{16,20},{20,16},{24,28},{28,24},{1,5},{5... | collective-permute-start | bytes 6291464 | tf_op jit(solution)/shard_map/ppermute | solution.py:17
  91.8 14.7 %collective-permute-start.16 = (bf16[4,288,512]{2,1,0:T(8,128)(2,1)}, bf16[4,288,512]{2,1,0:T(8,128)(2,1)}, u32[]{:S(2)}, u32[]{:S(2)}) collective-permute-start(bf16[4,288,512]{2,1,0:T(8,128)(2,1)} %get-tuple-element.86), channel_id=1, source_target_pairs={{0,4},{4,0},{8,12},{12,8},{16,20},{20,16},{24,28},{28,24},{1,5},{5... | collective-permute-start | bytes 3538952 | tf_op jit(solution)/shard_map/ppermute | solution.py:17
  92.4 60.2 %all-to-all-start = ((bf16[4,512,256]{2,1,0:T(8,128)(2,1)}), bf16[4,512,256]{2,1,0:T(8,128)(2,1)S(1)}, u32[]{:S(2)}, u32[]{:S(2)}) async-start(bf16[4,512,256]{2,1,0:T(8,128)(2,1)} %get-tuple-element.84), calls=%async_computation | async-start | bytes 2097152 | tf_op jit(solution)/shard_map/all_to_all | solution.py:659
  97.4 22.2 %collective-permute-start.30 = (bf16[1024,256]{1,0:T(8,128)(2,1)S(1)}, bf16[1024,256]{1,0:T(8,128)(2,1)S(1)}, u32[]{:S(2)}, u32[]{:S(2)}) collective-permute-start(bf16[1024,256]{1,0:T(8,128)(2,1)S(1)} %get-tuple-element.111.refs_0_), channel_id=1, source_target_pairs={{0,16},{4,20},{8,24},{12,28},{16,0},{20,4},{24,8},{28,12},{1,17},{... | collective-permute-start | bytes 1572872 | tf_op jit(solution)/shard_map/ppermute | solution.py:17
  99.0 20.7 %collective-permute-start.31 = (bf16[1024,256]{1,0:T(8,128)(2,1)S(1)}, bf16[1024,256]{1,0:T(8,128)(2,1)S(1)}, u32[]{:S(2)}, u32[]{:S(2)}) collective-permute-start(bf16[1024,256]{1,0:T(8,128)(2,1)S(1)} %get-tuple-element.112.refs_2_), channel_id=1, source_target_pairs={{0,8},{4,12},{8,0},{12,4},{16,24},{20,28},{24,16},{28,20},{1,9},{5... | collective-permute-start | bytes 1572872 | tf_op jit(solution)/shard_map/ppermute | solution.py:17
  108.1 13.0 %collective-permute-start.17 = (bf16[2,160,512]{2,1,0:T(8,128)(2,1)S(1)}, bf16[2,160,512]{2,1,0:T(8,128)(2,1)S(1)}, u32[]{:S(2)}, u32[]{:S(2)}) collective-permute-start(bf16[2,160,512]{2,1,0:T(8,128)(2,1)S(1)} %get-tuple-element.88), channel_id=1, source_target_pairs={{0,8},{4,12},{8,0},{12,4},{16,24},{20,28},{24,16},{28,20},{1,9},{5... | collective-permute-start | bytes 983048 | tf_op jit(solution)/shard_map/ppermute | solution.py:17
  108.8 12.3 %collective-permute-start.18 = (bf16[2,128,512]{2,1,0:T(8,128)(2,1)S(1)}, bf16[2,128,512]{2,1,0:T(8,128)(2,1)S(1)}, u32[]{:S(2)}, u32[]{:S(2)}) collective-permute-start(bf16[2,128,512]{2,1,0:T(8,128)(2,1)S(1)} %get-tuple-element.90), channel_id=1, source_target_pairs={{0,16},{4,20},{8,24},{12,28},{16,0},{20,4},{24,8},{28,12},{1,17},{... | collective-permute-start | bytes 786440 | tf_op jit(solution)/shard_map/ppermute | solution.py:17
  121.1 35.2 %collective-permute-start.32 = (bf16[4096,256]{1,0:T(8,128)(2,1)}, bf16[4096,256]{1,0:T(8,128)(2,1)}, u32[]{:S(2)}, u32[]{:S(2)}) collective-permute-start(bf16[4096,256]{1,0:T(8,128)(2,1)} %shard_map.74), channel_id=1, source_target_pairs={{0,4},{4,0},{8,12},{12,8},{16,20},{20,16},{24,28},{28,24},{1,5},{5... | collective-permute-start | bytes 6291464 | tf_op jit(solution)/shard_map/ppermute | solution.py:17
  136.1 13.2 %collective-permute-start.27 = (bf16[4,288,512]{2,1,0:T(8,128)(2,1)S(1)}, bf16[4,288,512]{2,1,0:T(8,128)(2,1)S(1)}, u32[]{:S(2)}, u32[]{:S(2)}) collective-permute-start(bf16[4,288,512]{2,1,0:T(8,128)(2,1)S(1)} %get-tuple-element.106), channel_id=1, source_target_pairs={{0,4},{4,0},{8,12},{12,8},{16,20},{20,16},{24,28},{28,24},{1,5},{5... | collective-permute-start | bytes 3538952 | tf_op jit(solution)/shard_map/ppermute | solution.py:17
  144.0 25.1 %collective-permute-start.26 = (bf16[256,512]{1,0:T(8,128)(2,1)}, bf16[256,512]{1,0:T(8,128)(2,1)S(1)}, u32[]{:S(2)}, u32[]{:S(2)}) collective-permute-start(bf16[256,512]{1,0:T(8,128)(2,1)} %bitcast.22), channel_id=1, source_target_pairs={{0,0},{1,10},{2,17},{3,27},{4,4},{5,14},{6,21},{7,31},{8,1},{9,11}... | collective-permute-start | bytes 786440 | tf_op jit(solution)/shard_map/ppermute | solution.py:557
  150.2 16.6 %collective-permute-start.28 = (bf16[2,160,512]{2,1,0:T(8,128)(2,1)}, bf16[2,160,512]{2,1,0:T(8,128)(2,1)S(1)}, u32[]{:S(2)}, u32[]{:S(2)}) collective-permute-start(bf16[2,160,512]{2,1,0:T(8,128)(2,1)} %get-tuple-element.108), channel_id=1, source_target_pairs={{0,8},{4,12},{8,0},{12,4},{16,24},{20,28},{24,16},{28,20},{1,9},{5... | collective-permute-start | bytes 983048 | tf_op jit(solution)/shard_map/ppermute | solution.py:17
  152.6 14.2 %collective-permute-start.29 = (bf16[2,128,512]{2,1,0:T(8,128)(2,1)}, bf16[2,128,512]{2,1,0:T(8,128)(2,1)}, u32[]{:S(2)}, u32[]{:S(2)}) collective-permute-start(bf16[2,128,512]{2,1,0:T(8,128)(2,1)} %get-tuple-element.110), channel_id=1, source_target_pairs={{0,16},{4,20},{8,24},{12,28},{16,0},{20,4},{24,8},{28,12},{1,17},{... | collective-permute-start | bytes 786440 | tf_op jit(solution)/shard_map/ppermute | solution.py:17
  152.6 33.4 %all-to-all-start.1 = ((bf16[4,512,256]{2,1,0:T(8,128)(2,1)}), bf16[4,512,256]{2,1,0:T(8,128)(2,1)S(1)}, u32[]{:S(2)}, u32[]{:S(2)}) async-start(bf16[4,512,256]{2,1,0:T(8,128)(2,1)} %get-tuple-element.104), calls=%async_computation.1 | async-start | bytes 2097152 | tf_op jit(solution)/shard_map/all_to_all | solution.py:659
  186.0 36.8 %all-to-all-start.2 = ((bf16[4,512,256]{2,1,0:T(8,128)(2,1)}), bf16[4,512,256]{2,1,0:T(8,128)(2,1)S(1)}, u32[]{:S(2)}, u32[]{:S(2)}) async-start(bf16[4,512,256]{2,1,0:T(8,128)(2,1)} %copy-done.4), calls=%async_computation.2 | async-start | bytes 2097152 | tf_op jit(solution)/shard_map/all_to_all | solution.py:659
  208.9 13.9 %collective-permute-start.39 = (bf16[1,160,512]{2,1,0:T(8,128)(2,1)}, bf16[1,160,512]{2,1,0:T(8,128)(2,1)}, u32[]{:S(2)}, u32[]{:S(2)}) collective-permute-start(bf16[1,160,512]{2,1,0:T(8,128)(2,1)} %get-tuple-element.131), channel_id=1, source_target_pairs={{0,16},{4,20},{8,24},{12,28},{16,0},{20,4},{24,8},{28,12},{1,17},{... | collective-permute-start | bytes 491528 | tf_op jit(solution)/shard_map/ppermute | solution.py:17
  213.3 12.9 %collective-permute-start.43 = (f32[2,1,32,256]{3,2,0,1:T(8,128)}, f32[2,1,32,256]{3,2,0,1:T(8,128)}, u32[]{:S(2)}, u32[]{:S(2)}) collective-permute-start(f32[2,1,32,256]{3,2,0,1:T(8,128)} %fusion.7), channel_id=1, source_target_pairs={{0,2},{1,3},{2,0},{3,1},{4,6},{5,7},{6,4},{7,5},{8,10},{9,11},{10,... | collective-permute-start | bytes 196616 | tf_op jit(solution)/shard_map/ppermute | solution.py:17
  219.4 27.5 %collective-permute-start.38 = (bf16[256,512]{1,0:T(8,128)(2,1)}, bf16[256,512]{1,0:T(8,128)(2,1)}, u32[]{:S(2)}, u32[]{:S(2)}) collective-permute-start(bf16[256,512]{1,0:T(8,128)(2,1)} %bitcast.98), channel_id=1, source_target_pairs={{0,0},{1,10},{2,17},{3,27},{4,4},{5,14},{6,21},{7,31},{8,1},{9,11}... | collective-permute-start | bytes 786440 | tf_op jit(solution)/shard_map/ppermute | solution.py:557
  227.2 19.7 %collective-permute-start.41 = (bf16[256,512]{1,0:T(8,128)(2,1)S(1)}, bf16[256,512]{1,0:T(8,128)(2,1)S(1)}, u32[]{:S(2)}, u32[]{:S(2)}) collective-permute-start(bf16[256,512]{1,0:T(8,128)(2,1)S(1)} %bitcast.99), channel_id=1, source_target_pairs={{0,0},{1,10},{2,17},{3,27},{4,4},{5,14},{6,21},{7,31},{8,1},{9,11}... | collective-permute-start | bytes 786440 | tf_op jit(solution)/shard_map/ppermute | solution.py:557
  (50 other events, 379.3 us)

commit v5 on v4

--- a/solution.py
+++ b/solution.py
@@ -214,7 +214,7 @@
         ],
         scratch_shapes=[
             pltpu.VMEM((parts * (listed + 8), LANES), F32),
-            pltpu.VMEM((parts * max(rows, cols), LANES), F32),
+            pltpu.VMEM((parts * (max(rows, cols) + 8), LANES), F32),
         ],
         compiler_params=pltpu.CompilerParams(vmem_limit_bytes=28 * 2**20),
         cost_estimate=pl.CostEstimate(

time: 257 us -> 257 us (level)
  no operation moved by 1% of the time
where the time goes in v5:
time: 257 us; the launch traced here: 254 us
  Pallas kernels  104 us (40%)
  starting transfers between devices  87.3 us (34%)
  waiting for transfers between devices  41.4 us (16%)
  local copies, waits for them, and re-layouts  16.8 us (7%)
  other arithmetic  3.5 us (1%)
    ppermute x49, starting transfers between devices, swap(): return lax.ppermute(x, axis, [(i, i ^ bit) for i in range(count)])  59.9 us
    pallas_call x3, Pallas kernels, terms(): pl.pallas_call(terms_kernel, grid_spec=grid_spec, out_shape=[jax.ShapeDty...  44.8 us
    ppermute x49, waiting for transfers between devices, swap(): return lax.ppermute(x, axis, [(i, i ^ bit) for i in range(count)])  41.4 us
    pallas_call x3, Pallas kernels, tables(): pl.pallas_call(functools.partial(tables_kernel, chunk), in_specs=[smem, s...  30.6 us
    unnamed x56, local copies, waits for them, and re-layouts  14.8 us
    ppermute x3, starting transfers between devices, to_owner(): return lax.ppermute(x, ('row', 'col'), pairs)  13.7 us
    all_to_all x3, starting transfers between devices, per_device(): direct.append(lax.all_to_all(parts, 'col', 0, 0, tiled=True))  13.7 us
    pallas_call x9, Pallas kernels, sums(): pl.pallas_call(functools.partial(sums_kernel, width, [len(group) for grou...  8.64 us
  transfers between devices with their start and end apart: 55, of which 18 were waited for; matrix products, arithmetic and copies ran while one was open for 1% of the time, Pallas kernels for 40%

profile of v5, /device:TPU:4, one launch (start us, length us, event | category | flops | bytes accessed | tf_op | source)
XLA Modules:
  0.0 254.2 jit_solution(17078848855657190953)
XLA Ops:
  4.1 2.6 %collective-permute-start.1 = (bf16[272,256]{1,0:T(8,128)(2,1)S(1)}, bf16[272,256]{1,0:T(8,128)(2,1)S(1)}, u32[]{:S(2)}, u32[]{:S(2)}) collective-permute-start(bf16[272,256]{1,0:T(8,128)(2,1)S(1)} %fusion.1.refs_0_), channel_id=1, source_target_pairs={{0,2},{1,3},{2,0},{3,1},{4,6},{5,7},{6,4},{7,5},{8,10},{9,11},{10,... | collective-permute-start | bytes 417800 | tf_op jit(solution)/shard_map/ppermute | solution.py:17
  6.9 6.1 %shard_map.59 = (bf16[2048,4096]{1,0:T(8,128)(2,1)S(1)}, f32[2048,1]{1,0:T(8,128)S(1)}, f32[8,128]{1,0:T(8,128)S(1)}) custom-call(bf16[2048,4096]{1,0:T(8,128)(2,1)} %ancestor.1), custom_call_target="tpu_custom_call" | custom-call | flops 8388608 | bytes 33554432 | tf_op jit(solution)/shard_map/pallas_call | solution.py:276
  13.1 5.8 %copy-done.19 = bf16[2048,4096]{1,0:T(8,128)(2,1)} copy-done((bf16[2048,4096]{1,0:T(8,128)(2,1)}, bf16[2048,4096]{1,0:T(8,128)(2,1)S(1)}, u32[]{:S(2)}) %copy-start.19) | copy-done | bytes 16777240
  22.0 3.4 %collective-permute-start.6 = (bf16[256,256]{1,0:T(8,128)(2,1)S(1)}, bf16[256,256]{1,0:T(8,128)(2,1)S(1)}, u32[]{:S(2)}, u32[]{:S(2)}) collective-permute-start(bf16[256,256]{1,0:T(8,128)(2,1)S(1)} %get-tuple-element.72.refs_4_), channel_id=1, source_target_pairs={{0,2},{1,3},{2,0},{3,1},{4,6},{5,7},{6,4},{7,5},{8,10},{9,11},{10,... | collective-permute-start | bytes 393224 | tf_op jit(solution)/shard_map/ppermute | solution.py:17
  27.3 7.0 %collective-permute-done.6.refs_6_ = bf16[256,256]{1,0:T(8,128)(2,1)S(1)} collective-permute-done((bf16[256,256]{1,0:T(8,128)(2,1)S(1)}, bf16[256,256]{1,0:T(8,128)(2,1)S(1)}, u32[]{:S(2)}, u32[]{:S(2)}) %collective-permute-start.6) | collective-permute-done | bytes 131104 | tf_op jit(solution)/shard_map/ppermute | solution.py:17
  42.3 3.8 %collective-permute-done.13.refs_10_ = bf16[256,256]{1,0:T(8,128)(2,1)S(1)} collective-permute-done((bf16[256,256]{1,0:T(8,128)(2,1)S(1)}, bf16[256,256]{1,0:T(8,128)(2,1)S(1)}, u32[]{:S(2)}, u32[]{:S(2)}) %collective-permute-start.13) | collective-permute-done | bytes 131104 | tf_op jit(solution)/shard_map/ppermute | solution.py:17
  46.2 4.7 %collective-permute-start.14 = (bf16[256,256]{1,0:T(8,128)(2,1)S(1)}, bf16[256,256]{1,0:T(8,128)(2,1)S(1)}, u32[]{:S(2)}, u32[]{:S(2)}) collective-permute-start(bf16[256,256]{1,0:T(8,128)(2,1)S(1)} %get-tuple-element.77.refs_8_), channel_id=1, source_target_pairs={{0,3},{1,2},{2,1},{3,0},{4,7},{5,6},{6,5},{7,4},{8,11},{9,10},{10,... | collective-permute-start | bytes 393224 | tf_op jit(solution)/shard_map/ppermute | solution.py:17
  50.8 2.9 %collective-permute-done.14.refs_11_ = bf16[256,256]{1,0:T(8,128)(2,1)S(1)} collective-permute-done((bf16[256,256]{1,0:T(8,128)(2,1)S(1)}, bf16[256,256]{1,0:T(8,128)(2,1)S(1)}, u32[]{:S(2)}, u32[]{:S(2)}) %collective-permute-start.14) | collective-permute-done | bytes 131104 | tf_op jit(solution)/shard_map/ppermute | solution.py:17
  59.3 3.1 %shard_map.63 = s32[1,128,128]{2,1,0:T(8,128)S(1)} custom-call(bf16[16,272,256]{2,1,0:T(8,128)(2,1)S(1)} %bitcast.94, bf16[16,272,256]{2,1,0:T(8,128)(2,1)} %bitcast.6.p1), custom_call_target="tpu_custom_call" | custom-call | flops 1000000000 | bytes 65536 | tf_op jit(solution)/shard_map/pallas_call | solution.py:130
  63.1 9.9 %shard_map.64 = (bf16[256,2048]{1,0:T(8,128)(2,1)S(1)}, bf16[4096,256]{1,0:T(8,128)(2,1)S(1)}, f32[8,128]{1,0:T(8,128)S(1)}) custom-call(s32[16,128]{1,0:T(8,128)S(1)} %dynamic-slice_bitcast_fusion.5.row_inv, s32[32,128]{1,0:T(8,128)S(1)} %dynamic-slice_bitcast_fusion.2.col_inv, bf16[16,272,256]{2,1,0:T(8,128)(2,1)S(1)} %bitcast.95, ...), custom_call_target="tpu_custom_call" | custom-call | flops 10000000000 | bytes 7340032 | tf_op jit(solution)/shard_map/pallas_call | solution.py:206
  73.0 2.1 collective-permute-done.21.refs_5_
  76.7 15.2 %shard_map.66 = (bf16[4,288,512]{2,1,0:T(8,128)(2,1)}, bf16[4,288,512]{2,1,0:T(8,128)(2,1)S(1)}, bf16[4,512,256]{2,1,0:T(8,128)(2,1)}) custom-call(s32[8]{0:T(128)S(1)} %stack.104.plan, bf16[2048,4096]{1,0:T(8,128)(2,1)} %copy-done.19, f32[2048,1]{1,0:T(8,128)S(1)} %copy-done.21, bf16[256,2048]{1,0:T(8,128)(2,1)S(1)} %get-tuple-element.82.row_t, ...), custom_call_target="tpu_custom_call" | custom-call | flops 10737418240 | bytes 16777216 | tf_op jit(solution)/shard_map/pallas_call | solution.py:390
  92.4 5.1 %all-to-all-start = ((bf16[4,512,256]{2,1,0:T(8,128)(2,1)}), bf16[4,512,256]{2,1,0:T(8,128)(2,1)S(1)}, u32[]{:S(2)}, u32[]{:S(2)}) async-start(bf16[4,512,256]{2,1,0:T(8,128)(2,1)} %get-tuple-element.84), calls=%async_computation | async-start | bytes 2097152 | tf_op jit(solution)/shard_map/all_to_all | solution.py:659
  102.0 4.5 %shard_map.65 = s32[2,128,128]{2,1,0:T(8,128)S(1)} custom-call(bf16[16,272,256]{2,1,0:T(8,128)(2,1)S(1)} %bitcast.96, bf16[16,272,256]{2,1,0:T(8,128)(2,1)} %bitcast.6.p1, f32[8,128]{1,0:T(8,128)S(1)} %get-tuple-element.79.refs_0_.refs_8_), custom_call_target="tpu_custom_call" | custom-call | flops 2000000000 | bytes 131072 | tf_op jit(solution)/shard_map/pallas_call | solution.py:130
  109.3 10.3 %shard_map.69 = (bf16[256,2048]{1,0:T(8,128)(2,1)S(1)}, bf16[4096,256]{1,0:T(8,128)(2,1)S(1)}, f32[8,128]{1,0:T(8,128)S(1)}) custom-call(s32[16,128]{1,0:T(8,128)S(1)} %get-tuple-element.152.row_inv, s32[32,128]{1,0:T(8,128)S(1)} %get-tuple-element.150.col_inv, bf16[16,256,256]{2,1,0:T(8,128)(2,1)} %bitcast.20.p0, bf16[16,256,256]{2,1,0:T(8,128)(2,1)} %bitcast.21.p1, ...), custom_call_target="tpu_custom_call" | custom-call | flops 10000000000 | bytes 7340032 | tf_op jit(solution)/shard_map/pallas_call | solution.py:206
  121.3 14.8 %shard_map.72 = (bf16[4,288,512]{2,1,0:T(8,128)(2,1)S(1)}, bf16[4,288,512]{2,1,0:T(8,128)(2,1)S(1)}, bf16[4,512,256]{2,1,0:T(8,128)(2,1)}) custom-call(s32[8]{0:T(128)S(1)} %stack.104.plan, bf16[2048,4096]{1,0:T(8,128)(2,1)} %copy-done.19, f32[2048,1]{1,0:T(8,128)S(1)} %copy-done.22, bf16[256,2048]{1,0:T(8,128)(2,1)S(1)} %get-tuple-element.102.row_t, ...), custom_call_target="tpu_custom_call" | custom-call | flops 10737418240 | bytes 16777216 | tf_op jit(solution)/shard_map/pallas_call | solution.py:390
  139.5 3.7 %collective-permute-done.25.refs_3_ = bf16[1,128,512]{2,1,0:T(8,128)(2,1)S(1)} collective-permute-done((bf16[1,128,512]{2,1,0:T(8,128)(2,1)S(1)}, bf16[1,128,512]{2,1,0:T(8,128)(2,1)S(1)}, u32[]{:S(2)}, u32[]{:S(2)}) %collective-permute-start.25) | collective-permute-done | bytes 131104 | tf_op jit(solution)/shard_map/ppermute | solution.py:17
  144.0 5.2 %collective-permute-start.26 = (bf16[256,512]{1,0:T(8,128)(2,1)}, bf16[256,512]{1,0:T(8,128)(2,1)S(1)}, u32[]{:S(2)}, u32[]{:S(2)}) collective-permute-start(bf16[256,512]{1,0:T(8,128)(2,1)} %bitcast.22), channel_id=1, source_target_pairs={{0,0},{1,10},{2,17},{3,27},{4,4},{5,14},{6,21},{7,31},{8,1},{9,11}... | collective-permute-start | bytes 786440 | tf_op jit(solution)/shard_map/ppermute | solution.py:557
  150.2 2.4 collective-permute-start.28
  152.6 3.7 %all-to-all-start.1 = ((bf16[4,512,256]{2,1,0:T(8,128)(2,1)}), bf16[4,512,256]{2,1,0:T(8,128)(2,1)S(1)}, u32[]{:S(2)}, u32[]{:S(2)}) async-start(bf16[4,512,256]{2,1,0:T(8,128)(2,1)} %get-tuple-element.104), calls=%async_computation.1 | async-start | bytes 2097152 | tf_op jit(solution)/shard_map/all_to_all | solution.py:659
  156.3 10.4 %shard_map.75 = (bf16[256,2048]{1,0:T(8,128)(2,1)S(1)}, bf16[4096,256]{1,0:T(8,128)(2,1)S(1)}, f32[8,128]{1,0:T(8,128)S(1)}) custom-call(s32[16,128]{1,0:T(8,128)S(1)} %get-tuple-element.151.row_inv, s32[32,128]{1,0:T(8,128)S(1)} %get-tuple-element.149.col_inv, bf16[16,256,256]{2,1,0:T(8,128)(2,1)} %bitcast.25.p0, bf16[16,256,256]{2,1,0:T(8,128)(2,1)} %bitcast.26.p1, ...), custom_call_target="tpu_custom_call" | custom-call | flops 10000000000 | bytes 7340032 | tf_op jit(solution)/shard_map/pallas_call | solution.py:206
  169.2 14.8 %shard_map.77 = (bf16[4,288,512]{2,1,0:T(8,128)(2,1)}, bf16[4,288,512]{2,1,0:T(8,128)(2,1)S(1)}, bf16[4,512,256]{2,1,0:T(8,128)(2,1)S(1)}) custom-call(s32[8]{0:T(128)S(1)} %stack.104.plan, bf16[2048,4096]{1,0:T(8,128)(2,1)} %copy-done.19, f32[2048,1]{1,0:T(8,128)S(1)} %copy-done.23, bf16[256,2048]{1,0:T(8,128)(2,1)S(1)} %get-tuple-element.119.row_t, ...), custom_call_target="tpu_custom_call" | custom-call | flops 10737418240 | bytes 16777216 | tf_op jit(solution)/shard_map/pallas_call | solution.py:390
  186.0 4.8 %all-to-all-start.2 = ((bf16[4,512,256]{2,1,0:T(8,128)(2,1)}), bf16[4,512,256]{2,1,0:T(8,128)(2,1)S(1)}, u32[]{:S(2)}, u32[]{:S(2)}) async-start(bf16[4,512,256]{2,1,0:T(8,128)(2,1)} %copy-done.4), calls=%async_computation.2 | async-start | bytes 2097152 | tf_op jit(solution)/shard_map/all_to_all | solution.py:659
  197.8 5.9 %collective-permute-done.37.refs_3_ = bf16[2,128,512]{2,1,0:T(8,128)(2,1)S(1)} collective-permute-done((bf16[2,128,512]{2,1,0:T(8,128)(2,1)S(1)}, bf16[2,128,512]{2,1,0:T(8,128)(2,1)S(1)}, u32[]{:S(2)}, u32[]{:S(2)}) %collective-permute-start.37) | collective-permute-done | bytes 262176 | tf_op jit(solution)/shard_map/ppermute | solution.py:17
  213.3 6.2 %collective-permute-start.43 = (f32[2,1,32,256]{3,2,0,1:T(8,128)}, f32[2,1,32,256]{3,2,0,1:T(8,128)}, u32[]{:S(2)}, u32[]{:S(2)}) collective-permute-start(f32[2,1,32,256]{3,2,0,1:T(8,128)} %fusion.7), channel_id=1, source_target_pairs={{0,2},{1,3},{2,0},{3,1},{4,6},{5,7},{6,4},{7,5},{8,10},{9,11},{10,... | collective-permute-start | bytes 196616 | tf_op jit(solution)/shard_map/ppermute | solution.py:17
  219.4 3.4 %collective-permute-start.38 = (bf16[256,512]{1,0:T(8,128)(2,1)}, bf16[256,512]{1,0:T(8,128)(2,1)}, u32[]{:S(2)}, u32[]{:S(2)}) collective-permute-start(bf16[256,512]{1,0:T(8,128)(2,1)} %bitcast.98), channel_id=1, source_target_pairs={{0,0},{1,10},{2,17},{3,27},{4,4},{5,14},{6,21},{7,31},{8,1},{9,11}... | collective-permute-start | bytes 786440 | tf_op jit(solution)/shard_map/ppermute | solution.py:557
  223.9 2.3 collective-permute-start.47
  227.2 5.2 %collective-permute-start.41 = (bf16[256,512]{1,0:T(8,128)(2,1)S(1)}, bf16[256,512]{1,0:T(8,128)(2,1)S(1)}, u32[]{:S(2)}, u32[]{:S(2)}) collective-permute-start(bf16[256,512]{1,0:T(8,128)(2,1)S(1)} %bitcast.99), channel_id=1, source_target_pairs={{0,0},{1,10},{2,17},{3,27},{4,4},{5,14},{6,21},{7,31},{8,1},{9,11}... | collective-permute-start | bytes 786440 | tf_op jit(solution)/shard_map/ppermute | solution.py:557
  235.9 2.1 collective-permute-done.48
  243.2 3.0 %collective-permute-start.50 = (f32[1,4,32,256]{3,2,1,0:T(8,128)S(1)}, f32[1,4,32,256]{3,2,1,0:T(8,128)S(1)}, u32[]{:S(2)}, u32[]{:S(2)}) collective-permute-start(f32[1,4,32,256]{3,2,1,0:T(8,128)S(1)} %add.79), channel_id=1, source_target_pairs={{0,2},{1,3},{2,0},{3,1},{4,6},{5,7},{6,4},{7,5},{8,10},{9,11},{10,... | collective-permute-start | bytes 393224 | tf_op jit(solution)/shard_map/ppermute | solution.py:17
  246.9 2.6 %shard_map.82 = bf16[512,768]{1,0:T(8,128)(2,1)} custom-call(s32[3,512]{1,0:T(4,128)S(1)} %pad_add_fusion.member, bf16[4,512,256]{2,1,0:T(8,128)(2,1)S(1)} %all-to-all-done.refs_2_.refs_0_, bf16[256,512]{1,0:T(8,128)(2,1)S(1)} %copy-done.10, bf16[4,512,256]{2,1,0:T(8,128)(2,1)S(1)} %all-to-all-done.1.refs_2_, ...), custom_call_target="tpu_custom_call" | custom-call | flops 1572864 | bytes 3145728 | tf_op jit(solution)/shard_map/pallas_call | solution.py:585
  249.6 2.1 collective-permute-done.50
  (193 shorter events, 73.5 us)
Async XLA Ops:
  2.5 16.5 %collective-permute-start = (bf16[272,256]{1,0:T(8,128)(2,1)S(1)}, bf16[272,256]{1,0:T(8,128)(2,1)S(1)}, u32[]{:S(2)}, u32[]{:S(2)}) collective-permute-start(bf16[272,256]{1,0:T(8,128)(2,1)S(1)} %fusion.1.refs_0_), channel_id=1, source_target_pairs={{0,1},{1,0},{2,3},{3,2},{4,5},{5,4},{6,7},{7,6},{8,9},{9,8},{10,11... | collective-permute-start | bytes 417800 | tf_op jit(solution)/shard_map/ppermute | solution.py:17
  4.1 14.8 %collective-permute-start.1 = (bf16[272,256]{1,0:T(8,128)(2,1)S(1)}, bf16[272,256]{1,0:T(8,128)(2,1)S(1)}, u32[]{:S(2)}, u32[]{:S(2)}) collective-permute-start(bf16[272,256]{1,0:T(8,128)(2,1)S(1)} %fusion.1.refs_0_), channel_id=1, source_target_pairs={{0,2},{1,3},{2,0},{3,1},{4,6},{5,7},{6,4},{7,5},{8,10},{9,11},{10,... | collective-permute-start | bytes 417800 | tf_op jit(solution)/shard_map/ppermute | solution.py:17
  6.7 12.2 %collective-permute-start.2 = (bf16[272,256]{1,0:T(8,128)(2,1)S(1)}, bf16[272,256]{1,0:T(8,128)(2,1)S(1)}, u32[]{:S(2)}, u32[]{:S(2)}) collective-permute-start(bf16[272,256]{1,0:T(8,128)(2,1)S(1)} %fusion.1.refs_0_), channel_id=1, source_target_pairs={{0,3},{1,2},{2,1},{3,0},{4,7},{5,6},{6,5},{7,4},{8,11},{9,10},{10,... | collective-permute-start | bytes 417800 | tf_op jit(solution)/shard_map/ppermute | solution.py:17
  19.0 15.3 %collective-permute-start.3 = (bf16[544,256]{1,0:T(8,128)(2,1)S(1)}, bf16[544,256]{1,0:T(8,128)(2,1)S(1)}, u32[]{:S(2)}, u32[]{:S(2)}) collective-permute-start(bf16[544,256]{1,0:T(8,128)(2,1)S(1)} %get-tuple-element.70.refs_0_), channel_id=1, source_target_pairs={{0,8},{4,12},{8,0},{12,4},{16,24},{20,28},{24,16},{28,20},{1,9},{5... | collective-permute-start | bytes 835592 | tf_op jit(solution)/shard_map/ppermute | solution.py:17
  20.5 13.8 %collective-permute-start.4 = (bf16[544,256]{1,0:T(8,128)(2,1)S(1)}, bf16[544,256]{1,0:T(8,128)(2,1)S(1)}, u32[]{:S(2)}, u32[]{:S(2)}) collective-permute-start(bf16[544,256]{1,0:T(8,128)(2,1)S(1)} %get-tuple-element.71.refs_2_), channel_id=1, source_target_pairs={{0,16},{4,20},{8,24},{12,28},{16,0},{20,4},{24,8},{28,12},{1,17},{... | collective-permute-start | bytes 835592 | tf_op jit(solution)/shard_map/ppermute | solution.py:17
  22.0 12.3 %collective-permute-start.6 = (bf16[256,256]{1,0:T(8,128)(2,1)S(1)}, bf16[256,256]{1,0:T(8,128)(2,1)S(1)}, u32[]{:S(2)}, u32[]{:S(2)}) collective-permute-start(bf16[256,256]{1,0:T(8,128)(2,1)S(1)} %get-tuple-element.72.refs_4_), channel_id=1, source_target_pairs={{0,2},{1,3},{2,0},{3,1},{4,6},{5,7},{6,4},{7,5},{8,10},{9,11},{10,... | collective-permute-start | bytes 393224 | tf_op jit(solution)/shard_map/ppermute | solution.py:17
  34.4 19.3 %collective-permute-start.8 = (bf16[1088,256]{1,0:T(8,128)(2,1)S(1)}, bf16[1088,256]{1,0:T(8,128)(2,1)S(1)}, u32[]{:S(2)}, u32[]{:S(2)}) collective-permute-start(bf16[1088,256]{1,0:T(8,128)(2,1)S(1)} %get-tuple-element.73.refs_0_), channel_id=1, source_target_pairs={{0,16},{4,20},{8,24},{12,28},{16,0},{20,4},{24,8},{28,12},{1,17},{... | collective-permute-start | bytes 1671176 | tf_op jit(solution)/shard_map/ppermute | solution.py:17
  36.0 17.8 %collective-permute-start.9 = (bf16[1088,256]{1,0:T(8,128)(2,1)S(1)}, bf16[1088,256]{1,0:T(8,128)(2,1)S(1)}, u32[]{:S(2)}, u32[]{:S(2)}) collective-permute-start(bf16[1088,256]{1,0:T(8,128)(2,1)S(1)} %get-tuple-element.74.refs_2_), channel_id=1, source_target_pairs={{0,8},{4,12},{8,0},{12,4},{16,24},{20,28},{24,16},{28,20},{1,9},{5... | collective-permute-start | bytes 1671176 | tf_op jit(solution)/shard_map/ppermute | solution.py:17
  39.5 14.2 %collective-permute-start.10 = (bf16[512,256]{1,0:T(8,128)(2,1)S(1)}, bf16[512,256]{1,0:T(8,128)(2,1)S(1)}, u32[]{:S(2)}, u32[]{:S(2)}) collective-permute-start(bf16[512,256]{1,0:T(8,128)(2,1)S(1)} %get-tuple-element.75.refs_4_), channel_id=1, source_target_pairs={{0,8},{4,12},{8,0},{12,4},{16,24},{20,28},{24,16},{28,20},{1,9},{5... | collective-permute-start | bytes 786440 | tf_op jit(solution)/shard_map/ppermute | solution.py:17
  41.9 11.9 %collective-permute-start.11 = (bf16[512,256]{1,0:T(8,128)(2,1)S(1)}, bf16[512,256]{1,0:T(8,128)(2,1)S(1)}, u32[]{:S(2)}, u32[]{:S(2)}) collective-permute-start(bf16[512,256]{1,0:T(8,128)(2,1)S(1)} %get-tuple-element.76.refs_6_), channel_id=1, source_target_pairs={{0,16},{4,20},{8,24},{12,28},{16,0},{20,4},{24,8},{28,12},{1,17},{... | collective-permute-start | bytes 786440 | tf_op jit(solution)/shard_map/ppermute | solution.py:17
  55.0 20.1 %collective-permute-start.19 = (bf16[1024,256]{1,0:T(8,128)(2,1)S(1)}, bf16[1024,256]{1,0:T(8,128)(2,1)S(1)}, u32[]{:S(2)}, u32[]{:S(2)}) collective-permute-start(bf16[1024,256]{1,0:T(8,128)(2,1)S(1)} %get-tuple-element.91.refs_0_), channel_id=1, source_target_pairs={{0,16},{4,20},{8,24},{12,28},{16,0},{20,4},{24,8},{28,12},{1,17},{... | collective-permute-start | bytes 1572872 | tf_op jit(solution)/shard_map/ppermute | solution.py:17
  55.5 19.6 %collective-permute-start.20 = (bf16[1024,256]{1,0:T(8,128)(2,1)S(1)}, bf16[1024,256]{1,0:T(8,128)(2,1)S(1)}, u32[]{:S(2)}, u32[]{:S(2)}) collective-permute-start(bf16[1024,256]{1,0:T(8,128)(2,1)S(1)} %get-tuple-element.92.refs_2_), channel_id=1, source_target_pairs={{0,8},{4,12},{8,0},{12,4},{16,24},{20,28},{24,16},{28,20},{1,9},{5... | collective-permute-start | bytes 1572872 | tf_op jit(solution)/shard_map/ppermute | solution.py:17
  57.0 18.1 %collective-permute-start.21 = (bf16[512,256]{1,0:T(8,128)(2,1)S(1)}, bf16[512,256]{1,0:T(8,128)(2,1)S(1)}, u32[]{:S(2)}, u32[]{:S(2)}) collective-permute-start(bf16[512,256]{1,0:T(8,128)(2,1)S(1)} %get-tuple-element.93.refs_4_), channel_id=1, source_target_pairs={{0,8},{4,12},{8,0},{12,4},{16,24},{20,28},{24,16},{28,20},{1,9},{5... | collective-permute-start | bytes 786440 | tf_op jit(solution)/shard_map/ppermute | solution.py:17
  57.5 17.6 %collective-permute-start.22 = (bf16[512,256]{1,0:T(8,128)(2,1)}, bf16[512,256]{1,0:T(8,128)(2,1)S(1)}, u32[]{:S(2)}, u32[]{:S(2)}) collective-permute-start(bf16[512,256]{1,0:T(8,128)(2,1)} %copy-done.11), channel_id=1, source_target_pairs={{0,16},{4,20},{8,24},{12,28},{16,0},{20,4},{24,8},{28,12},{1,17},{... | collective-permute-start | bytes 786440 | tf_op jit(solution)/shard_map/ppermute | solution.py:17
  76.7 32.6 %collective-permute-start.23 = (bf16[4096,256]{1,0:T(8,128)(2,1)}, bf16[4096,256]{1,0:T(8,128)(2,1)}, u32[]{:S(2)}, u32[]{:S(2)}) collective-permute-start(bf16[4096,256]{1,0:T(8,128)(2,1)} %get-tuple-element.95), channel_id=1, source_target_pairs={{0,4},{4,0},{8,12},{12,8},{16,20},{20,16},{24,28},{28,24},{1,5},{5... | collective-permute-start | bytes 6291464 | tf_op jit(solution)/shard_map/ppermute | solution.py:17
  91.8 14.7 %collective-permute-start.16 = (bf16[4,288,512]{2,1,0:T(8,128)(2,1)}, bf16[4,288,512]{2,1,0:T(8,128)(2,1)}, u32[]{:S(2)}, u32[]{:S(2)}) collective-permute-start(bf16[4,288,512]{2,1,0:T(8,128)(2,1)} %get-tuple-element.86), channel_id=1, source_target_pairs={{0,4},{4,0},{8,12},{12,8},{16,20},{20,16},{24,28},{28,24},{1,5},{5... | collective-permute-start | bytes 3538952 | tf_op jit(solution)/shard_map/ppermute | solution.py:17
  92.4 60.2 %all-to-all-start = ((bf16[4,512,256]{2,1,0:T(8,128)(2,1)}), bf16[4,512,256]{2,1,0:T(8,128)(2,1)S(1)}, u32[]{:S(2)}, u32[]{:S(2)}) async-start(bf16[4,512,256]{2,1,0:T(8,128)(2,1)} %get-tuple-element.84), calls=%async_computation | async-start | bytes 2097152 | tf_op jit(solution)/shard_map/all_to_all | solution.py:659
  97.4 22.2 %collective-permute-start.30 = (bf16[1024,256]{1,0:T(8,128)(2,1)S(1)}, bf16[1024,256]{1,0:T(8,128)(2,1)S(1)}, u32[]{:S(2)}, u32[]{:S(2)}) collective-permute-start(bf16[1024,256]{1,0:T(8,128)(2,1)S(1)} %get-tuple-element.111.refs_0_), channel_id=1, source_target_pairs={{0,16},{4,20},{8,24},{12,28},{16,0},{20,4},{24,8},{28,12},{1,17},{... | collective-permute-start | bytes 1572872 | tf_op jit(solution)/shard_map/ppermute | solution.py:17
  99.0 20.7 %collective-permute-start.31 = (bf16[1024,256]{1,0:T(8,128)(2,1)S(1)}, bf16[1024,256]{1,0:T(8,128)(2,1)S(1)}, u32[]{:S(2)}, u32[]{:S(2)}) collective-permute-start(bf16[1024,256]{1,0:T(8,128)(2,1)S(1)} %get-tuple-element.112.refs_2_), channel_id=1, source_target_pairs={{0,8},{4,12},{8,0},{12,4},{16,24},{20,28},{24,16},{28,20},{1,9},{5... | collective-permute-start | bytes 1572872 | tf_op jit(solution)/shard_map/ppermute | solution.py:17
  108.1 13.0 %collective-permute-start.17 = (bf16[2,160,512]{2,1,0:T(8,128)(2,1)S(1)}, bf16[2,160,512]{2,1,0:T(8,128)(2,1)S(1)}, u32[]{:S(2)}, u32[]{:S(2)}) collective-permute-start(bf16[2,160,512]{2,1,0:T(8,128)(2,1)S(1)} %get-tuple-element.88), channel_id=1, source_target_pairs={{0,8},{4,12},{8,0},{12,4},{16,24},{20,28},{24,16},{28,20},{1,9},{5... | collective-permute-start | bytes 983048 | tf_op jit(solution)/shard_map/ppermute | solution.py:17
  108.8 12.3 %collective-permute-start.18 = (bf16[2,128,512]{2,1,0:T(8,128)(2,1)S(1)}, bf16[2,128,512]{2,1,0:T(8,128)(2,1)S(1)}, u32[]{:S(2)}, u32[]{:S(2)}) collective-permute-start(bf16[2,128,512]{2,1,0:T(8,128)(2,1)S(1)} %get-tuple-element.90), channel_id=1, source_target_pairs={{0,16},{4,20},{8,24},{12,28},{16,0},{20,4},{24,8},{28,12},{1,17},{... | collective-permute-start | bytes 786440 | tf_op jit(solution)/shard_map/ppermute | solution.py:17
  121.1 35.2 %collective-permute-start.32 = (bf16[4096,256]{1,0:T(8,128)(2,1)}, bf16[4096,256]{1,0:T(8,128)(2,1)}, u32[]{:S(2)}, u32[]{:S(2)}) collective-permute-start(bf16[4096,256]{1,0:T(8,128)(2,1)} %shard_map.74), channel_id=1, source_target_pairs={{0,4},{4,0},{8,12},{12,8},{16,20},{20,16},{24,28},{28,24},{1,5},{5... | collective-permute-start | bytes 6291464 | tf_op jit(solution)/shard_map/ppermute | solution.py:17
  136.1 13.2 %collective-permute-start.27 = (bf16[4,288,512]{2,1,0:T(8,128)(2,1)S(1)}, bf16[4,288,512]{2,1,0:T(8,128)(2,1)S(1)}, u32[]{:S(2)}, u32[]{:S(2)}) collective-permute-start(bf16[4,288,512]{2,1,0:T(8,128)(2,1)S(1)} %get-tuple-element.106), channel_id=1, source_target_pairs={{0,4},{4,0},{8,12},{12,8},{16,20},{20,16},{24,28},{28,24},{1,5},{5... | collective-permute-start | bytes 3538952 | tf_op jit(solution)/shard_map/ppermute | solution.py:17
  144.0 25.1 %collective-permute-start.26 = (bf16[256,512]{1,0:T(8,128)(2,1)}, bf16[256,512]{1,0:T(8,128)(2,1)S(1)}, u32[]{:S(2)}, u32[]{:S(2)}) collective-permute-start(bf16[256,512]{1,0:T(8,128)(2,1)} %bitcast.22), channel_id=1, source_target_pairs={{0,0},{1,10},{2,17},{3,27},{4,4},{5,14},{6,21},{7,31},{8,1},{9,11}... | collective-permute-start | bytes 786440 | tf_op jit(solution)/shard_map/ppermute | solution.py:557
  150.2 16.6 %collective-permute-start.28 = (bf16[2,160,512]{2,1,0:T(8,128)(2,1)}, bf16[2,160,512]{2,1,0:T(8,128)(2,1)S(1)}, u32[]{:S(2)}, u32[]{:S(2)}) collective-permute-start(bf16[2,160,512]{2,1,0:T(8,128)(2,1)} %get-tuple-element.108), channel_id=1, source_target_pairs={{0,8},{4,12},{8,0},{12,4},{16,24},{20,28},{24,16},{28,20},{1,9},{5... | collective-permute-start | bytes 983048 | tf_op jit(solution)/shard_map/ppermute | solution.py:17
  152.6 14.2 %collective-permute-start.29 = (bf16[2,128,512]{2,1,0:T(8,128)(2,1)}, bf16[2,128,512]{2,1,0:T(8,128)(2,1)}, u32[]{:S(2)}, u32[]{:S(2)}) collective-permute-start(bf16[2,128,512]{2,1,0:T(8,128)(2,1)} %get-tuple-element.110), channel_id=1, source_target_pairs={{0,16},{4,20},{8,24},{12,28},{16,0},{20,4},{24,8},{28,12},{1,17},{... | collective-permute-start | bytes 786440 | tf_op jit(solution)/shard_map/ppermute | solution.py:17
  152.6 33.4 %all-to-all-start.1 = ((bf16[4,512,256]{2,1,0:T(8,128)(2,1)}), bf16[4,512,256]{2,1,0:T(8,128)(2,1)S(1)}, u32[]{:S(2)}, u32[]{:S(2)}) async-start(bf16[4,512,256]{2,1,0:T(8,128)(2,1)} %get-tuple-element.104), calls=%async_computation.1 | async-start | bytes 2097152 | tf_op jit(solution)/shard_map/all_to_all | solution.py:659
  186.0 36.8 %all-to-all-start.2 = ((bf16[4,512,256]{2,1,0:T(8,128)(2,1)}), bf16[4,512,256]{2,1,0:T(8,128)(2,1)S(1)}, u32[]{:S(2)}, u32[]{:S(2)}) async-start(bf16[4,512,256]{2,1,0:T(8,128)(2,1)} %copy-done.4), calls=%async_computation.2 | async-start | bytes 2097152 | tf_op jit(solution)/shard_map/all_to_all | solution.py:659
  208.9 13.9 %collective-permute-start.39 = (bf16[1,160,512]{2,1,0:T(8,128)(2,1)}, bf16[1,160,512]{2,1,0:T(8,128)(2,1)}, u32[]{:S(2)}, u32[]{:S(2)}) collective-permute-start(bf16[1,160,512]{2,1,0:T(8,128)(2,1)} %get-tuple-element.131), channel_id=1, source_target_pairs={{0,16},{4,20},{8,24},{12,28},{16,0},{20,4},{24,8},{28,12},{1,17},{... | collective-permute-start | bytes 491528 | tf_op jit(solution)/shard_map/ppermute | solution.py:17
  213.3 12.9 %collective-permute-start.43 = (f32[2,1,32,256]{3,2,0,1:T(8,128)}, f32[2,1,32,256]{3,2,0,1:T(8,128)}, u32[]{:S(2)}, u32[]{:S(2)}) collective-permute-start(f32[2,1,32,256]{3,2,0,1:T(8,128)} %fusion.7), channel_id=1, source_target_pairs={{0,2},{1,3},{2,0},{3,1},{4,6},{5,7},{6,4},{7,5},{8,10},{9,11},{10,... | collective-permute-start | bytes 196616 | tf_op jit(solution)/shard_map/ppermute | solution.py:17
  219.4 27.5 %collective-permute-start.38 = (bf16[256,512]{1,0:T(8,128)(2,1)}, bf16[256,512]{1,0:T(8,128)(2,1)}, u32[]{:S(2)}, u32[]{:S(2)}) collective-permute-start(bf16[256,512]{1,0:T(8,128)(2,1)} %bitcast.98), channel_id=1, source_target_pairs={{0,0},{1,10},{2,17},{3,27},{4,4},{5,14},{6,21},{7,31},{8,1},{9,11}... | collective-permute-start | bytes 786440 | tf_op jit(solution)/shard_map/ppermute | solution.py:557
  227.2 19.7 %collective-permute-start.41 = (bf16[256,512]{1,0:T(8,128)(2,1)S(1)}, bf16[256,512]{1,0:T(8,128)(2,1)S(1)}, u32[]{:S(2)}, u32[]{:S(2)}) collective-permute-start(bf16[256,512]{1,0:T(8,128)(2,1)S(1)} %bitcast.99), channel_id=1, source_target_pairs={{0,0},{1,10},{2,17},{3,27},{4,4},{5,14},{6,21},{7,31},{8,1},{9,11}... | collective-permute-start | bytes 786440 | tf_op jit(solution)/shard_map/ppermute | solution.py:557
  (50 other events, 379.3 us)
